TPU v7x, 256 devices: a whole 4x4x8 slice. The times are simulated.
256 devices in a mesh: pipe: 2 (over y_hi), ctx: 16 (over z, core), exp: 8 (over y_lo, x).
Axes of the slice: x: 4, y: 4 (y_hi: 2, y_lo: 2; y = y_hi * 2 + y_lo), z: 8, core: 2. Of those that a mesh axis runs over, the one named last changes fastest.
Arguments:
- queries: bfloat16 [2, 2048, 64, 576], P('pipe', 'ctx', 'exp'), may hold values from -24 to 24
- latent_rows: bfloat16 [2, 2048, 576], P('pipe', 'ctx'), may hold values from -4 to 4
- doc_ids: int32 [2, 2048], P('pipe', 'ctx'), may hold values from 0 to 2, never falling along the last dimension, each value on 1 to 1024 neighbouring positions
- value_up: bfloat16 [2, 64, 512, 128], P('pipe', 'exp'), may hold values from -0.25 to 0.25
- out_proj: bfloat16 [2, 8192, 7168], P('pipe', 'exp', 'ctx'), may hold values from -0.0625 to 0.0625
- residual_in: bfloat16 [2, 2048, 7168], P('pipe', ('ctx', 'exp')), may hold values from -6 to 6
- norm_gain: float32 [2, 7168], P('pipe'), may hold values from 0.1 to 1.9
- expert_ids: int32 [2, 2048, 2], P('pipe', ('ctx', 'exp')), may hold values from 0 to 7, all different within a row; in each aligned block of 16 rows (0 to 15, 16 to 31, ..., all dimensions but the last counted through in order) at most 5 rows name the same one
- gate_weights: float32 [2, 2048, 2], P('pipe', ('ctx', 'exp')), may hold values from 0.1 to 1
- gate_proj: bfloat16 [2, 8, 7168, 2048], P('pipe', 'exp', None, 'ctx'), may hold values from -0.0625 to 0.0625
- up_proj: bfloat16 [2, 8, 7168, 2048], P('pipe', 'exp', None, 'ctx'), may hold values from -0.0625 to 0.0625
- down_proj: bfloat16 [2, 8, 2048, 7168], P('pipe', 'exp', 'ctx'), may hold values from -0.125 to 0.125
Outputs:
- handed: bfloat16 [2, 2048, 7168], P('pipe', ('ctx', 'exp'))
Inputs may be any that keep to these rules, and one draw needn't show every extreme that they name: `doc_ids`: within each section the ids never fall; each of the 3 documents holds 1 to 1024 positions, and one holds exactly 1024. `expert_ids`: each token names 2 different experts. Among the 16 tokens of one device no expert is named by more than 5 tokens, a bound that some block reaches.
All inputs are finite; a program needn't handle non-finite values.
Results may differ from a plain program's by a relative error of at most 0.02.
Values may be sent and summed in bfloat16 or wider, within the bound.
A program may use at most 64 MiB of HBM per device.

v0:
```python
import math

import jax
import jax.numpy as jnp
from jax import lax
from jax.sharding import PartitionSpec as P

D = 7168
HD = 128
ROPE = 64
LAT = 512
TOP = 2


epsilon = 1e-06
masked_score = -1e30


def shifted(shard, axis, by):
    devices = lax.axis_size(axis)
    return lax.ppermute(shard, axis, [(i, (i + by) % devices) for i in range(devices)])


def on_device(
    queries,
    latent_rows,
    doc_ids,
    value_up,
    out_proj,
    residual_in,
    norm_gain,
    expert_ids,
    gate_weights,
    gate_proj,
    up_proj,
    down_proj,
):
    ctx_count = lax.axis_size("ctx")
    exp_count = lax.axis_size("exp")
    ctx_rank = lax.axis_index("ctx")
    query_rows = queries[0]
    local_len = query_rows.shape[0]
    head_count = query_rows.shape[1]
    query_pos = ctx_rank * local_len + jnp.arange(local_len, dtype=jnp.int32)
    query_doc = doc_ids[0]
    score_scale = 1.0 / math.sqrt(HD + ROPE)
    start_top = jnp.full((head_count, local_len), masked_score, jnp.float32)
    start_sum = jnp.zeros((head_count, local_len), jnp.float32)
    start_acc = jnp.zeros((head_count, local_len, LAT), jnp.float32)
    key_rows = lax.all_gather(latent_rows[0], "ctx", axis=0, tiled=True)
    key_docs = lax.all_gather(doc_ids[0], "ctx", axis=0, tiled=True)
    key_span = key_rows.shape[0]

    def visit(current):
        running, totals, weighted = current
        key_pos = jnp.arange(key_span, dtype=jnp.int32)
        allowed = (key_pos[None, :] <= query_pos[:, None]) & (
            key_docs[None, :] == query_doc[:, None]
        )
        scores = (
            jnp.einsum("qhc,kc->hqk", query_rows, key_rows, preferred_element_type=jnp.float32)
            * score_scale
        )
        scores = jnp.where(allowed[None], scores, masked_score)
        highest = jnp.maximum(running, jnp.max(scores, axis=2))
        weights_now = jnp.where(allowed[None], jnp.exp(scores - highest[:, :, None]), 0.0)
        totals = jnp.sum(weights_now, axis=2)
        update = jnp.einsum(
            "hqk,kc->hqc",
            weights_now.astype(jnp.bfloat16),
            key_rows[:, :LAT],
            preferred_element_type=jnp.float32,
        )
        weighted = update
        return (highest, totals, weighted)

    running, totals, weighted = lax.cond(
        jnp.int32(0) <= query_pos[-1],
        visit,
        lambda current: current,
        (start_top, start_sum, start_acc),
    )
    latent_out = (weighted / totals[:, :, None]).astype(jnp.bfloat16)
    heads = jnp.einsum(
        "hqc,hcd->qhd", latent_out, value_up[0], preferred_element_type=jnp.float32
    ).astype(jnp.bfloat16)
    heads = heads.reshape(local_len, head_count * HD)
    everyone = lax.all_gather(heads, "ctx", axis=0, tiled=True)
    tok_count = local_len // exp_count
    grid_rows = everyone.reshape(ctx_count, exp_count, tok_count, head_count * HD)
    column_proj = out_proj[0]
    block_rows = ctx_count * tok_count
    picked = grid_rows
    picked = jnp.swapaxes(picked, 0, 1).reshape(block_rows * lax.axis_size("exp"), head_count * HD)
    attn_part = lax.psum_scatter(
        jnp.dot(picked, column_proj, preferred_element_type=jnp.float32).astype(jnp.bfloat16),
        "exp",
        scatter_dimension=0,
        tiled=True,
    )
    attention = lax.all_to_all(attn_part, "ctx", split_axis=0, concat_axis=1, tiled=True)
    stream = (residual_in[0].astype(jnp.float32) + attention.astype(jnp.float32)).astype(
        jnp.bfloat16
    )
    stream = lax.optimization_barrier(stream)
    stream_wide = stream.astype(jnp.float32)
    mean_square = jnp.mean(stream_wide * stream_wide, axis=1, keepdims=True)
    normed = (stream_wide * lax.rsqrt(mean_square + epsilon) * norm_gain[0][None, :]).astype(
        jnp.bfloat16
    )
    capacity = min(tok_count, max(2, (5 * tok_count * TOP + 4 * exp_count - 1) // (4 * exp_count)))
    chosen_flat = expert_ids[0].reshape(-1)
    matches = (chosen_flat[:, None] == jnp.arange(exp_count, dtype=jnp.int32)[None, :]).astype(
        jnp.int32
    )
    earlier = jnp.sum((jnp.cumsum(matches, axis=0) - matches) * matches, axis=1)
    slot_index = chosen_flat * capacity + earlier
    slot_table = slot_index[None, :] == jnp.arange(exp_count * capacity, dtype=jnp.int32)[:, None]
    slot_table = slot_table.reshape(exp_count * capacity, tok_count, TOP)
    placing = jnp.sum(slot_table.astype(jnp.float32), axis=2).astype(jnp.bfloat16)
    outbox = jnp.dot(placing, normed, preferred_element_type=jnp.float32).astype(jnp.bfloat16)
    inbox = lax.all_to_all(
        outbox.reshape(exp_count, capacity, D), "exp", split_axis=0, concat_axis=0, tiled=True
    )
    expert_in = inbox.reshape(exp_count * capacity, D)
    gate_cols = gate_proj[0, 0]
    up_cols = up_proj[0, 0]
    down_rows = down_proj[0, 0]
    block_in = lax.all_gather(expert_in, "ctx", axis=0, tiled=True)
    gate_value = jnp.dot(block_in, gate_cols, preferred_element_type=jnp.float32)
    up_value = jnp.dot(block_in, up_cols, preferred_element_type=jnp.float32)
    hidden = (jax.nn.silu(gate_value) * up_value).astype(jnp.bfloat16)
    expert_out = lax.psum_scatter(
        jnp.dot(hidden, down_rows, preferred_element_type=jnp.float32).astype(jnp.bfloat16),
        "ctx",
        scatter_dimension=0,
        tiled=True,
    )
    returned = lax.all_to_all(
        expert_out.reshape(exp_count, capacity, D), "exp", split_axis=0, concat_axis=0, tiled=True
    )
    mixing = jnp.sum(jnp.where(slot_table, gate_weights[0][None, :, :], 0.0), axis=2)
    returned_wide = returned.reshape(exp_count * capacity, D).astype(jnp.float32)
    combined = jnp.dot(mixing.T, returned_wide, precision=lax.Precision.HIGHEST)
    layer_out = (stream_wide + combined).astype(jnp.bfloat16)
    return shifted(layer_out[None], "pipe", 1)


def solution(mesh):
    return jax.shard_map(
        on_device,
        mesh=mesh,
        in_specs=(
            P("pipe", "ctx", "exp", None),
            P("pipe", "ctx", None),
            P("pipe", "ctx"),
            P("pipe", "exp", None, None),
            P("pipe", "exp", "ctx"),
            P("pipe", ("ctx", "exp"), None),
            P("pipe", None),
            P("pipe", ("ctx", "exp"), None),
            P("pipe", ("ctx", "exp"), None),
            P("pipe", "exp", None, "ctx"),
            P("pipe", "exp", None, "ctx"),
            P("pipe", "exp", "ctx", None),
        ),
        out_specs=P("pipe", ("ctx", "exp"), None),
        check_vma=False,
    )
```

profile of v0, /device:TPU:1, one launch (start us, length us, event | category | flops | bytes accessed | tf_op | source)
XLA Modules:
  0.0 370.5 jit_solution(10761864257041107715)
XLA Ops:
  6.5 1.8 copy.37
  9.8 21.3 %all-gather = s32[1,2048]{1,0:T(1,128)S(1)} all-gather(s32[1,128]{1,0:T(1,128)} %param.16), channel_id=2, replica_groups=mesh['pipe'=2,'ctx'=16,'exp'=8] {'ctx'}, dimensions={1}, use_global_device_ids=true | all-gather | bytes 8704 | tf_op jit(solution)/shard_map/all_gather | solution.py:51
  31.2 22.6 %all-gather.10.cloned.1.call-done = bf16[1,2048,576]{2,1,0:T(8,128)(2,1)} async-done(((bf16[1,128,576]{2,1,0:T(8,128)(2,1)}), bf16[1,2048,576]{2,1,0:T(8,128)(2,1)}) %all-gather.10.cloned.1.call-update) | async-done | bytes 2359312 | tf_op jit(solution)/shard_map/all_gather | solution.py:50
  53.8 11.7 %conditional.1 = (f32[8,128]{1,0:T(8,128)S(1)}, f32[8,128,512]{2,1,0:T(8,128)S(1)}) conditional(s32[]{:T(128)} %bitcast.6, () %tuple.13, (s32[128]{0:T(128)S(1)}, s32[2048]{0:T(1024)S(1)}, s32[1,128]{1,0:T(1,128)}, bf16[1,128,8,576]{1,3,2,0:T(8,128)(2,1)}, bf16[2048,576]{1,0:T(8,128)(2,1)}) %tuple.30), branch_computations={%region_0.0_spmd, %region_1.4_spmd} | conditional | flops 4591451136 | bytes 43418668 | solution.py:77
  54.9 6.1 %fusion = (f32[8,128]{1,0:T(8,128)S(1)}, f32[2048,128,8]{1,0,2:T(8,128)S(1)}) fusion(pred[128,2048]{0,1:T(8,128)(4,1)S(1)} %fusion.11, bf16[1,128,8,576]{1,3,2,0:T(8,128)(2,1)} %get-tuple-element.26, bf16[2048,576]{1,0:T(8,128)(2,1)} %get-tuple-element.19), kind=kOutput, calls=%fused_computation.2 | convolution fusion | flops 2422209536 | bytes 12193792 | tf_op jit(solution)/shard_map/cond/branch_1_fun/qhc,kc->hqk/dot_general | solution.py:61
  61.0 2.5 fusion.3
  63.5 2.0 fusion.2
  67.2 40.8 %all-gather.6.cloned.1.call-done = bf16[2048,1024]{1,0:T(8,128)(2,1)} async-done(((bf16[128,1024]{1,0:T(8,128)(2,1)}), bf16[2048,1024]{1,0:T(8,128)(2,1)}) %all-gather.6.cloned.1.call-update) | async-done | bytes 4194320 | tf_op jit(solution)/shard_map/all_gather | solution.py:88
  107.9 2.7 copy.40
  110.7 3.4 convolution_convert_fusion.2
  114.4 37.0 %reduce-scatter.3.cloned.1.call-done = bf16[256,448]{0,1:T(8,128)(2,1)} async-done(((bf16[2048,448]{0,1:T(8,128)(2,1)}), bf16[256,448]{0,1:T(8,128)(2,1)}) %reduce-scatter.3.cloned.1.call-update) | async-done | bytes 229392 | tf_op jit(solution)/shard_map/reduce_scatter | solution.py:95
  151.4 1.8 copy.41
  153.2 13.0 %all-to-all-start = ((bf16[16,16,448]{2,1,0:T(8,128)(2,1)}), bf16[16,16,448]{2,1,0:T(8,128)(2,1)S(1)}, u32[]{:S(2)}, u32[]{:S(2)}) async-start(bf16[16,16,448]{2,1,0:T(8,128)(2,1)} %bitcast.16), calls=%async_computation.1 | async-start | bytes 524288 | tf_op jit(solution)/shard_map/all_to_all | solution.py:101
  167.5 10.4 %all-to-all-done = bf16[16,16,448]{2,1,0:T(8,128)(2,1)S(1)} async-done(((bf16[16,16,448]{2,1,0:T(8,128)(2,1)}), bf16[16,16,448]{2,1,0:T(8,128)(2,1)S(1)}, u32[]{:S(2)}, u32[]{:S(2)}) %all-to-all-start) | async-done | bytes 229408 | tf_op jit(solution)/shard_map/all_to_all | solution.py:101
  179.4 17.9 %all_to_all.23 = bf16[8,5,7168]{2,1,0:T(8,128)(2,1)} all-to-all(bf16[8,5,7168]{2,1,0:T(8,128)(2,1)S(1)} %reshape.116), channel_id=1, replica_groups=mesh['pipe'=2,'ctx'=16,'exp'=8] {'exp'}, dimensions={0} | all-to-all | bytes 1146880 | tf_op jit(solution)/shard_map/all_to_all | solution.py:122
  197.3 2.3 reshape.117
  199.7 54.6 %all-gather.8.cloned.1.call-done = bf16[640,7168]{1,0:T(8,128)(2,1)} async-done(((bf16[40,7168]{1,0:T(8,128)(2,1)}), bf16[640,7168]{1,0:T(8,128)(2,1)}) %all-gather.8.cloned.1.call-update) | async-done | bytes 9175056 | tf_op jit(solution)/shard_map/all_gather | solution.py:129
  254.3 6.8 %fusion.20 = f32[640,128]{1,0:T(8,128)S(1)} fusion(bf16[640,7168]{1,0:T(8,128)(2,1)} %all-gather.8.cloned.1.call-done, bf16[1,1,7168,128]{3,2,1,0:T(8,128)(2,1)} %param.23), kind=kOutput, calls=%fused_computation.28 | convolution fusion | flops 1174405120 | bytes 11337728 | tf_op jit(solution)/shard_map/dot_general | solution.py:130
  261.6 2.5 fusion.25
  264.1 6.1 %convolution_convert_fusion = bf16[640,7168]{1,0:T(8,128)(2,1)} fusion(bf16[640,128]{1,0:T(8,128)(2,1)S(1)} %fusion.25, bf16[1,1,128,7168]{3,2,1,0:T(8,128)(2,1)S(1)} %copy-done), kind=kOutput, calls=%fused_computation.18 | convolution fusion | flops 1178992640 | bytes 11173888 | tf_op jit(solution)/shard_map/dot_general | solution.py:134
  270.2 68.0 %reduce-scatter.5.cloned.1.call-done = bf16[40,7168]{1,0:T(8,128)(2,1)} async-done(((bf16[640,7168]{1,0:T(8,128)(2,1)}), bf16[40,7168]{1,0:T(8,128)(2,1)}) %reduce-scatter.5.cloned.1.call-update) | async-done | bytes 573456 | tf_op jit(solution)/shard_map/reduce_scatter | solution.py:133
  339.5 15.5 %all_to_all.24 = bf16[8,5,7168]{2,1,0:T(8,128)(2,1)} all-to-all(bf16[8,5,7168]{2,1,0:T(8,128)(2,1)S(1)} %reshape.118), channel_id=1, replica_groups=mesh['pipe'=2,'ctx'=16,'exp'=8] {'exp'}, dimensions={0} | all-to-all | bytes 1146880 | tf_op jit(solution)/shard_map/all_to_all | solution.py:139
  356.9 2.2 collective-permute-start
  359.0 4.3 %collective-permute-done = bf16[1,16,7168]{2,1,0:T(8,128)(2,1)S(1)} collective-permute-done((bf16[1,16,7168]{2,1,0:T(8,128)(2,1)S(1)}, bf16[1,16,7168]{2,1,0:T(8,128)(2,1)S(1)}, u32[]{:S(2)}, u32[]{:S(2)}) %collective-permute-start) | collective-permute-done | bytes 229408 | tf_op jit(solution)/shard_map/ppermute | solution.py:21
  (59 shorter events, 10.9 us)
Async XLA Ops:
  6.5 257.6 %copy-start = (bf16[1,1,128,7168]{3,2,1,0:T(8,128)(2,1)S(1)}, bf16[1,1,128,7168]{3,2,1,0:T(8,128)(2,1)}, u32[]{:S(2)}) copy-start(bf16[1,1,128,7168]{3,2,1,0:T(8,128)(2,1)} %param.25) | copy-start | bytes 5505028
  6.5 47.3 %all-gather.10.cloned.1.call-start = ((), (), s32[]{:S(2)}) async-start(), calls=%async_computation.9 | async-start | bytes 2785280 | tf_op jit(solution)/shard_map/all_gather | solution.py:50
  8.4 99.5 %all-gather.6.cloned.1.call-start = ((), (), s32[]{:S(2)}) async-start(), calls=%async_computation.5 | async-start | bytes 4456448 | tf_op jit(solution)/shard_map/all_gather | solution.py:88
  53.8 11.7 %copy-start.9 = (bf16[1,8,512,128]{3,2,1,0:T(8,128)(2,1)S(1)}, bf16[1,8,512,128]{3,2,1,0:T(8,128)(2,1)}, u32[]{:S(2)}) copy-start(bf16[1,8,512,128]{3,2,1,0:T(8,128)(2,1)} %param.17) | copy-start | bytes 3145732
  54.9 6.1 %copy-start.7 = (bf16[2048,576]{1,0:T(8,128)(2,1)S(1)}, bf16[2048,576]{1,0:T(8,128)(2,1)}, u32[]{:S(2)}) copy-start(bf16[2048,576]{1,0:T(8,128)(2,1)} %get-tuple-element.19) | copy-start | bytes 7077892 | tf_op jit(solution)/shard_map/cond
  67.1 84.2 %reduce-scatter.3.cloned.1.call-start = ((), (), s32[]{:S(2)}) async-start(), calls=%async_computation.6 | async-start | bytes 2064384 | tf_op jit(solution)/shard_map/reduce_scatter | solution.py:95
  107.9 2.7 copy-start.10
  110.7 3.4 copy-start.4
  110.7 56.1 %copy-start.5 = (f32[1,16,2]{1,2,0:T(2,128)S(1)}, f32[1,16,2]{1,2,0:T(2,128)}, u32[]{:S(2)}) copy-start(f32[1,16,2]{1,2,0:T(2,128)} %param.22) | copy-start | bytes 388
  114.0 64.5 %copy-start.1 = (bf16[1,16,7168]{2,1,0:T(8,128)(2,1)S(1)}, bf16[1,16,7168]{2,1,0:T(8,128)(2,1)}, u32[]{:S(2)}) copy-start(bf16[1,16,7168]{2,1,0:T(8,128)(2,1)} %param.19) | copy-start | bytes 688132
  114.0 64.7 %copy-start.3 = (f32[1,7168]{1,0:T(1,128)S(1)}, f32[1,7168]{1,0:T(1,128)}, u32[]{:S(2)}) copy-start(f32[1,7168]{1,0:T(1,128)} %param.20) | copy-start | bytes 86020
  153.2 24.8 %all-to-all-start = ((bf16[16,16,448]{2,1,0:T(8,128)(2,1)}), bf16[16,16,448]{2,1,0:T(8,128)(2,1)S(1)}, u32[]{:S(2)}, u32[]{:S(2)}) async-start(bf16[16,16,448]{2,1,0:T(8,128)(2,1)} %bitcast.16), calls=%async_computation.1 | async-start | bytes 524288 | tf_op jit(solution)/shard_map/all_to_all | solution.py:101
  166.2 88.1 %all-gather.8.cloned.1.call-start = ((), (), s32[]{:S(2)}) async-start(), calls=%async_computation.7 | async-start | bytes 9748480 | tf_op jit(solution)/shard_map/all_gather | solution.py:129
  199.6 138.6 %reduce-scatter.5.cloned.1.call-start = ((), (), s32[]{:S(2)}) async-start(), calls=%async_computation.8 | async-start | bytes 9748480 | tf_op jit(solution)/shard_map/reduce_scatter | solution.py:133
  254.3 6.8 %copy-start.6 = (bf16[640,7168]{1,0:T(8,128)(2,1)S(1)}, bf16[640,7168]{1,0:T(8,128)(2,1)}, u32[]{:S(2)}) copy-start(bf16[640,7168]{1,0:T(8,128)(2,1)} %all-gather.8.cloned.1.call-done) | copy-start | bytes 27525124
  254.3 7.2 %copy-start.8 = (bf16[1,1,7168,128]{3,2,1,0:T(8,128)(2,1)S(1)}, bf16[1,1,7168,128]{3,2,1,0:T(8,128)(2,1)}, u32[]{:S(2)}) copy-start(bf16[1,1,7168,128]{3,2,1,0:T(8,128)(2,1)} %param.24) | copy-start | bytes 5505028
  270.2 86.3 %copy-start.2 = (f32[40,16]{0,1:T(8,128)S(1)}, f32[40,16]{0,1:T(8,128)}, u32[]{:S(2)}) copy-start(f32[40,16]{0,1:T(8,128)} %get-tuple-element.28) | copy-start | bytes 7684
  356.9 6.5 %collective-permute-start = (bf16[1,16,7168]{2,1,0:T(8,128)(2,1)S(1)}, bf16[1,16,7168]{2,1,0:T(8,128)(2,1)S(1)}, u32[]{:S(2)}, u32[]{:S(2)}) collective-permute-start(bf16[1,16,7168]{2,1,0:T(8,128)(2,1)S(1)} %fusion.16), channel_id=1, source_target_pairs={{0,128},{128,0},{1,129},{129,1},{2,130},{130,2},{3,131},{131,3},{4... | collective-permute-start | bytes 688136 | tf_op jit(solution)/shard_map/ppermute | solution.py:21
Sparse Core Ops, SparseCore 0:
  9.2 44.5 all-gather.9
  67.3 40.6 all-gather.5
  114.2 37.1 reduce-scatter.2
  199.7 54.5 all-gather.7
  270.3 67.8 reduce-scatter.4
where the time goes:
time: 375 us; the launch traced here: 371 us
  waiting for transfers between devices  238 us (63%)
  blocking collectives  54.8 us (15%)
  matrix products  28.8 us (8%)
  starting transfers between devices  15.6 us (4%)
  local copies, waits for them, and re-layouts  15.2 us (4%)
  between operations  14 us (4%)
  other arithmetic  4.39 us (1%)
    reduce_scatter x1, waiting for transfers between devices, on_device(): lax.psum_scatter(jnp.dot(hidden, down_rows, preferred_element_type=jnp.fl...  68 us
    all_gather x1, waiting for transfers between devices, on_device(): block_in = lax.all_gather(expert_in, 'ctx', axis=0, tiled=True)  54.6 us
    all_gather x1, waiting for transfers between devices, on_device(): everyone = lax.all_gather(heads, 'ctx', axis=0, tiled=True)  40.8 us
    reduce_scatter x1, waiting for transfers between devices, on_device(): lax.psum_scatter(jnp.dot(picked, column_proj, preferred_element_type=jnp....  37 us
    all_gather x1, waiting for transfers between devices, on_device(): key_rows = lax.all_gather(latent_rows[0], 'ctx', axis=0, tiled=True)  22.6 us
    all_gather x1, blocking collectives, on_device(): key_docs = lax.all_gather(doc_ids[0], 'ctx', axis=0, tiled=True)  21.3 us
    all_to_all x1, blocking collectives, on_device(): lax.all_to_all(outbox.reshape(exp_count, capacity, D), 'exp', split_axis=...  17.9 us
    all_to_all x1, blocking collectives, on_device(): lax.all_to_all(expert_out.reshape(exp_count, capacity, D), 'exp', split_a...  15.5 us
  transfers between devices with their start and end apart: 7, of which 7 were waited for; matrix products, arithmetic and copies ran while one was open for 1% of the time, Pallas kernels for 0%

commit v1 on v0

--- a/solution.py
+++ b/solution.py
@@ -2,7 +2,10 @@
 
 import jax
 import jax.numpy as jnp
+import numpy as np
 from jax import lax
+from jax.experimental import pallas as pl
+from jax.experimental.pallas import tpu as pltpu
 from jax.sharding import PartitionSpec as P
 
 D = 7168
@@ -14,11 +17,356 @@
 
 epsilon = 1e-06
 masked_score = -1e30
-
-
-def shifted(shard, axis, by):
-    devices = lax.axis_size(axis)
-    return lax.ppermute(shard, axis, [(i, (i + by) % devices) for i in range(devices)])
+HALF = D // 2
+MESH = pl.DeviceIdType.MESH
+
+
+def remote(src, dst, send_sem, recv_sem, **device):
+    return pltpu.make_async_remote_copy(
+        src_ref=src,
+        dst_ref=dst,
+        send_sem=send_sem,
+        recv_sem=recv_sem,
+        device_id=device,
+        device_id_type=MESH,
+    )
+
+
+def meet(peers):
+    barrier = pltpu.get_barrier_semaphore()
+    for device in peers:
+        pl.semaphore_signal(barrier, 1, device_id=device, device_id_type=MESH)
+    pl.semaphore_wait(barrier, len(peers))
+
+
+def squeeze_map(rows, groups, group, dtype=jnp.bfloat16):
+    row = lax.broadcasted_iota(jnp.int32, (80, 8 * rows), 0).astype(jnp.float32)
+    col = lax.broadcasted_iota(jnp.int32, (80, 8 * rows), 1).astype(jnp.float32)
+    source = jnp.floor((row + 0.5) * 0.1)
+    want = source * rows + (row - source * 10) + group * 10
+    return jnp.where(col == want, 1.0, 0.0).astype(dtype)
+
+
+def spread_map(rows, groups, group, dtype=jnp.bfloat16):
+    row = lax.broadcasted_iota(jnp.int32, (8 * rows, 80), 0).astype(jnp.float32)
+    col = lax.broadcasted_iota(jnp.int32, (8 * rows, 80), 1).astype(jnp.float32)
+    source = jnp.floor((col + 0.5) * 0.1)
+    want = source * rows + (col - source * 10) + group * 10
+    return jnp.where(row == want, 1.0, 0.0).astype(dtype)
+
+
+PARTS = ((0, 4, 48), (4, 3, 32))
+PIECES = ((0, 1024), (1024, 1024), (2048, 768), (2816, 768))
+SUBS = ((0, 896), (896, 896), (1792, 896), (2688, 896))
+
+
+def expert_kernel(
+    stream_ref, gain_ref, sel0, sel1, mix0, mix1, gate_ref, up_ref, down_ref, out_ref,
+    normed, pn, ps, xg0, xg1, sg0, sg1, outbox0, outbox1, inbox0, inbox1, w_in, w_down,
+    rows, half, half_other, total, arrived, summed, ret0, ret1, back0, back1, ready, landed,
+    pair_s, pair_r, loc, box_s, box_r, ag_s, ag_r, half_s, half_r, rs_s, rs_r, back_s, back_r, fin_s, fin_r,
+):
+    p, c, e = lax.axis_index("pipe"), lax.axis_index("ctx"), lax.axis_index("exp")
+    k = lax.rem(c, 2)
+    z = lax.div(c, 2)
+    kk = 1 - k
+    other = 2 * z + kk
+    right = 2 * lax.rem(z + 1, 8) + k
+    left = 2 * lax.rem(z + 7, 8) + k
+    over = 1 - p
+    mine = pl.multiple_of(k * HALF, 128)
+    theirs = pl.multiple_of(kk * HALF, 128)
+    my_lane = pl.multiple_of(k * 128, 128)
+    up_lane = pl.multiple_of(256 + k * 128, 128)
+
+    local = [
+        pltpu.make_async_copy(gate_ref.at[pl.ds(mine, HALF), :], w_in.at[:, pl.ds(my_lane, 128)], loc.at[0]),
+        pltpu.make_async_copy(up_ref.at[pl.ds(mine, HALF), :], w_in.at[:, pl.ds(up_lane, 128)], loc.at[1]),
+        pltpu.make_async_copy(down_ref.at[:, pl.ds(mine, HALF)], w_down.at[pl.ds(my_lane, 128), :], loc.at[2]),
+    ]
+    for copy in local:
+        copy.start()
+
+    wide = stream_ref[...].astype(jnp.float32)
+    mean_square = jnp.mean(wide * wide, axis=1, keepdims=True)
+    normed[...] = (wide * lax.rsqrt(mean_square + epsilon) * gain_ref[...]).astype(jnp.bfloat16)
+
+    meet(
+        [{"ctx": other}, {"ctx": right}, {"ctx": left}]
+        + [{"exp": lax.rem(e + i, 8)} for i in range(1, 8)]
+        + [{"pipe": over}, {"pipe": over, "ctx": other}]
+    )
+    pair = [
+        remote(normed.at[:, pl.ds(theirs, HALF)], pn, pair_s.at[0], pair_r.at[0], ctx=other),
+        remote(stream_ref.at[:, pl.ds(theirs, HALF)], ps, pair_s.at[1], pair_r.at[1], ctx=other),
+        remote(gate_ref.at[pl.ds(theirs, HALF), :], w_in.at[:, pl.ds(my_lane, 128)], pair_s.at[2], pair_r.at[2], ctx=other),
+        remote(up_ref.at[pl.ds(theirs, HALF), :], w_in.at[:, pl.ds(up_lane, 128)], pair_s.at[3], pair_r.at[3], ctx=other),
+        remote(down_ref.at[:, pl.ds(theirs, HALF)], w_down.at[pl.ds(my_lane, 128), :], pair_s.at[4], pair_r.at[4], ctx=other),
+    ]
+    for copy in pair:
+        copy.start()
+    my_rows = [pl.multiple_of(g * 32 + k * 16, 16) for g in range(4)]
+    their_rows = [pl.multiple_of(g * 32 + kk * 16, 16) for g in range(4)]
+    xgs, sgs = (xg0, xg1), (sg0, sg1)
+    for part, (first, groups, _) in enumerate(PARTS):
+        for g in range(groups):
+            lanes = pl.ds(pl.multiple_of(mine + (first + g) * 512, 128), 512)
+            xgs[part][pl.ds(my_rows[g], 16), :] = normed[:, lanes]
+            sgs[part][pl.ds(my_rows[g], 16), :] = stream_ref[:, lanes]
+    pair[0].wait_recv()
+    outboxes, inboxes, sels = (outbox0, outbox1), (inbox0, inbox1), (sel0, sel1)
+
+    def box(part, i):
+        return remote(
+            outboxes[part].at[lax.rem(e + i, 8)], inboxes[part].at[e], box_s.at[part, i], box_r.at[part, i],
+            exp=lax.rem(e + i, 8),
+        )
+
+    def box_in(part, i):
+        source = lax.rem(e + 8 - i, 8)
+        return remote(outboxes[part].at[source], inboxes[part].at[source], box_s.at[part, i], box_r.at[part, i], exp=source)
+
+    for part, (first, groups, height) in enumerate(PARTS):
+        for g in range(groups):
+            lanes = slice((first + g) * 512, (first + g + 1) * 512)
+            xgs[part][pl.ds(their_rows[g], 16), :] = pn[:, lanes]
+        chosen = jnp.dot(sels[part][...], xgs[part][...], preferred_element_type=jnp.float32).astype(jnp.bfloat16)
+        outboxes[part][...] = chosen.reshape(8, height, 512)
+        for i in range(1, 8):
+            box(part, i).start()
+        inboxes[part][pl.ds(e, 1)] = outboxes[part][pl.ds(e, 1)]
+
+    pair[1].wait_recv()
+    for part, (first, groups, _) in enumerate(PARTS):
+        for g in range(groups):
+            lanes = slice((first + g) * 512, (first + g + 1) * 512)
+            sgs[part][pl.ds(their_rows[g], 16), :] = ps[:, lanes]
+
+    def gather(d, q, r):
+        columns = pl.ds(PIECES[q][0], PIECES[q][1])
+        if d == 0:
+            return remote(rows.at[r - 1, :, columns], rows.at[r, :, columns], ag_s.at[d, q, r], ag_r.at[d, q, r], ctx=right)
+        return remote(
+            rows.at[lax.rem(9 - r, 8), :, columns], rows.at[8 - r, :, columns], ag_s.at[d, q, r], ag_r.at[d, q, r], ctx=left
+        )
+
+    def reach(d, q):
+        return 4 if (q % 2 == 0) == (d == 0) else 3
+
+    for part, (first, groups, height) in enumerate(PARTS):
+        for i in range(1, 8):
+            box_in(part, i).wait_recv()
+        landed_rows = inboxes[part][...].reshape(8 * height, 512)
+        for g in range(groups):
+            rows[0, :, (first + g) * 512 : (first + g + 1) * 512] = jnp.dot(
+                squeeze_map(height, groups, g), landed_rows, preferred_element_type=jnp.float32
+            ).astype(jnp.bfloat16)
+        for q in (2 * part, 2 * part + 1):
+            for d in range(2):
+                gather(d, q, 1).start()
+    for copy in local:
+        copy.wait()
+    for copy in pair[2:]:
+        copy.wait_recv()
+
+    def swap(slot):
+        return remote(half.at[slot], half_other.at[slot], half_s.at[slot], half_r.at[slot], ctx=other)
+
+    def first_half(slot):
+        half[slot] = jnp.dot(rows[slot], w_in[...], preferred_element_type=jnp.float32)
+        swap(slot).start()
+
+    def second_half(slot):
+        swap(slot).wait_recv()
+        both = half[slot] + half_other[slot]
+        gate = both[:, :256]
+        hidden = (gate / (1.0 + jnp.exp(-gate)) * both[:, 256:]).astype(jnp.bfloat16)
+        total[slot] = jnp.dot(hidden, w_down[...], preferred_element_type=jnp.float32).astype(jnp.bfloat16)
+
+    first_half(0)
+    second_half(0)
+
+    def pass_on(m, step):
+        columns = pl.ds(SUBS[m][0], SUBS[m][1])
+        slot = step + 1 if m < 2 else 7 - step
+        return remote(
+            total.at[slot, :, columns], arrived.at[m, step], rs_s.at[m, step], rs_r.at[m, step], ctx=right if m < 2 else left
+        )
+
+    def turn(r, carry):
+        @pl.when(r <= 4)
+        def _():
+            for q in range(4):
+                for d in range(2):
+                    @pl.when(r <= reach(d, q))
+                    def _(d=d, q=q):
+                        gather(d, q, r).wait_recv()
+
+                    @pl.when(r + 1 <= reach(d, q))
+                    def _(d=d, q=q):
+                        gather(d, q, r + 1).start()
+
+            first_half(r)
+
+            @pl.when(r < 4)
+            def _():
+                first_half(8 - r)
+
+            second_half(r)
+
+            @pl.when(r < 4)
+            def _():
+                second_half(8 - r)
+
+        for m in (0, 2, 1, 3):
+            slot = r if m < 2 else 8 - r
+            columns = pl.ds(SUBS[m][0], SUBS[m][1])
+
+            @pl.when(r >= 2)
+            def _(m=m, slot=slot, columns=columns):
+                pass_on(m, r - 2).wait_recv()
+                total[slot, :, columns] = (
+                    total[slot, :, columns].astype(jnp.float32) + arrived[m, r - 2].astype(jnp.float32)
+                ).astype(jnp.bfloat16)
+
+            pass_on(m, r - 1).start()
+        return carry
+
+    lax.fori_loop(1, 8, turn, 0)
+    for m in (0, 2, 1, 3):
+        pass_on(m, 6).wait_recv()
+        columns = slice(SUBS[m][0], SUBS[m][0] + SUBS[m][1])
+        summed[:, columns] = (total[0, :, columns].astype(jnp.float32) + arrived[m, 6].astype(jnp.float32)).astype(jnp.bfloat16)
+
+    rets, backs, mixes, readies = (ret0, ret1), (back0, back1), (mix0, mix1), ready
+
+    def give(part, i):
+        return remote(
+            rets[part].at[lax.rem(e + i, 8)], backs[part].at[e], back_s.at[part, i], back_r.at[part, i], exp=lax.rem(e + i, 8)
+        )
+
+    def give_in(part, i):
+        source = lax.rem(e + 8 - i, 8)
+        return remote(rets[part].at[source], backs[part].at[source], back_s.at[part, i], back_r.at[part, i], exp=source)
+
+    for part, (first, groups, height) in enumerate(PARTS):
+        spread = jnp.zeros((8 * height, 512), jnp.float32)
+        for g in range(groups):
+            spread = spread + jnp.dot(
+                spread_map(height, groups, g), summed[:, (first + g) * 512 : (first + g + 1) * 512],
+                preferred_element_type=jnp.float32,
+            )
+        rets[part][...] = spread.astype(jnp.bfloat16).reshape(8, height, 512)
+        for i in range(1, 8):
+            give(part, i).start()
+        backs[part][pl.ds(e, 1)] = rets[part][pl.ds(e, 1)]
+    for part, (first, groups, height) in enumerate(PARTS):
+        for i in range(1, 8):
+            give_in(part, i).wait_recv()
+        span = groups * 32
+        mixed = jnp.dot(mixes[part][...], backs[part][...].reshape(8 * height, 512), preferred_element_type=jnp.float32)
+        combined = mixed[:span] + mixed[span:]
+        layer_out = (sgs[part][...].astype(jnp.float32) + combined).astype(jnp.bfloat16)
+        for g in range(groups):
+            for b in range(2):
+                readies[b, :, (first + g) * 512 : (first + g + 1) * 512] = layer_out[g * 32 + b * 16 : g * 32 + b * 16 + 16]
+
+    def hand(b, core):
+        return remote(ready.at[b], landed.at[core], fin_s.at[b], fin_r.at[core], pipe=over, ctx=2 * z + b)
+
+    for b in range(2):
+        hand(b, k).start()
+    for b in range(2):
+        hand(b, b).wait_recv()
+        out_ref[:, b * HALF : (b + 1) * HALF] = landed[b]
+
+    for b in range(2):
+        hand(b, k).wait_send()
+    for copy in pair:
+        copy.wait_send()
+    for part in range(2):
+        for i in range(1, 8):
+            box(part, i).wait_send()
+            give(part, i).wait_send()
+    for q in range(4):
+        for d in range(2):
+            def done(r, carry, d=d, q=q):
+                gather(d, q, r).wait_send()
+                return carry
+
+            lax.fori_loop(1, reach(d, q) + 1, done, 0)
+
+    def sent(step, carry):
+        for m in range(4):
+            pass_on(m, step).wait_send()
+        return carry
+
+    lax.fori_loop(0, 7, sent, 0)
+
+    def swapped(slot, carry):
+        swap(slot).wait_send()
+        return carry
+
+    lax.fori_loop(0, 8, swapped, 0)
+
+
+def slot_tables(ids, weights):
+    sels, mixes = [], []
+    chosen = ids.reshape(2, 32)
+    matches = (chosen[:, :, None] == jnp.arange(8, dtype=jnp.int32)).astype(jnp.int32)
+    rank = jnp.sum((jnp.cumsum(matches, axis=1) - matches) * matches, axis=2)
+    slot = (chosen * 8 + rank).reshape(32, 2)
+    for first, groups, height in PARTS:
+        row = np.arange(8 * height)
+        inner = row % height
+        row_group, row_block, row_slot = inner // 10, inner % 10 // 5, row // height * 8 + inner % 5
+        row_slot = np.where(inner < groups * 10, row_slot, -1)
+        col = np.arange(groups * 32)
+        same = (row_group[:, None] == col[None, :] // 32) & (row_block[:, None] == col[None, :] % 32 // 16)
+        tiled = jnp.tile(slot, (groups, 1))
+        tiled_weights = jnp.tile(weights, (groups, 1))
+        hit = (row_slot[:, None, None] == tiled[None]) & same[:, :, None]
+        sels.append(jnp.any(hit, axis=2).astype(jnp.bfloat16))
+        mix = jnp.sum(
+            jnp.where((row_slot[None, :, None] == tiled[:, None]) & same.T[:, :, None], tiled_weights[:, None, :], 0.0), axis=2
+        )
+        high = mix.astype(jnp.bfloat16)
+        low = (mix - high.astype(jnp.float32)).astype(jnp.bfloat16)
+        mixes.append(jnp.concatenate([high, low], axis=0))
+    return sels, mixes
+
+
+def experts(stream, gain, ids, weights, gate_cols, up_cols, down_rows):
+    packed = jnp.concatenate([ids.astype(jnp.float32), weights], axis=1)
+    partner = lax.ppermute(packed, "ctx", [(i, i ^ 1) for i in range(16)])
+    first = lax.rem(lax.axis_index("ctx"), 2) == 0
+    low, high = jnp.where(first, packed, partner), jnp.where(first, partner, packed)
+    both = jnp.concatenate([low, high], axis=0)
+    (sel0, sel1), (mix0, mix1) = slot_tables(both[:, :2].astype(jnp.int32), both[:, 2:])
+    bf, f32 = jnp.bfloat16, jnp.float32
+    vmem, any_space = pl.BlockSpec(memory_space=pltpu.VMEM), pl.BlockSpec(memory_space=pl.ANY)
+    dma = pltpu.SemaphoreType.DMA
+    return pl.pallas_call(
+        expert_kernel,
+        out_shape=jax.ShapeDtypeStruct((16, D), bf),
+        in_specs=[vmem] * 6 + [any_space] * 3,
+        out_specs=vmem,
+        scratch_shapes=[
+            pltpu.VMEM((16, D), bf), pltpu.VMEM((16, HALF), bf), pltpu.VMEM((16, HALF), bf),
+            pltpu.VMEM((128, 512), bf), pltpu.VMEM((96, 512), bf), pltpu.VMEM((128, 512), bf), pltpu.VMEM((96, 512), bf),
+            pltpu.VMEM((8, 48, 512), bf), pltpu.VMEM((8, 32, 512), bf), pltpu.VMEM((8, 48, 512), bf), pltpu.VMEM((8, 32, 512), bf),
+            pltpu.VMEM((HALF, 512), bf), pltpu.VMEM((256, HALF), bf),
+            pltpu.VMEM((8, 80, HALF), bf), pltpu.VMEM((8, 80, 512), f32), pltpu.VMEM((8, 80, 512), f32),
+            pltpu.VMEM((8, 80, HALF), bf), pltpu.VMEM((4, 7, 80, 896), bf), pltpu.VMEM((80, HALF), bf),
+            pltpu.VMEM((8, 48, 512), bf), pltpu.VMEM((8, 32, 512), bf), pltpu.VMEM((8, 48, 512), bf), pltpu.VMEM((8, 32, 512), bf),
+            pltpu.VMEM((2, 16, HALF), bf), pltpu.VMEM((2, 16, HALF), bf),
+            dma((5,)), dma((5,)), dma((3,)), dma((2, 8)), dma((2, 8)), dma((2, 4, 5)), dma((2, 4, 5)), dma((8,)), dma((8,)),
+            dma((4, 7)), dma((4, 7)), dma((2, 8)), dma((2, 8)), dma((2,)), dma((2,)),
+        ],
+        compiler_params=pltpu.CompilerParams(collective_id=3, has_side_effects=True, vmem_limit_bytes=56 << 20),
+        cost_estimate=pl.CostEstimate(flops=3_600_000_000, bytes_accessed=6_000_000, transcendentals=164_000),
+        name="experts",
+    )(stream, gain, sel0, sel1, mix0, mix1, gate_cols, up_cols, down_rows)
 
 
 def on_device(
@@ -103,47 +451,7 @@
         jnp.bfloat16
     )
     stream = lax.optimization_barrier(stream)
-    stream_wide = stream.astype(jnp.float32)
-    mean_square = jnp.mean(stream_wide * stream_wide, axis=1, keepdims=True)
-    normed = (stream_wide * lax.rsqrt(mean_square + epsilon) * norm_gain[0][None, :]).astype(
-        jnp.bfloat16
-    )
-    capacity = min(tok_count, max(2, (5 * tok_count * TOP + 4 * exp_count - 1) // (4 * exp_count)))
-    chosen_flat = expert_ids[0].reshape(-1)
-    matches = (chosen_flat[:, None] == jnp.arange(exp_count, dtype=jnp.int32)[None, :]).astype(
-        jnp.int32
-    )
-    earlier = jnp.sum((jnp.cumsum(matches, axis=0) - matches) * matches, axis=1)
-    slot_index = chosen_flat * capacity + earlier
-    slot_table = slot_index[None, :] == jnp.arange(exp_count * capacity, dtype=jnp.int32)[:, None]
-    slot_table = slot_table.reshape(exp_count * capacity, tok_count, TOP)
-    placing = jnp.sum(slot_table.astype(jnp.float32), axis=2).astype(jnp.bfloat16)
-    outbox = jnp.dot(placing, normed, preferred_element_type=jnp.float32).astype(jnp.bfloat16)
-    inbox = lax.all_to_all(
-        outbox.reshape(exp_count, capacity, D), "exp", split_axis=0, concat_axis=0, tiled=True
-    )
-    expert_in = inbox.reshape(exp_count * capacity, D)
-    gate_cols = gate_proj[0, 0]
-    up_cols = up_proj[0, 0]
-    down_rows = down_proj[0, 0]
-    block_in = lax.all_gather(expert_in, "ctx", axis=0, tiled=True)
-    gate_value = jnp.dot(block_in, gate_cols, preferred_element_type=jnp.float32)
-    up_value = jnp.dot(block_in, up_cols, preferred_element_type=jnp.float32)
-    hidden = (jax.nn.silu(gate_value) * up_value).astype(jnp.bfloat16)
-    expert_out = lax.psum_scatter(
-        jnp.dot(hidden, down_rows, preferred_element_type=jnp.float32).astype(jnp.bfloat16),
-        "ctx",
-        scatter_dimension=0,
-        tiled=True,
-    )
-    returned = lax.all_to_all(
-        expert_out.reshape(exp_count, capacity, D), "exp", split_axis=0, concat_axis=0, tiled=True
-    )
-    mixing = jnp.sum(jnp.where(slot_table, gate_weights[0][None, :, :], 0.0), axis=2)
-    returned_wide = returned.reshape(exp_count * capacity, D).astype(jnp.float32)
-    combined = jnp.dot(mixing.T, returned_wide, precision=lax.Precision.HIGHEST)
-    layer_out = (stream_wide + combined).astype(jnp.bfloat16)
-    return shifted(layer_out[None], "pipe", 1)
+    return experts(stream, norm_gain, expert_ids[0], gate_weights[0], gate_proj[0, 0], up_proj[0, 0], down_proj[0, 0])[None]
 
 
 def solution(mesh):

time: 375 us -> 309 us (0.82); the launches traced: 371 us -> 308 us
  waiting for transfers between devices: 238 us -> 107 us
  Pallas kernels: 0 us -> 121 us
  blocking collectives: 54.8 us -> 21.3 us
  matrix products: 28.8 us -> 12.5 us
    pallas_call x0 -> x1, Pallas kernels: none -> 121 us  [experts(): pl.pallas_call(expert_kernel, out_shape=jax.ShapeDtypeStruct((16, D), bf)...]
    reduce_scatter x1 -> x0, waiting for transfers between devices: 68 us -> none  [on_device(): lax.psum_scatter(jnp.dot(hidden, down_rows, preferred_element_type=jnp.fl...]
    all_gather x1 -> x0, waiting for transfers between devices: 54.6 us -> none  [on_device(): block_in = lax.all_gather(expert_in, 'ctx', axis=0, tiled=True)]
    all_to_all x2 -> x0, blocking collectives: 33.4 us -> none  [the longest x1 17.9 us: on_device(): lax.all_to_all(outbox.reshape(exp_count, capacity, D), 'exp', split_axis=...]
    dot_general x5 -> x0, matrix products: 16.2 us -> none  [the longest x1 6.78 us: on_device(): jnp.dot(block_in, gate_cols, preferred_element_type=jnp.float32)]
    reshape x4 -> x0, local copies, waits for them, and re-layouts: 5.29 us -> none  [the longest x1 2.26 us: on_device(): expert_in = inbox.reshape(exp_count * capacity, D)]
    reduce_scatter x1, waiting for transfers between devices: 37 us -> 32.5 us  [on_device(): lax.psum_scatter(jnp.dot(picked, column_proj, preferred_element_type=jnp....]
  transfers between devices with their start and end apart: 7 -> 5, of which waited for: 7 -> 5; matrix products, arithmetic and copies ran while one was open for 1% -> 2% of each run, Pallas kernels for 0% -> 0%
where the time goes in v1:
time: 309 us; the launch traced here: 308 us
  Pallas kernels  121 us (39%)
  waiting for transfers between devices  107 us (35%)
  blocking collectives  21.3 us (7%)
  between operations  14.1 us (5%)
  starting transfers between devices  13.9 us (4%)
  matrix products  12.5 us (4%)
  local copies, waits for them, and re-layouts  11.5 us (4%)
  other arithmetic  6.79 us (2%)
    pallas_call x1, Pallas kernels, experts(): pl.pallas_call(expert_kernel, out_shape=jax.ShapeDtypeStruct((16, D), bf)...  121 us
    all_gather x1, waiting for transfers between devices, on_device(): everyone = lax.all_gather(heads, 'ctx', axis=0, tiled=True)  40.7 us
    reduce_scatter x1, waiting for transfers between devices, on_device(): lax.psum_scatter(jnp.dot(picked, column_proj, preferred_element_type=jnp....  32.5 us
    all_gather x1, waiting for transfers between devices, on_device(): key_rows = lax.all_gather(latent_rows[0], 'ctx', axis=0, tiled=True)  22.7 us
    all_gather x1, blocking collectives, on_device(): key_docs = lax.all_gather(doc_ids[0], 'ctx', axis=0, tiled=True)  21.3 us
    all_to_all x1, starting transfers between devices, on_device(): lax.all_to_all(attn_part, 'ctx', split_axis=0, concat_axis=1, tiled=True)  13.3 us
    all_to_all x1, waiting for transfers between devices, on_device(): lax.all_to_all(attn_part, 'ctx', split_axis=0, concat_axis=1, tiled=True)  10.3 us
  transfers between devices with their start and end apart: 5, of which 5 were waited for; matrix products, arithmetic and copies ran while one was open for 2% of the time, Pallas kernels for 0%

profile of v1, /device:TPU:1, one launch (start us, length us, event | category | flops | bytes accessed | tf_op | source)
XLA Modules:
  0.0 308.3 jit_solution(9067042580046398301)
XLA Ops:
  6.5 1.8 copy.71
  9.8 21.3 %all-gather = s32[1,2048]{1,0:T(1,128)S(1)} all-gather(s32[1,128]{1,0:T(1,128)} %param.24), channel_id=2, replica_groups=mesh['pipe'=2,'ctx'=16,'exp'=8] {'ctx'}, dimensions={1}, use_global_device_ids=true | all-gather | bytes 8704 | tf_op jit(solution)/shard_map/all_gather | solution.py:399
  31.1 22.7 %all-gather.7.cloned.1.call-done = bf16[1,2048,576]{2,1,0:T(8,128)(2,1)} async-done(((bf16[1,128,576]{2,1,0:T(8,128)(2,1)}), bf16[1,2048,576]{2,1,0:T(8,128)(2,1)}) %all-gather.7.cloned.1.call-update) | async-done | bytes 2359312 | tf_op jit(solution)/shard_map/all_gather | solution.py:398
  53.8 11.5 %conditional.1 = (f32[8,128]{1,0:T(8,128)S(1)}, f32[8,128,512]{2,1,0:T(8,128)S(1)}) conditional(s32[]{:T(128)} %bitcast.6, () %tuple.13, (s32[128]{0:T(128)S(1)}, s32[2048]{0:T(1024)S(1)}, s32[1,128]{1,0:T(1,128)}, bf16[1,128,8,576]{1,3,2,0:T(8,128)(2,1)}, bf16[2048,576]{1,0:T(8,128)(2,1)}) %tuple.29), branch_computations={%region_0.0_spmd, %region_1.4_spmd} | conditional | flops 4591451136 | bytes 43418668 | solution.py:425
  53.8 1.0 fusion.11
  54.8 5.9 %fusion = (f32[8,128]{1,0:T(8,128)S(1)}, f32[2048,128,8]{1,0,2:T(8,128)S(1)}) fusion(pred[128,2048]{0,1:T(8,128)(4,1)S(1)} %fusion.11, bf16[1,128,8,576]{1,3,2,0:T(8,128)(2,1)} %get-tuple-element.26, bf16[2048,576]{1,0:T(8,128)(2,1)} %get-tuple-element.19), kind=kOutput, calls=%fused_computation.2 | convolution fusion | flops 2422209536 | bytes 12193792 | tf_op jit(solution)/shard_map/cond/branch_1_fun/qhc,kc->hqk/dot_general | solution.py:409
  60.8 2.0 fusion.2
  62.8 2.5 fusion.3
  65.3 0.7 convolution_convert_fusion.1
  66.0 0.8 copy.73
  66.9 40.7 %all-gather.5.cloned.1.call-done = bf16[2048,1024]{1,0:T(8,128)(2,1)} async-done(((bf16[128,1024]{1,0:T(8,128)(2,1)}), bf16[2048,1024]{1,0:T(8,128)(2,1)}) %all-gather.5.cloned.1.call-update) | async-done | bytes 4194320 | tf_op jit(solution)/shard_map/all_gather | solution.py:436
  107.7 2.7 copy.74
  110.5 3.4 %convolution_convert_fusion = bf16[2048,448]{0,1:T(8,128)(2,1)} fusion(bf16[2048,1024]{1,0:T(8,128)(2,1)S(1)} %bitcast.65, bf16[1,1024,448]{1,2,0:T(8,128)(2,1)S(1)} %copy-done.11), kind=kOutput, calls=%fused_computation.18 | convolution fusion | flops 1879965696 | bytes 6946816 | tf_op jit(solution)/shard_map/dot_general | solution.py:444
  114.5 0.8 collective-permute-done
  116.4 0.7 convert_element_type.91.sel0
  117.3 0.7 copy.79.sel1
  118.5 32.5 %reduce-scatter.2.cloned.1.call-done = bf16[256,448]{0,1:T(8,128)(2,1)} async-done(((bf16[2048,448]{0,1:T(8,128)(2,1)}), bf16[256,448]{0,1:T(8,128)(2,1)}) %reduce-scatter.2.cloned.1.call-update) | async-done | bytes 229392 | tf_op jit(solution)/shard_map/reduce_scatter | solution.py:443
  150.9 1.8 copy.75
  152.7 13.3 %all-to-all-start = ((bf16[16,16,448]{2,1,0:T(8,128)(2,1)}), bf16[16,16,448]{2,1,0:T(8,128)(2,1)S(1)}, u32[]{:S(2)}, u32[]{:S(2)}) async-start(bf16[16,16,448]{2,1,0:T(8,128)(2,1)} %bitcast.16), calls=%async_computation.1 | async-start | bytes 524288 | tf_op jit(solution)/shard_map/all_to_all | solution.py:449
  166.7 0.7 pad_maximum_fusion.mix0
  167.4 10.3 %all-to-all-done = bf16[16,16,448]{2,1,0:T(8,128)(2,1)S(1)} async-done(((bf16[16,16,448]{2,1,0:T(8,128)(2,1)}), bf16[16,16,448]{2,1,0:T(8,128)(2,1)S(1)}, u32[]{:S(2)}, u32[]{:S(2)}) %all-to-all-start) | async-done | bytes 229408 | tf_op jit(solution)/shard_map/all_to_all | solution.py:449
  178.3 0.7 fusion.17.stream_ref
  179.0 121.1 %experts.1 = bf16[16,7168]{1,0:T(8,128)(2,1)} custom-call(bf16[16,7168]{1,0:T(8,128)(2,1)} %fusion.17.stream_ref, f32[1,7168]{1,0:T(1,128)} %gain_ref.1, bf16[384,128]{1,0:T(8,128)(2,1)} %convert_element_type.91.sel0, bf16[256,96]{1,0:T(8,128)(2,1)} %copy.79.sel1, bf16[256,384]{1,0:T(8,128)(2,1)} %pad_maximum_fusion.mix0, ...), custom_call_target="tpu_custom_call" | custom-call | flops 3600000000 | bytes 6000000 | tf_op jit(solution)/shard_map/experts/pallas_call | solution.py:349
  300.2 1.6 copy.92
  (69 shorter events, 4.3 us)
Async XLA Ops:
  6.5 58.8 %copy-start = (bf16[1,8,512,128]{3,2,1,0:T(8,128)(2,1)S(1)}, bf16[1,8,512,128]{3,2,1,0:T(8,128)(2,1)}, u32[]{:S(2)}) copy-start(bf16[1,8,512,128]{3,2,1,0:T(8,128)(2,1)} %param.25) | copy-start | bytes 3145732
  6.5 47.3 %all-gather.7.cloned.1.call-start = ((), (), s32[]{:S(2)}) async-start(), calls=%async_computation.4 | async-start | bytes 2785280 | tf_op jit(solution)/shard_map/all_gather | solution.py:398
  8.4 99.3 %all-gather.5.cloned.1.call-start = ((), (), s32[]{:S(2)}) async-start(), calls=%async_computation.2 | async-start | bytes 4456448 | tf_op jit(solution)/shard_map/all_gather | solution.py:436
  60.7 2.0 copy-start.10
  66.9 84.1 %reduce-scatter.2.cloned.1.call-start = ((), (), s32[]{:S(2)}) async-start(), calls=%async_computation.3 | async-start | bytes 2064384 | tf_op jit(solution)/shard_map/reduce_scatter | solution.py:443
  107.7 2.7 copy-start.11
  110.4 3.5 %copy-start.9 = (s32[1,16,2]{1,2,0:T(2,128)S(1)}, s32[1,16,2]{1,2,0:T(2,128)}, u32[]{:S(2)}) copy-start(s32[1,16,2]{1,2,0:T(2,128)} %param.29) | copy-start | bytes 388
  110.4 3.5 %copy-start.8 = (f32[1,16,2]{1,2,0:T(2,128)S(1)}, f32[1,16,2]{1,2,0:T(2,128)}, u32[]{:S(2)}) copy-start(f32[1,16,2]{1,2,0:T(2,128)} %param.30) | copy-start | bytes 388
  110.4 4.0 %copy-start.5 = (pred[256,96]{0,1:T(32,128)(4,1)S(1)}, pred[256,96]{0,1:T(32,128)(4,1)}, u32[]{:S(2)}) copy-start(pred[256,96]{0,1:T(32,128)(4,1)} %constant.77) | copy-start | bytes 73732
  110.4 4.0 %copy-start.3 = (pred[128,384]{1,0:T(32,128)(4,1)S(1)}, pred[128,384]{1,0:T(32,128)(4,1)}, u32[]{:S(2)}) copy-start(pred[128,384]{1,0:T(32,128)(4,1)} %constant.79) | copy-start | bytes 147460
  110.4 4.1 %copy-start.4 = (pred[96,256]{1,0:T(32,128)(4,1)S(1)}, pred[96,256]{1,0:T(32,128)(4,1)}, u32[]{:S(2)}) copy-start(pred[96,256]{1,0:T(32,128)(4,1)} %constant.81) | copy-start | bytes 73732
  110.5 5.8 %copy-start.2 = (pred[384,128]{1,0:T(32,128)(4,1)S(1)}, pred[384,128]{1,0:T(32,128)(4,1)}, u32[]{:S(2)}) copy-start(pred[384,128]{1,0:T(32,128)(4,1)} %constant.75) | copy-start | bytes 147460
  110.5 5.8 %copy-start.6 = (s32[384]{0:T(512)S(1)}, s32[384]{0:T(512)}, u32[]{:S(2)}) copy-start(s32[384]{0:T(512)} %constant.74) | copy-start | bytes 4612
  110.5 6.7 %copy-start.7 = (s32[256]{0:T(256)S(1)}, s32[256]{0:T(256)}, u32[]{:S(2)}) copy-start(s32[256]{0:T(256)} %constant.76) | copy-start | bytes 3076
  113.9 64.4 %copy-start.1 = (bf16[1,16,7168]{2,1,0:T(8,128)(2,1)S(1)}, bf16[1,16,7168]{2,1,0:T(8,128)(2,1)}, u32[]{:S(2)}) copy-start(bf16[1,16,7168]{2,1,0:T(8,128)(2,1)} %param.27) | copy-start | bytes 688132
  113.9 1.4 collective-permute-start
  152.7 25.0 %all-to-all-start = ((bf16[16,16,448]{2,1,0:T(8,128)(2,1)}), bf16[16,16,448]{2,1,0:T(8,128)(2,1)S(1)}, u32[]{:S(2)}, u32[]{:S(2)}) async-start(bf16[16,16,448]{2,1,0:T(8,128)(2,1)} %bitcast.16), calls=%async_computation.1 | async-start | bytes 524288 | tf_op jit(solution)/shard_map/all_to_all | solution.py:449
Sparse Core Ops, SparseCore 0:
  9.2 44.5 all-gather.6
  67.0 40.6 all-gather.4
  114.0 36.8 reduce-scatter.1

commit v2 on v1

v2 whole, which is shorter than its diff:
```python
import math
import types

import jax
import jax.numpy as jnp
from jax import lax
from jax.experimental import pallas as pl
from jax.experimental.pallas import tpu as pltpu
from jax.sharding import PartitionSpec as P

D = 7168
HALF = D // 2
HD = 128
ROPE = 64
LAT = 512
KV = LAT + ROPE
MESH = pl.DeviceIdType.MESH

epsilon = 1e-06
masked_score = -1e30
score_scale = 1.0 / math.sqrt(HD + ROPE)


def remote(src, dst, send_sem, recv_sem, **device):
    return pltpu.make_async_remote_copy(
        src_ref=src,
        dst_ref=dst,
        send_sem=send_sem,
        recv_sem=recv_sem,
        device_id=device,
        device_id_type=MESH,
    )


def meet(peers):
    barrier = pltpu.get_barrier_semaphore()
    for device in peers:
        pl.semaphore_signal(barrier, 1, device_id=device, device_id_type=MESH)
    pl.semaphore_wait(barrier, len(peers))


def squeeze_map(rows, groups, group, dtype=jnp.bfloat16):
    row = lax.broadcasted_iota(jnp.int32, (80, 8 * rows), 0).astype(jnp.float32)
    col = lax.broadcasted_iota(jnp.int32, (80, 8 * rows), 1).astype(jnp.float32)
    source = jnp.floor((row + 0.5) * 0.1)
    want = source * rows + (row - source * 10) + group * 10
    return jnp.where(col == want, 1.0, 0.0).astype(dtype)


def spread_map(rows, groups, group, dtype=jnp.bfloat16):
    row = lax.broadcasted_iota(jnp.int32, (8 * rows, 80), 0).astype(jnp.float32)
    col = lax.broadcasted_iota(jnp.int32, (8 * rows, 80), 1).astype(jnp.float32)
    source = jnp.floor((col + 0.5) * 0.1)
    want = source * rows + (col - source * 10) + group * 10
    return jnp.where(row == want, 1.0, 0.0).astype(dtype)


PARTS = ((0, 4, 48), (4, 3, 32))
PIECES = ((0, 1024), (1024, 1024), (2048, 768), (2816, 768))
SUBS = ((0, 896), (896, 896), (1792, 896), (2688, 896))


def attend(w, q_ref, lat_ref, doc_ref, vu_ref, op_ref, residual_ref, start_rest):
    p, c, e = lax.axis_index("pipe"), lax.axis_index("ctx"), lax.axis_index("exp")
    k = lax.rem(c, 2)
    z = lax.div(c, 2)
    kk = 1 - k
    other = 2 * z + kk
    right = 2 * lax.rem(z + 1, 8) + k
    left = 2 * lax.rem(z + 7, 8) + k
    y = lax.div(e, 4)
    x = lax.rem(e, 4)
    bf, f32 = jnp.bfloat16, jnp.float32

    def chain(s, q):
        piece = pl.ds(q * 32, 32)
        return remote(w.keys.at[s - 1, k, piece], w.keys.at[s, k, piece], w.chain_s.at[s, q], w.chain_r.at[s, q], ctx=right)

    def share(s):
        return remote(w.keys.at[s, k], w.keys.at[s, k], w.share_s.at[s], w.share_r.at[s], ctx=other)

    def share_in(s):
        return remote(w.keys.at[s, kk], w.keys.at[s, kk], w.share_s.at[s], w.share_r.at[s], ctx=other)

    for q in range(4):
        chain(1, q).start()
    share(0).start()
    own_proj = pltpu.make_async_copy(op_ref, w.proj.at[k], w.load.at[8])
    own_proj.start()
    pair_proj = remote(op_ref, w.proj.at[k], w.proj_s.at[0], w.proj_r.at[0], ctx=other)
    pair_proj.start()
    up_loads = [
        pltpu.make_async_copy(vu_ref.at[h], w.value_up.at[:, pl.ds(h * 128, 128)], w.load.at[h]) for h in range(8)
    ]
    for copy in up_loads:
        copy.start()
    start_rest()

    def flatten(j, carry):
        block = q_ref[pl.ds(j * 16, 16)].astype(f32).reshape(128, KV)
        w.queries[pl.ds(pl.multiple_of(j * 128, 128), 128), :] = block.astype(bf)
        return carry

    lax.fori_loop(0, 8, flatten, 0)
    expand = lax.shift_right_logical(lax.broadcasted_iota(jnp.int32, (1024, 128), 0), 3) == lax.broadcasted_iota(
        jnp.int32, (1024, 128), 1
    )
    own_tail = w.keys[0, pl.ds(k, 1), :, 512:640].reshape(128, 128)
    own_docs = jnp.dot(jnp.where(expand, 1.0, 0.0).astype(bf), own_tail, preferred_element_type=f32)
    w.query_doc[...] = jnp.broadcast_to(own_docs[:, 64:65], (1024, 128))
    w.top[...] = jnp.full((1024, 128), masked_score, f32)
    w.sums[...] = jnp.zeros((1024, 128), f32)
    w.mixed[...] = jnp.zeros((1024, LAT), f32)
    picker = jnp.where(lax.broadcasted_iota(jnp.int32, (8, 128), 1) == 64, 1.0, 0.0).astype(bf)
    contract_last = (((1,), (1,)), ((), ()))

    def visit(s, carry):
        @pl.when(s >= 1)
        def _():
            for q in range(4):
                chain(s, q).wait_recv()

                @pl.when(s < 4)
                def _(q=q):
                    chain(s + 1, q).start()

            share(s).start()

        share_in(s).wait_recv()
        block = w.keys[s].reshape(256, 640)
        key_doc = lax.dot_general(picker, block[:, 512:640], contract_last, preferred_element_type=f32)[0:1]
        key_pos = lax.rem(z + 8 - s, 8) * 256 + lax.broadcasted_iota(jnp.int32, (256, 256), 1)

        def some(j, carry):
            at = pl.ds(pl.multiple_of(j * 256, 256), 256)
            scores = lax.dot_general(w.queries[at], block[:, :KV], contract_last, preferred_element_type=f32) * score_scale
            query_pos = c * 128 + j * 32 + lax.shift_right_logical(lax.broadcasted_iota(jnp.int32, (256, 256), 0), 3)
            query_doc = w.query_doc[at]
            allowed = (key_pos <= query_pos) & (jnp.concatenate([query_doc, query_doc], axis=1) == key_doc)
            scores = jnp.where(allowed, scores, masked_score)
            before = w.top[at]
            highest = jnp.maximum(before, jnp.max(scores, axis=1, keepdims=True))
            shrink = jnp.exp(before - highest)
            weights = jnp.where(allowed, jnp.exp(scores - jnp.concatenate([highest, highest], axis=1)), 0.0)
            w.top[at] = highest
            w.sums[at] = w.sums[at] * shrink + jnp.sum(weights, axis=1, keepdims=True)
            update = jnp.dot(weights.astype(bf), block[:, :LAT], preferred_element_type=f32)
            w.mixed[at] = w.mixed[at] * jnp.concatenate([shrink] * 4, axis=1) + update
            return carry

        lax.fori_loop(0, 4, some, 0)
        return carry

    lax.fori_loop(0, 5, visit, 0)

    for copy in up_loads:
        copy.wait()

    def gather(d, q, r):
        piece = pl.ds(q * 64, 64)
        if d == 0:
            return remote(w.heads.at[r - 1, piece], w.heads.at[r, piece], w.head_s.at[d, q, r], w.head_r.at[d, q, r], ctx=right)
        return remote(
            w.heads.at[lax.rem(9 - r, 8), piece], w.heads.at[8 - r, piece], w.head_s.at[d, q, r], w.head_r.at[d, q, r], ctx=left
        )

    def reach(d, q):
        return 4 if q == d else 3

    own_head = lax.shift_right_logical(lax.broadcasted_iota(jnp.int32, (256, 1024), 1), 7) == (
        lax.broadcasted_iota(jnp.int32, (256, 1024), 0) & 7
    )
    for q in range(2):
        def finish(j, carry):
            at = pl.ds(pl.multiple_of(j * 256, 256), 256)
            latent_out = (w.mixed[at] / jnp.concatenate([w.sums[at]] * 4, axis=1)).astype(bf)
            every = jnp.dot(latent_out, w.value_up[...], preferred_element_type=f32)
            chosen = jnp.sum(jnp.where(own_head, every, 0.0).reshape(32, 8, 1024), axis=1)
            w.heads[0, pl.ds(pl.multiple_of(j * 32, 32), 32), :] = chosen.astype(bf)
            return carry

        lax.fori_loop(2 * q, 2 * q + 2, finish, 0)
        for d in range(2):
            gather(d, q, 1).start()

    own_proj.wait()
    pair_proj.wait_recv()
    w.proj_all[:, 0:448] = w.proj[0]
    w.proj_all[:, 448:896] = w.proj[1]

    y_mine = pl.multiple_of(y * 64, 64)
    y_theirs = pl.multiple_of((1 - y) * 64, 64)
    x_mine = pl.multiple_of(x * 16, 16)

    def fold(slot):
        return remote(w.fold_out.at[slot], w.fold_in.at[slot], w.fold_s.at[slot], w.fold_r.at[slot], exp=lax.rem(e + 4, 8))

    def cross(slot, i):
        to = lax.rem(x + i, 4)
        return remote(
            w.cross_out.at[slot, pl.ds(pl.multiple_of(to * 16, 16), 16)], w.cross_in.at[slot, i - 1],
            w.cross_s.at[slot, i - 1], w.cross_r.at[slot, i - 1], exp=4 * y + to,
        )

    def deliver(slot):
        return remote(
            w.part_out.at[slot], w.parts.at[z], w.part_s.at[slot], w.part_r.at[slot], ctx=2 * lax.rem(z + 8 - slot, 8) + k
        )

    def deliver_in(slot):
        source = lax.rem(z + slot, 8)
        return remote(w.part_out.at[slot], w.parts.at[source], w.part_s.at[slot], w.part_r.at[slot], ctx=2 * source + k)

    def project(slot):
        w.product[slot] = jnp.dot(w.heads[slot], w.proj_all[...], preferred_element_type=f32)
        w.fold_out[slot] = w.product[slot, pl.ds(y_theirs, 64), :].astype(bf)
        fold(slot).start()

    def over_y(slot):
        fold(slot).wait_recv()
        both = w.product[slot, pl.ds(y_mine, 64), :] + w.fold_in[slot].astype(f32)
        w.product[slot, pl.ds(y_mine, 64), :] = both
        w.cross_out[slot] = both.astype(bf)
        for i in range(1, 4):
            cross(slot, i).start()

    def over_x(slot):
        whole = w.product[slot, pl.ds(pl.multiple_of(y_mine + x_mine, 16), 16), :]
        for i in range(1, 4):
            cross(slot, i).wait_recv()
            whole = whole + w.cross_in[slot, i - 1].astype(f32)
        w.part_out[slot] = whole.astype(bf)

        @pl.when(slot >= 1)
        def _():
            deliver(slot).start()

    def turn(r, carry):
        @pl.when((r >= 1) & (r <= 4))
        def _():
            for q in range(2):
                for d in range(2):
                    @pl.when(r <= reach(d, q))
                    def _(d=d, q=q):
                        gather(d, q, r).wait_recv()

                    @pl.when(r + 1 <= reach(d, q))
                    def _(d=d, q=q):
                        gather(d, q, r + 1).start()

        for stage, act in enumerate((project, over_y, over_x)):
            now = r - stage

            @pl.when((now >= 0) & (now <= 4))
            def _(act=act, now=now):
                act(now)

            @pl.when((now >= 1) & (now <= 3))
            def _(act=act, now=now):
                act(8 - now)

        return carry

    lax.fori_loop(0, 7, turn, 0)
    w.parts[pl.ds(z, 1)] = w.part_out[0:1]
    for slot in range(1, 8):
        deliver_in(slot).wait_recv()
    for other_z in range(8):
        columns = slice(other_z * 896, (other_z + 1) * 896)
        w.stream[:, columns] = (residual_ref[:, columns].astype(f32) + w.parts[other_z].astype(f32)).astype(bf)

    def settle():
        pair_proj.wait_send()

        def chained(s, carry):
            for q in range(4):
                chain(s, q).wait_send()
            return carry

        lax.fori_loop(1, 5, chained, 0)

        def shared(s, carry):
            share(s).wait_send()
            return carry

        lax.fori_loop(0, 5, shared, 0)
        for q in range(2):
            for d in range(2):
                def gathered(r, carry, d=d, q=q):
                    gather(d, q, r).wait_send()
                    return carry

                lax.fori_loop(1, reach(d, q) + 1, gathered, 0)

        def folded(slot, carry):
            fold(slot).wait_send()
            for i in range(1, 4):
                cross(slot, i).wait_send()

            @pl.when(slot >= 1)
            def _():
                deliver(slot).wait_send()
            return carry

        lax.fori_loop(0, 8, folded, 0)

    return settle


def tables(w, ids_ref, weights_ref, k):
    f32 = jnp.float32
    ids = ids_ref[...].astype(f32)
    lane = lax.broadcasted_iota(jnp.int32, (16, 128), 1)
    expert = lane.astype(f32)
    first, second = (jnp.where(ids[:, i : i + 1] == expert, 1.0, 0.0) for i in range(2))
    earlier = lax.broadcasted_iota(jnp.int32, (16, 16), 1) < lax.broadcasted_iota(jnp.int32, (16, 16), 0)
    counts = jnp.dot(jnp.where(earlier, 1.0, 0.0), first + second, preferred_element_type=f32)
    ranks = (
        jnp.sum(first * counts, axis=1, keepdims=True),
        jnp.sum(second * (counts + first), axis=1, keepdims=True),
    )
    weights = weights_ref[...]
    table = jnp.zeros((16, 128), f32)
    for i in range(2):
        table = jnp.where(lane == i, ids[:, i : i + 1] * 8.0 + ranks[i], table)
        table = jnp.where(lane == i + 2, weights[:, i : i + 1], table)
    w.table[pl.ds(k, 1)] = table[None]


def matrices(w):
    bf, f32 = jnp.bfloat16, jnp.float32
    both = w.table[...].reshape(32, 128)
    columns = jnp.concatenate([both] * 4, axis=0)
    lanes = jnp.transpose(columns)
    for part, (_, groups, height) in enumerate(PARTS):
        span, count = groups * 32, 8 * height

        def decode(shape, axis):
            row = lax.broadcasted_iota(jnp.int32, shape, axis).astype(f32)
            expert = jnp.floor((row + 0.5) * (1.0 / height))
            inner = row - expert * height
            group = jnp.floor((inner + 0.5) * 0.1)
            within = inner - group * 10.0
            block = jnp.where(within >= 5.0, 1.0, 0.0)
            slot = jnp.where(group < groups, expert * 8.0 + within - block * 5.0, -1.0)
            token = lax.broadcasted_iota(jnp.int32, shape, 1 - axis)
            owner = lax.shift_right_logical(token, 4).astype(f32)
            return slot, owner == group * 2.0 + block

        slot, same = decode((count, span), 0)
        hit = same & ((slot == lanes[0:1, :span]) | (slot == lanes[1:2, :span]))
        (w.sel0, w.sel1)[part][...] = jnp.where(hit, 1.0, 0.0).astype(bf)
        slot, same = decode((span, count), 1)
        weight = jnp.zeros((span, count), f32)
        for i in range(2):
            weight = weight + jnp.where(same & (slot == columns[:span, i : i + 1]), columns[:span, i + 2 : i + 3], 0.0)
        high = weight.astype(bf)
        mix = (w.mix0, w.mix1)[part]
        mix[0:span, :] = high
        mix[span : 2 * span, :] = (weight - high.astype(f32)).astype(bf)


def layer_kernel(
    q_ref, lat_ref, doc_ref, ids_ref, weights_ref, residual_ref, gain_ref, vu_ref, op_ref, gate_ref, up_ref, down_ref,
    out_ref, *scratch
):
    w = types.SimpleNamespace(**dict(zip(SCRATCH, scratch, strict=True)))
    p, c, e = lax.axis_index("pipe"), lax.axis_index("ctx"), lax.axis_index("exp")
    k = lax.rem(c, 2)
    z = lax.div(c, 2)
    kk = 1 - k
    other = 2 * z + kk
    right = 2 * lax.rem(z + 1, 8) + k
    left = 2 * lax.rem(z + 7, 8) + k
    over = 1 - p
    mine = pl.multiple_of(k * HALF, 128)
    theirs = pl.multiple_of(kk * HALF, 128)
    my_lane = pl.multiple_of(k * 128, 128)
    up_lane = pl.multiple_of(256 + k * 128, 128)

    bf, f32 = jnp.bfloat16, jnp.float32

    w.keys[0, pl.ds(k, 1), :, 0:KV] = lat_ref[...][None]
    diagonal = lax.broadcasted_iota(jnp.int32, (128, 128), 0) == lax.broadcasted_iota(jnp.int32, (128, 128), 1)
    doc_column = jnp.sum(jnp.where(diagonal, doc_ref[...].astype(f32), 0.0), axis=1, keepdims=True)
    w.keys[0, pl.ds(k, 1), :, KV:640] = jnp.broadcast_to(doc_column, (128, 640 - KV)).astype(bf)[None]
    tables(w, ids_ref, weights_ref, k)
    meet(
        [{"ctx": other}, {"pipe": over}, {"pipe": over, "ctx": other}]
        + [{"ctx": 2 * lax.rem(z + i, 8) + k} for i in range(1, 8)]
        + [{"exp": lax.rem(e + i, 8)} for i in range(1, 8)]
    )
    local = [
        pltpu.make_async_copy(gate_ref.at[pl.ds(mine, HALF), :], w.w_in.at[:, pl.ds(my_lane, 128)], w.loc.at[0]),
        pltpu.make_async_copy(up_ref.at[pl.ds(mine, HALF), :], w.w_in.at[:, pl.ds(up_lane, 128)], w.loc.at[1]),
        pltpu.make_async_copy(down_ref.at[:, pl.ds(mine, HALF)], w.w_down.at[pl.ds(my_lane, 128), :], w.loc.at[2]),
    ]
    pair = [
        remote(w.normed.at[:, pl.ds(theirs, HALF)], w.pn, w.pair_s.at[0], w.pair_r.at[0], ctx=other),
        remote(w.stream.at[:, pl.ds(theirs, HALF)], w.ps, w.pair_s.at[1], w.pair_r.at[1], ctx=other),
        remote(gate_ref.at[pl.ds(theirs, HALF), :], w.w_in.at[:, pl.ds(my_lane, 128)], w.pair_s.at[2], w.pair_r.at[2], ctx=other),
        remote(up_ref.at[pl.ds(theirs, HALF), :], w.w_in.at[:, pl.ds(up_lane, 128)], w.pair_s.at[3], w.pair_r.at[3], ctx=other),
        remote(down_ref.at[:, pl.ds(theirs, HALF)], w.w_down.at[pl.ds(my_lane, 128), :], w.pair_s.at[4], w.pair_r.at[4], ctx=other),
    ]
    pair.append(remote(w.table.at[k], w.table.at[k], w.pair_s.at[5], w.pair_r.at[5], ctx=other))

    def start_rest():
        pair[5].start()
        for copy in local:
            copy.start()
        for copy in pair[2:5]:
            copy.start()

    settle = attend(w, q_ref, lat_ref, doc_ref, vu_ref, op_ref, residual_ref, start_rest)
    wide = w.stream[...].astype(f32)
    mean_square = jnp.mean(wide * wide, axis=1, keepdims=True)
    w.normed[...] = (wide * lax.rsqrt(mean_square + epsilon) * gain_ref[...]).astype(bf)
    for copy in pair[:2]:
        copy.start()
    my_rows = [pl.multiple_of(g * 32 + k * 16, 16) for g in range(4)]
    their_rows = [pl.multiple_of(g * 32 + kk * 16, 16) for g in range(4)]
    xgs, sgs = (w.xg0, w.xg1), (w.sg0, w.sg1)
    for part, (first, groups, _) in enumerate(PARTS):
        for g in range(groups):
            lanes = pl.ds(pl.multiple_of(mine + (first + g) * 512, 128), 512)
            xgs[part][pl.ds(my_rows[g], 16), :] = w.normed[:, lanes]
            sgs[part][pl.ds(my_rows[g], 16), :] = w.stream[:, lanes]
    pair[5].wait_recv()
    matrices(w)
    pair[0].wait_recv()
    outboxes, inboxes, sels = (w.outbox0, w.outbox1), (w.inbox0, w.inbox1), (w.sel0, w.sel1)

    def box(part, i):
        return remote(
            outboxes[part].at[lax.rem(e + i, 8)], inboxes[part].at[e], w.box_s.at[part, i], w.box_r.at[part, i],
            exp=lax.rem(e + i, 8),
        )

    def box_in(part, i):
        source = lax.rem(e + 8 - i, 8)
        return remote(outboxes[part].at[source], inboxes[part].at[source], w.box_s.at[part, i], w.box_r.at[part, i], exp=source)

    for part, (first, groups, height) in enumerate(PARTS):
        for g in range(groups):
            lanes = slice((first + g) * 512, (first + g + 1) * 512)
            xgs[part][pl.ds(their_rows[g], 16), :] = w.pn[:, lanes]
        chosen = jnp.dot(sels[part][...], xgs[part][...], preferred_element_type=jnp.float32).astype(jnp.bfloat16)
        outboxes[part][...] = chosen.reshape(8, height, 512)
        for i in range(1, 8):
            box(part, i).start()
        inboxes[part][pl.ds(e, 1)] = outboxes[part][pl.ds(e, 1)]

    pair[1].wait_recv()
    for part, (first, groups, _) in enumerate(PARTS):
        for g in range(groups):
            lanes = slice((first + g) * 512, (first + g + 1) * 512)
            sgs[part][pl.ds(their_rows[g], 16), :] = w.ps[:, lanes]

    def gather(d, q, r):
        columns = pl.ds(PIECES[q][0], PIECES[q][1])
        if d == 0:
            return remote(w.rows.at[r - 1, :, columns], w.rows.at[r, :, columns], w.ag_s.at[d, q, r], w.ag_r.at[d, q, r], ctx=right)
        return remote(
            w.rows.at[lax.rem(9 - r, 8), :, columns], w.rows.at[8 - r, :, columns], w.ag_s.at[d, q, r], w.ag_r.at[d, q, r], ctx=left
        )

    def reach(d, q):
        return 4 if (q % 2 == 0) == (d == 0) else 3

    for part, (first, groups, height) in enumerate(PARTS):
        for i in range(1, 8):
            box_in(part, i).wait_recv()
        landed_rows = inboxes[part][...].reshape(8 * height, 512)
        for g in range(groups):
            w.rows[0, :, (first + g) * 512 : (first + g + 1) * 512] = jnp.dot(
                squeeze_map(height, groups, g), landed_rows, preferred_element_type=jnp.float32
            ).astype(jnp.bfloat16)
        for q in (2 * part, 2 * part + 1):
            for d in range(2):
                gather(d, q, 1).start()
    for copy in local:
        copy.wait()
    for copy in pair[2:5]:
        copy.wait_recv()

    def swap(slot):
        return remote(w.half.at[slot], w.half_other.at[slot], w.half_s.at[slot], w.half_r.at[slot], ctx=other)

    def first_half(slot):
        w.half[slot] = jnp.dot(w.rows[slot], w.w_in[...], preferred_element_type=jnp.float32)
        swap(slot).start()

    def second_half(slot):
        swap(slot).wait_recv()
        both = w.half[slot] + w.half_other[slot]
        gate = both[:, :256]
        hidden = (gate / (1.0 + jnp.exp(-gate)) * both[:, 256:]).astype(jnp.bfloat16)
        w.total[slot] = jnp.dot(hidden, w.w_down[...], preferred_element_type=jnp.float32).astype(jnp.bfloat16)

    first_half(0)
    second_half(0)

    def pass_on(m, step):
        columns = pl.ds(SUBS[m][0], SUBS[m][1])
        slot = step + 1 if m < 2 else 7 - step
        return remote(
            w.total.at[slot, :, columns], w.arrived.at[m, step], w.rs_s.at[m, step], w.rs_r.at[m, step], ctx=right if m < 2 else left
        )

    def turn(r, carry):
        @pl.when(r <= 4)
        def _():
            for q in range(4):
                for d in range(2):
                    @pl.when(r <= reach(d, q))
                    def _(d=d, q=q):
                        gather(d, q, r).wait_recv()

                    @pl.when(r + 1 <= reach(d, q))
                    def _(d=d, q=q):
                        gather(d, q, r + 1).start()

            first_half(r)

            @pl.when(r < 4)
            def _():
                first_half(8 - r)

            second_half(r)

            @pl.when(r < 4)
            def _():
                second_half(8 - r)

        for m in (0, 2, 1, 3):
            slot = r if m < 2 else 8 - r
            columns = pl.ds(SUBS[m][0], SUBS[m][1])

            @pl.when(r >= 2)
            def _(m=m, slot=slot, columns=columns):
                pass_on(m, r - 2).wait_recv()
                w.total[slot, :, columns] = (
                    w.total[slot, :, columns].astype(jnp.float32) + w.arrived[m, r - 2].astype(jnp.float32)
                ).astype(jnp.bfloat16)

            pass_on(m, r - 1).start()
        return carry

    lax.fori_loop(1, 8, turn, 0)
    for m in (0, 2, 1, 3):
        pass_on(m, 6).wait_recv()
        columns = slice(SUBS[m][0], SUBS[m][0] + SUBS[m][1])
        w.summed[:, columns] = (w.total[0, :, columns].astype(jnp.float32) + w.arrived[m, 6].astype(jnp.float32)).astype(jnp.bfloat16)

    rets, backs, mixes, readies = (w.ret0, w.ret1), (w.back0, w.back1), (w.mix0, w.mix1), w.ready

    def give(part, i):
        return remote(
            rets[part].at[lax.rem(e + i, 8)], backs[part].at[e], w.back_s.at[part, i], w.back_r.at[part, i], exp=lax.rem(e + i, 8)
        )

    def give_in(part, i):
        source = lax.rem(e + 8 - i, 8)
        return remote(rets[part].at[source], backs[part].at[source], w.back_s.at[part, i], w.back_r.at[part, i], exp=source)

    for part, (first, groups, height) in enumerate(PARTS):
        spread = jnp.zeros((8 * height, 512), jnp.float32)
        for g in range(groups):
            spread = spread + jnp.dot(
                spread_map(height, groups, g), w.summed[:, (first + g) * 512 : (first + g + 1) * 512],
                preferred_element_type=jnp.float32,
            )
        rets[part][...] = spread.astype(jnp.bfloat16).reshape(8, height, 512)
        for i in range(1, 8):
            give(part, i).start()
        backs[part][pl.ds(e, 1)] = rets[part][pl.ds(e, 1)]
    for part, (first, groups, height) in enumerate(PARTS):
        for i in range(1, 8):
            give_in(part, i).wait_recv()
        span = groups * 32
        mixed = jnp.dot(mixes[part][...], backs[part][...].reshape(8 * height, 512), preferred_element_type=jnp.float32)
        combined = mixed[:span] + mixed[span:]
        layer_out = (sgs[part][...].astype(jnp.float32) + combined).astype(jnp.bfloat16)
        for g in range(groups):
            for b in range(2):
                readies[b, :, (first + g) * 512 : (first + g + 1) * 512] = layer_out[g * 32 + b * 16 : g * 32 + b * 16 + 16]

    def hand(b, core):
        return remote(w.ready.at[b], w.landed.at[core], w.fin_s.at[b], w.fin_r.at[core], pipe=over, ctx=2 * z + b)

    for b in range(2):
        hand(b, k).start()
    for b in range(2):
        hand(b, b).wait_recv()
        out_ref[:, b * HALF : (b + 1) * HALF] = w.landed[b]

    for b in range(2):
        hand(b, k).wait_send()
    for copy in pair:
        copy.wait_send()
    for part in range(2):
        for i in range(1, 8):
            box(part, i).wait_send()
            give(part, i).wait_send()
    for q in range(4):
        for d in range(2):
            def done(r, carry, d=d, q=q):
                gather(d, q, r).wait_send()
                return carry

            lax.fori_loop(1, reach(d, q) + 1, done, 0)

    def sent(step, carry):
        for m in range(4):
            pass_on(m, step).wait_send()
        return carry

    lax.fori_loop(0, 7, sent, 0)

    def swapped(slot, carry):
        swap(slot).wait_send()
        return carry

    lax.fori_loop(0, 8, swapped, 0)
    settle()


BF, F32 = jnp.bfloat16, jnp.float32
SCRATCH = {
    "keys": ((5, 2, 128, 640), BF), "queries": ((1024, KV), BF), "query_doc": ((1024, 128), F32), "top": ((1024, 128), F32),
    "sums": ((1024, 128), F32), "mixed": ((1024, LAT), F32), "value_up": ((LAT, 1024), BF), "heads": ((8, 128, 1024), BF),
    "proj": ((2, 1024, 448), BF), "proj_all": ((1024, 896), BF), "product": ((8, 128, 896), F32),
    "fold_out": ((8, 64, 896), BF), "fold_in": ((8, 64, 896), BF), "cross_out": ((8, 64, 896), BF),
    "cross_in": ((8, 3, 16, 896), BF), "part_out": ((8, 16, 896), BF), "parts": ((8, 16, 896), BF), "stream": ((16, D), BF),
    "table": ((2, 16, 128), F32), "sel0": ((384, 128), BF), "sel1": ((256, 96), BF), "mix0": ((256, 384), BF), "mix1": ((192, 256), BF),
    "normed": ((16, D), BF), "pn": ((16, HALF), BF), "ps": ((16, HALF), BF),
    "xg0": ((128, 512), BF), "xg1": ((96, 512), BF), "sg0": ((128, 512), BF), "sg1": ((96, 512), BF),
    "outbox0": ((8, 48, 512), BF), "outbox1": ((8, 32, 512), BF), "inbox0": ((8, 48, 512), BF), "inbox1": ((8, 32, 512), BF),
    "w_in": ((HALF, 512), BF), "w_down": ((256, HALF), BF), "rows": ((8, 80, HALF), BF),
    "half": ((8, 80, 512), F32), "half_other": ((8, 80, 512), F32), "total": ((8, 80, HALF), BF),
    "arrived": ((4, 7, 80, 896), BF), "summed": ((80, HALF), BF),
    "ret0": ((8, 48, 512), BF), "ret1": ((8, 32, 512), BF), "back0": ((8, 48, 512), BF), "back1": ((8, 32, 512), BF),
    "ready": ((2, 16, HALF), BF), "landed": ((2, 16, HALF), BF),
    "load": ((9,), None), "chain_s": ((5, 4), None), "chain_r": ((5, 4), None), "share_s": ((5,), None), "share_r": ((5,), None),
    "proj_s": ((1,), None), "proj_r": ((1,), None), "head_s": ((2, 2, 5), None), "head_r": ((2, 2, 5), None),
    "fold_s": ((8,), None), "fold_r": ((8,), None), "cross_s": ((8, 3), None), "cross_r": ((8, 3), None),
    "part_s": ((8,), None), "part_r": ((8,), None),
    "pair_s": ((6,), None), "pair_r": ((6,), None), "loc": ((3,), None), "box_s": ((2, 8), None), "box_r": ((2, 8), None),
    "ag_s": ((2, 4, 5), None), "ag_r": ((2, 4, 5), None), "half_s": ((8,), None), "half_r": ((8,), None),
    "rs_s": ((4, 7), None), "rs_r": ((4, 7), None), "back_s": ((2, 8), None), "back_r": ((2, 8), None),
    "fin_s": ((2,), None), "fin_r": ((2,), None),
}


def on_device(
    queries, latent_rows, doc_ids, value_up, out_proj, residual_in, norm_gain, expert_ids, gate_weights, gate_proj, up_proj,
    down_proj,
):
    vmem, any_space = pl.BlockSpec(memory_space=pltpu.VMEM), pl.BlockSpec(memory_space=pl.ANY)
    return pl.pallas_call(
        layer_kernel,
        out_shape=jax.ShapeDtypeStruct((16, D), BF),
        in_specs=[vmem] * 7 + [any_space] * 5,
        out_specs=vmem,
        scratch_shapes=[
            pltpu.SemaphoreType.DMA(shape) if kind is None else pltpu.VMEM(shape, kind) for shape, kind in SCRATCH.values()
        ],
        compiler_params=pltpu.CompilerParams(collective_id=1, has_side_effects=True, vmem_limit_bytes=60 << 20),
        cost_estimate=pl.CostEstimate(flops=8_000_000_000, bytes_accessed=10_000_000, transcendentals=2_000_000),
        name="layer",
    )(
        queries[0], latent_rows[0], doc_ids, expert_ids[0], gate_weights[0], residual_in[0], norm_gain,
        value_up[0], out_proj[0], gate_proj[0, 0], up_proj[0, 0], down_proj[0, 0],
    )[None]


def solution(mesh):
    return jax.shard_map(
        on_device,
        mesh=mesh,
        in_specs=(
            P("pipe", "ctx", "exp", None),
            P("pipe", "ctx", None),
            P("pipe", "ctx"),
            P("pipe", "exp", None, None),
            P("pipe", "exp", "ctx"),
            P("pipe", ("ctx", "exp"), None),
            P("pipe", None),
            P("pipe", ("ctx", "exp"), None),
            P("pipe", ("ctx", "exp"), None),
            P("pipe", "exp", None, "ctx"),
            P("pipe", "exp", None, "ctx"),
            P("pipe", "exp", "ctx", None),
        ),
        out_specs=P("pipe", ("ctx", "exp"), None),
        check_vma=False,
    )
```

time: 309 us -> 206 us (0.67)
  waiting for transfers between devices: 107 us -> 0 us
  Pallas kernels: 121 us -> 195 us
  blocking collectives: 21.3 us -> 0 us
  between operations: 14.1 us -> 0.01 us
  starting transfers between devices: 13.9 us -> 0 us
  matrix products: 12.5 us -> 0 us
  other arithmetic: 6.79 us -> 0 us
    pallas_call x1, Pallas kernels: 121 us -> 195 us  [on_device(): pl.pallas_call(layer_kernel, out_shape=jax.ShapeDtypeStruct((16, D), BF),...]
    all_gather x2 -> x0, waiting for transfers between devices: 63.4 us -> none  [the longest x1 40.7 us: on_device(): everyone = lax.all_gather(heads, 'ctx', axis=0, tiled=True)]
    reduce_scatter x1 -> x0, waiting for transfers between devices: 32.5 us -> none  [on_device(): lax.psum_scatter(jnp.dot(picked, column_proj, preferred_element_type=jnp....]
    all_gather x1 -> x0, blocking collectives: 21.3 us -> none  [on_device(): key_docs = lax.all_gather(doc_ids[0], 'ctx', axis=0, tiled=True)]
    all_to_all x1 -> x0, starting transfers between devices: 13.3 us -> none  [on_device(): lax.all_to_all(attn_part, 'ctx', split_axis=0, concat_axis=1, tiled=True)]
    dot_general x4 -> x0, matrix products: 12.5 us -> none  [the longest x1 5.92 us: visit(): jnp.einsum('qhc,kc->hqk', query_rows, key_rows, preferred_element_type=jn...]
    all_to_all x1 -> x0, waiting for transfers between devices: 10.3 us -> none  [on_device(): lax.all_to_all(attn_part, 'ctx', split_axis=0, concat_axis=1, tiled=True)]
    unnamed x27 -> x6, local copies, waits for them, and re-layouts: 3.56 us -> 7.64 us
  transfers between devices with their start and end apart: 5 -> 0, of which waited for: 5 -> 0; matrix products, arithmetic and copies ran while one was open for 2% -> 0% of each run, Pallas kernels for 0% -> 0%
where the time goes in v2:
time: 206 us
  Pallas kernels  195 us (95%)
  local copies, waits for them, and re-layouts  10.4 us (5%)
    pallas_call x1, Pallas kernels, on_device(): pl.pallas_call(layer_kernel, out_shape=jax.ShapeDtypeStruct((16, D), BF),...  195 us
    unnamed x6, local copies, waits for them, and re-layouts  7.64 us

profile of v2, /device:TPU:1, one launch (start us, length us, event | category | flops | bytes accessed | tf_op | source)
XLA Modules:
  0.0 205.6 jit_solution(5701396862393123272)
XLA Ops:
  0.0 0.0 copy-start
  0.0 1.4 copy.16.ids_ref
  1.4 1.3 copy.17.weights_ref
  2.8 1.7 copy.14
  4.5 2.3 %copy.15 = bf16[1,1024,448]{2,1,0:T(8,128)(2,1)} copy(bf16[1,1024,448]{1,2,0:T(8,128)(2,1)} %param.16) | data formatting | bytes 1835008 | tf_op args[4]
  6.8 0.0 copy-done
  6.8 2.0 copy.13
  8.8 195.2 %layer.1 = bf16[16,7168]{1,0:T(8,128)(2,1)} custom-call(bf16[128,8,576]{2,1,0:T(8,128)(2,1)} %bitcast.11, bf16[128,576]{1,0:T(8,128)(2,1)} %bitcast.14, s32[1,128]{1,0:T(1,128)} %doc_ref.1, s32[16,2]{1,0:T(8,128)} %copy.16.ids_ref, f32[16,2]{1,0:T(8,128)} %copy.17.weights_ref, bf16[16,7168]{1,0:T(8,128)(2,1)} %bitcast.21, f32[1,7168]{1,0:T(1,128)} %gain_ref.1, ...), custom_call_target="tpu_custom_call" | custom-call | flops 8000000000 | bytes 10000000 | tf_op jit(solution)/shard_map/layer/pallas_call | solution.py:660
  204.0 1.6 copy.19
Async XLA Ops:
  0.0 6.8 %copy-start = (bf16[1,128,8,576]{1,3,2,0:T(8,128)(2,1)S(1)}, bf16[1,128,8,576]{1,3,2,0:T(8,128)(2,1)}, u32[]{:S(2)}) copy-start(bf16[1,128,8,576]{1,3,2,0:T(8,128)(2,1)} %param.12) | copy-start | bytes 3538948

commit v3 on v2

--- a/solution.py
+++ b/solution.py
@@ -19,6 +19,7 @@
 epsilon = 1e-06
 masked_score = -1e30
 score_scale = 1.0 / math.sqrt(HD + ROPE)
+KEY_PIECES = ((0, 144), (144, 144), (288, 144), (432, 160))
 
 
 def remote(src, dst, send_sem, recv_sem, **device):
@@ -71,48 +72,43 @@
     y = lax.div(e, 4)
     x = lax.rem(e, 4)
     bf, f32 = jnp.bfloat16, jnp.float32
+    my_lanes = pl.ds(pl.multiple_of(k * 128, 128), 128)
+    their_lanes = pl.ds(pl.multiple_of(kk * 128, 128), 128)
+    my_columns = pl.ds(pl.multiple_of(k * 448, 16), 448)
 
     def chain(s, q):
-        piece = pl.ds(q * 32, 32)
-        return remote(w.keys.at[s - 1, k, piece], w.keys.at[s, k, piece], w.chain_s.at[s, q], w.chain_r.at[s, q], ctx=right)
+        piece = pl.ds(*KEY_PIECES[q])
+        return remote(
+            w.keys.at[s - 1, piece, my_lanes], w.keys.at[s, piece, my_lanes], w.chain_s.at[s, q], w.chain_r.at[s, q], ctx=right
+        )
 
     def share(s):
-        return remote(w.keys.at[s, k], w.keys.at[s, k], w.share_s.at[s], w.share_r.at[s], ctx=other)
+        return remote(w.keys.at[s, :, my_lanes], w.keys.at[s, :, my_lanes], w.share_s.at[s], w.share_r.at[s], ctx=other)
 
     def share_in(s):
-        return remote(w.keys.at[s, kk], w.keys.at[s, kk], w.share_s.at[s], w.share_r.at[s], ctx=other)
+        return remote(w.keys.at[s, :, their_lanes], w.keys.at[s, :, their_lanes], w.share_s.at[s], w.share_r.at[s], ctx=other)
 
     for q in range(4):
         chain(1, q).start()
     share(0).start()
-    own_proj = pltpu.make_async_copy(op_ref, w.proj.at[k], w.load.at[8])
+    own_proj = pltpu.make_async_copy(op_ref, w.proj.at[my_columns], w.load.at[8])
     own_proj.start()
-    pair_proj = remote(op_ref, w.proj.at[k], w.proj_s.at[0], w.proj_r.at[0], ctx=other)
+    pair_proj = remote(op_ref, w.proj.at[my_columns], w.proj_s.at[0], w.proj_r.at[0], ctx=other)
     pair_proj.start()
     up_loads = [
-        pltpu.make_async_copy(vu_ref.at[h], w.value_up.at[:, pl.ds(h * 128, 128)], w.load.at[h]) for h in range(8)
+        pltpu.make_async_copy(vu_ref.at[h], w.value_up.at[h], w.load.at[h]) for h in range(8)
     ]
     for copy in up_loads:
         copy.start()
     start_rest()
 
-    def flatten(j, carry):
-        block = q_ref[pl.ds(j * 16, 16)].astype(f32).reshape(128, KV)
-        w.queries[pl.ds(pl.multiple_of(j * 128, 128), 128), :] = block.astype(bf)
-        return carry
-
-    lax.fori_loop(0, 8, flatten, 0)
-    expand = lax.shift_right_logical(lax.broadcasted_iota(jnp.int32, (1024, 128), 0), 3) == lax.broadcasted_iota(
-        jnp.int32, (1024, 128), 1
-    )
-    own_tail = w.keys[0, pl.ds(k, 1), :, 512:640].reshape(128, 128)
-    own_docs = jnp.dot(jnp.where(expand, 1.0, 0.0).astype(bf), own_tail, preferred_element_type=f32)
-    w.query_doc[...] = jnp.broadcast_to(own_docs[:, 64:65], (1024, 128))
+    for h in range(8):
+        w.queries[h * 128 : (h + 1) * 128, :] = jnp.transpose(q_ref[h])
     w.top[...] = jnp.full((1024, 128), masked_score, f32)
     w.sums[...] = jnp.zeros((1024, 128), f32)
     w.mixed[...] = jnp.zeros((1024, LAT), f32)
-    picker = jnp.where(lax.broadcasted_iota(jnp.int32, (8, 128), 1) == 64, 1.0, 0.0).astype(bf)
     contract_last = (((1,), (1,)), ((), ()))
+    query_pos = c * 128 + lax.broadcasted_iota(jnp.int32, (128, 256), 0)
 
     def visit(s, carry):
         @pl.when(s >= 1)
@@ -127,28 +123,26 @@
             share(s).start()
 
         share_in(s).wait_recv()
-        block = w.keys[s].reshape(256, 640)
-        key_doc = lax.dot_general(picker, block[:, 512:640], contract_last, preferred_element_type=f32)[0:1]
-        key_pos = lax.rem(z + 8 - s, 8) * 256 + lax.broadcasted_iota(jnp.int32, (256, 256), 1)
+        key_doc = w.keys[s, KV:, :].astype(f32)[0:1]
+        key_pos = lax.rem(z + 8 - s, 8) * 256 + lax.broadcasted_iota(jnp.int32, (128, 256), 1)
+        query_doc = jnp.concatenate([w.query_doc[...]] * 2, axis=1)
+        hidden = jnp.where((key_pos <= query_pos) & (query_doc == key_doc), 0.0, masked_score)
+        hidden = jnp.concatenate([hidden] * 4, axis=0)
 
         def some(j, carry):
-            at = pl.ds(pl.multiple_of(j * 256, 256), 256)
-            scores = lax.dot_general(w.queries[at], block[:, :KV], contract_last, preferred_element_type=f32) * score_scale
-            query_pos = c * 128 + j * 32 + lax.shift_right_logical(lax.broadcasted_iota(jnp.int32, (256, 256), 0), 3)
-            query_doc = w.query_doc[at]
-            allowed = (key_pos <= query_pos) & (jnp.concatenate([query_doc, query_doc], axis=1) == key_doc)
-            scores = jnp.where(allowed, scores, masked_score)
+            at = pl.ds(pl.multiple_of(j * 512, 512), 512)
+            scores = jnp.dot(w.queries[at], w.keys[s, 0:KV, :], preferred_element_type=f32) * score_scale + hidden
             before = w.top[at]
             highest = jnp.maximum(before, jnp.max(scores, axis=1, keepdims=True))
             shrink = jnp.exp(before - highest)
-            weights = jnp.where(allowed, jnp.exp(scores - jnp.concatenate([highest, highest], axis=1)), 0.0)
+            weights = jnp.exp(scores - jnp.concatenate([highest, highest], axis=1))
             w.top[at] = highest
             w.sums[at] = w.sums[at] * shrink + jnp.sum(weights, axis=1, keepdims=True)
-            update = jnp.dot(weights.astype(bf), block[:, :LAT], preferred_element_type=f32)
+            update = lax.dot_general(weights.astype(bf), w.keys[s, 0:LAT, :], contract_last, preferred_element_type=f32)
             w.mixed[at] = w.mixed[at] * jnp.concatenate([shrink] * 4, axis=1) + update
             return carry
 
-        lax.fori_loop(0, 4, some, 0)
+        lax.fori_loop(0, 2, some, 0)
         return carry
 
     lax.fori_loop(0, 5, visit, 0)
@@ -167,26 +161,17 @@
     def reach(d, q):
         return 4 if q == d else 3
 
-    own_head = lax.shift_right_logical(lax.broadcasted_iota(jnp.int32, (256, 1024), 1), 7) == (
-        lax.broadcasted_iota(jnp.int32, (256, 1024), 0) & 7
-    )
+    for h in range(8):
+        at = slice(h * 128, (h + 1) * 128)
+        latent_out = (w.mixed[at] / jnp.concatenate([w.sums[at]] * 4, axis=1)).astype(bf)
+        w.heads[0, :, at] = jnp.dot(latent_out, w.value_up[h], preferred_element_type=f32).astype(bf)
     for q in range(2):
-        def finish(j, carry):
-            at = pl.ds(pl.multiple_of(j * 256, 256), 256)
-            latent_out = (w.mixed[at] / jnp.concatenate([w.sums[at]] * 4, axis=1)).astype(bf)
-            every = jnp.dot(latent_out, w.value_up[...], preferred_element_type=f32)
-            chosen = jnp.sum(jnp.where(own_head, every, 0.0).reshape(32, 8, 1024), axis=1)
-            w.heads[0, pl.ds(pl.multiple_of(j * 32, 32), 32), :] = chosen.astype(bf)
-            return carry
-
-        lax.fori_loop(2 * q, 2 * q + 2, finish, 0)
         for d in range(2):
             gather(d, q, 1).start()
 
     own_proj.wait()
     pair_proj.wait_recv()
-    w.proj_all[:, 0:448] = w.proj[0]
-    w.proj_all[:, 448:896] = w.proj[1]
+    w.proj_all[...] = jnp.transpose(w.proj[...])
 
     y_mine = pl.multiple_of(y * 64, 64)
     y_theirs = pl.multiple_of((1 - y) * 64, 64)
@@ -307,23 +292,28 @@
     return settle
 
 
+def column_of(rows):
+    diagonal = lax.broadcasted_iota(jnp.int32, rows.shape, 0) == lax.broadcasted_iota(jnp.int32, rows.shape, 1)
+    return jnp.sum(jnp.where(diagonal, rows, 0.0), axis=1, keepdims=True)
+
+
 def tables(w, ids_ref, weights_ref, k):
     f32 = jnp.float32
-    ids = ids_ref[...].astype(f32)
+    ids = [column_of(jnp.broadcast_to(ids_ref[i : i + 1, :].astype(f32), (16, 16))) for i in range(2)]
+    weights = [column_of(jnp.broadcast_to(weights_ref[i : i + 1, :], (16, 16))) for i in range(2)]
     lane = lax.broadcasted_iota(jnp.int32, (16, 128), 1)
     expert = lane.astype(f32)
-    first, second = (jnp.where(ids[:, i : i + 1] == expert, 1.0, 0.0) for i in range(2))
+    first, second = (jnp.where(ids[i] == expert, 1.0, 0.0) for i in range(2))
     earlier = lax.broadcasted_iota(jnp.int32, (16, 16), 1) < lax.broadcasted_iota(jnp.int32, (16, 16), 0)
     counts = jnp.dot(jnp.where(earlier, 1.0, 0.0), first + second, preferred_element_type=f32)
     ranks = (
         jnp.sum(first * counts, axis=1, keepdims=True),
         jnp.sum(second * (counts + first), axis=1, keepdims=True),
     )
-    weights = weights_ref[...]
     table = jnp.zeros((16, 128), f32)
     for i in range(2):
-        table = jnp.where(lane == i, ids[:, i : i + 1] * 8.0 + ranks[i], table)
-        table = jnp.where(lane == i + 2, weights[:, i : i + 1], table)
+        table = jnp.where(lane == i, ids[i] * 8.0 + ranks[i], table)
+        table = jnp.where(lane == i + 2, weights[i], table)
     w.table[pl.ds(k, 1)] = table[None]
 
 
@@ -380,10 +370,10 @@
 
     bf, f32 = jnp.bfloat16, jnp.float32
 
-    w.keys[0, pl.ds(k, 1), :, 0:KV] = lat_ref[...][None]
-    diagonal = lax.broadcasted_iota(jnp.int32, (128, 128), 0) == lax.broadcasted_iota(jnp.int32, (128, 128), 1)
-    doc_column = jnp.sum(jnp.where(diagonal, doc_ref[...].astype(f32), 0.0), axis=1, keepdims=True)
-    w.keys[0, pl.ds(k, 1), :, KV:640] = jnp.broadcast_to(doc_column, (128, 640 - KV)).astype(bf)[None]
+    w.keys[0, 0:KV, pl.ds(my_lane, 128)] = lat_ref[...]
+    doc_row = jnp.broadcast_to(doc_ref[...].astype(f32), (128, 128))
+    w.keys[0, KV:, pl.ds(my_lane, 128)] = doc_row[0:16].astype(bf)
+    w.query_doc[...] = jnp.broadcast_to(column_of(doc_row), (128, 128))
     tables(w, ids_ref, weights_ref, k)
     meet(
         [{"ctx": other}, {"pipe": over}, {"pipe": over, "ctx": other}]
@@ -627,9 +617,9 @@
 
 BF, F32 = jnp.bfloat16, jnp.float32
 SCRATCH = {
-    "keys": ((5, 2, 128, 640), BF), "queries": ((1024, KV), BF), "query_doc": ((1024, 128), F32), "top": ((1024, 128), F32),
-    "sums": ((1024, 128), F32), "mixed": ((1024, LAT), F32), "value_up": ((LAT, 1024), BF), "heads": ((8, 128, 1024), BF),
-    "proj": ((2, 1024, 448), BF), "proj_all": ((1024, 896), BF), "product": ((8, 128, 896), F32),
+    "keys": ((5, KV + 16, 256), BF), "queries": ((1024, KV), BF), "query_doc": ((128, 128), F32), "top": ((1024, 128), F32),
+    "sums": ((1024, 128), F32), "mixed": ((1024, LAT), F32), "value_up": ((8, LAT, 128), BF), "heads": ((8, 128, 1024), BF),
+    "proj": ((896, 1024), BF), "proj_all": ((1024, 896), BF), "product": ((8, 128, 896), F32),
     "fold_out": ((8, 64, 896), BF), "fold_in": ((8, 64, 896), BF), "cross_out": ((8, 64, 896), BF),
     "cross_in": ((8, 3, 16, 896), BF), "part_out": ((8, 16, 896), BF), "parts": ((8, 16, 896), BF), "stream": ((16, D), BF),
     "table": ((2, 16, 128), F32), "sel0": ((384, 128), BF), "sel1": ((256, 96), BF), "mix0": ((256, 384), BF), "mix1": ((192, 256), BF),
@@ -669,8 +659,8 @@
         cost_estimate=pl.CostEstimate(flops=8_000_000_000, bytes_accessed=10_000_000, transcendentals=2_000_000),
         name="layer",
     )(
-        queries[0], latent_rows[0], doc_ids, expert_ids[0], gate_weights[0], residual_in[0], norm_gain,
-        value_up[0], out_proj[0], gate_proj[0, 0], up_proj[0, 0], down_proj[0, 0],
+        queries[0].transpose(1, 2, 0), latent_rows[0].T, doc_ids, expert_ids[0].T, gate_weights[0].T, residual_in[0], norm_gain,
+        value_up[0], out_proj[0].T, gate_proj[0, 0], up_proj[0, 0], down_proj[0, 0],
     )[None]
 
 

time: 206 us -> 193 us (0.937)
  local copies, waits for them, and re-layouts: 10.4 us -> 1.64 us
  Pallas kernels: 195 us -> 191 us
    unnamed x6 -> x1, local copies, waits for them, and re-layouts: 7.64 us -> 1.64 us
    pallas_call x1, Pallas kernels: 195 us -> 191 us  [on_device(): pl.pallas_call(layer_kernel, out_shape=jax.ShapeDtypeStruct((16, D), BF),...]
    squeeze x2 -> x0, local copies, waits for them, and re-layouts: 2.79 us -> none  [the longest x1 1.45 us: on_device(): expert_ids[0]]
where the time goes in v3:
time: 193 us
  Pallas kernels  191 us (99%)
    pallas_call x1, Pallas kernels, on_device(): pl.pallas_call(layer_kernel, out_shape=jax.ShapeDtypeStruct((16, D), BF),...  191 us

profile of v3, /device:TPU:1, one launch (start us, length us, event | category | flops | bytes accessed | tf_op | source)
XLA Modules:
  0.0 192.9 jit_solution(6597024782581614403)
XLA Ops:
  0.0 191.3 %layer.1 = bf16[16,7168]{1,0:T(8,128)(2,1)} custom-call(bf16[8,576,128]{2,1,0:T(8,128)(2,1)} %bitcast.25, bf16[576,128]{1,0:T(8,128)(2,1)} %bitcast.29, s32[1,128]{1,0:T(1,128)} %doc_ref.1, s32[2,16]{1,0:T(2,128)} %bitcast.30, f32[2,16]{1,0:T(2,128)} %bitcast.31, bf16[16,7168]{1,0:T(8,128)(2,1)} %bitcast.28, f32[1,7168]{1,0:T(1,128)} %gain_ref.1, ...), custom_call_target="tpu_custom_call" | custom-call | flops 8000000000 | bytes 10000000 | tf_op jit(solution)/shard_map/layer/pallas_call | solution.py:650
  191.3 1.6 copy.14

commit v4 on v3

--- a/solution.py
+++ b/solution.py
@@ -56,12 +56,16 @@
     return jnp.where(row == want, 1.0, 0.0).astype(dtype)
 
 
-PARTS = ((0, 4, 48), (4, 3, 32))
-PIECES = ((0, 1024), (1024, 1024), (2048, 768), (2816, 768))
-SUBS = ((0, 896), (896, 896), (1792, 896), (2688, 896))
-
-
-def attend(w, q_ref, lat_ref, doc_ref, vu_ref, op_ref, residual_ref, start_rest):
+RING = 2560
+GROUP = 640
+PLANE = HALF - RING
+
+
+def reach(d, q):
+    return 4 if q % 2 == d else 3
+
+
+def attend(w, q_ref, lat_ref, doc_ref, vu_ref, op_ref, residual_ref, start_rest, share_tables, make_tables):
     p, c, e = lax.axis_index("pipe"), lax.axis_index("ctx"), lax.axis_index("exp")
     k = lax.rem(c, 2)
     z = lax.div(c, 2)
@@ -146,6 +150,7 @@
         return carry
 
     lax.fori_loop(0, 5, visit, 0)
+    share_tables()
 
     for copy in up_loads:
         copy.wait()
@@ -158,9 +163,6 @@
             w.heads.at[lax.rem(9 - r, 8), piece], w.heads.at[8 - r, piece], w.head_s.at[d, q, r], w.head_r.at[d, q, r], ctx=left
         )
 
-    def reach(d, q):
-        return 4 if q == d else 3
-
     for h in range(8):
         at = slice(h * 128, (h + 1) * 128)
         latent_out = (w.mixed[at] / jnp.concatenate([w.sums[at]] * 4, axis=1)).astype(bf)
@@ -172,6 +174,7 @@
     own_proj.wait()
     pair_proj.wait_recv()
     w.proj_all[...] = jnp.transpose(w.proj[...])
+    make_tables()
 
     y_mine = pl.multiple_of(y * 64, 64)
     y_theirs = pl.multiple_of((1 - y) * 64, 64)
@@ -314,16 +317,16 @@
     for i in range(2):
         table = jnp.where(lane == i, ids[i] * 8.0 + ranks[i], table)
         table = jnp.where(lane == i + 2, weights[i], table)
-    w.table[pl.ds(k, 1)] = table[None]
+    w.table[0, pl.ds(k, 1)] = table[None]
 
 
 def matrices(w):
     bf, f32 = jnp.bfloat16, jnp.float32
-    both = w.table[...].reshape(32, 128)
-    columns = jnp.concatenate([both] * 4, axis=0)
-    lanes = jnp.transpose(columns)
-    for part, (_, groups, height) in enumerate(PARTS):
+    chip = jnp.concatenate([w.table[0].reshape(32, 128)] * 4, axis=0)
+    column = w.table[...].reshape(256, 128)
+    for columns, sel, mix, groups, height in ((chip, w.sel, w.mix, 4, 48), (column, w.plane_sel, w.plane_mix, 8, 80)):
         span, count = groups * 32, 8 * height
+        lanes = jnp.transpose(columns)
 
         def decode(shape, axis):
             row = lax.broadcasted_iota(jnp.int32, shape, axis).astype(f32)
@@ -333,19 +336,20 @@
             within = inner - group * 10.0
             block = jnp.where(within >= 5.0, 1.0, 0.0)
             slot = jnp.where(group < groups, expert * 8.0 + within - block * 5.0, -1.0)
-            token = lax.broadcasted_iota(jnp.int32, shape, 1 - axis)
-            owner = lax.shift_right_logical(token, 4).astype(f32)
-            return slot, owner == group * 2.0 + block
-
-        slot, same = decode((count, span), 0)
-        hit = same & ((slot == lanes[0:1, :span]) | (slot == lanes[1:2, :span]))
-        (w.sel0, w.sel1)[part][...] = jnp.where(hit, 1.0, 0.0).astype(bf)
-        slot, same = decode((span, count), 1)
+            owner = group * 2.0 + block
+            return slot, owner
+
+        slot, owner = decode((count, 1), 0)
+        token = lax.shift_right_logical(lax.broadcasted_iota(jnp.int32, (count, span), 1), 4).astype(f32)
+        hit = (owner == token) & ((slot == lanes[0:1, :]) | (slot == lanes[1:2, :]))
+        sel[...] = jnp.where(hit, 1.0, 0.0).astype(bf)
+        slot, owner = decode((1, count), 1)
+        token = lax.shift_right_logical(lax.broadcasted_iota(jnp.int32, (span, count), 0), 4).astype(f32)
+        slot = jnp.where(owner == token, slot, -1.0)
         weight = jnp.zeros((span, count), f32)
         for i in range(2):
-            weight = weight + jnp.where(same & (slot == columns[:span, i : i + 1]), columns[:span, i + 2 : i + 3], 0.0)
+            weight = weight + jnp.where(slot == columns[:, i : i + 1], columns[:, i + 2 : i + 3], 0.0)
         high = weight.astype(bf)
-        mix = (w.mix0, w.mix1)[part]
         mix[0:span, :] = high
         mix[span : 2 * span, :] = (weight - high.astype(f32)).astype(bf)
 
@@ -392,7 +396,7 @@
         remote(up_ref.at[pl.ds(theirs, HALF), :], w.w_in.at[:, pl.ds(up_lane, 128)], w.pair_s.at[3], w.pair_r.at[3], ctx=other),
         remote(down_ref.at[:, pl.ds(theirs, HALF)], w.w_down.at[pl.ds(my_lane, 128), :], w.pair_s.at[4], w.pair_r.at[4], ctx=other),
     ]
-    pair.append(remote(w.table.at[k], w.table.at[k], w.pair_s.at[5], w.pair_r.at[5], ctx=other))
+    pair.append(remote(w.table.at[0, k], w.table.at[0, k], w.pair_s.at[5], w.pair_r.at[5], ctx=other))
 
     def start_rest():
         pair[5].start()
@@ -401,73 +405,105 @@
         for copy in pair[2:5]:
             copy.start()
 
-    settle = attend(w, q_ref, lat_ref, doc_ref, vu_ref, op_ref, residual_ref, start_rest)
+    def spread_table(i):
+        return remote(w.table.at[0], w.table.at[i], w.table_s.at[i], w.table_r.at[i], ctx=2 * lax.rem(z + i, 8) + k)
+
+    def share_tables():
+        pair[5].wait_recv()
+        for i in range(1, 8):
+            spread_table(i).start()
+
+    def make_tables():
+        for i in range(1, 8):
+            spread_table(i).wait_recv()
+        matrices(w)
+
+    settle = attend(w, q_ref, lat_ref, doc_ref, vu_ref, op_ref, residual_ref, start_rest, share_tables, make_tables)
     wide = w.stream[...].astype(f32)
     mean_square = jnp.mean(wide * wide, axis=1, keepdims=True)
     w.normed[...] = (wide * lax.rsqrt(mean_square + epsilon) * gain_ref[...]).astype(bf)
     for copy in pair[:2]:
         copy.start()
-    my_rows = [pl.multiple_of(g * 32 + k * 16, 16) for g in range(4)]
-    their_rows = [pl.multiple_of(g * 32 + kk * 16, 16) for g in range(4)]
-    xgs, sgs = (w.xg0, w.xg1), (w.sg0, w.sg1)
-    for part, (first, groups, _) in enumerate(PARTS):
-        for g in range(groups):
-            lanes = pl.ds(pl.multiple_of(mine + (first + g) * 512, 128), 512)
-            xgs[part][pl.ds(my_rows[g], 16), :] = w.normed[:, lanes]
-            sgs[part][pl.ds(my_rows[g], 16), :] = w.stream[:, lanes]
-    pair[5].wait_recv()
-    matrices(w)
+
+    def place(target, plane_target, source, start, core):
+        for g in range(4):
+            lanes = pl.ds(start + g * GROUP if isinstance(start, int) else pl.multiple_of(start + g * GROUP, 128), GROUP)
+            target[pl.ds(pl.multiple_of(g * 32 + core * 16, 16), 16), :] = source[:, lanes]
+        lanes = pl.ds(start + RING if isinstance(start, int) else pl.multiple_of(start + RING, 128), PLANE)
+        plane_target[pl.ds(pl.multiple_of(core * 16, 16), 16), :] = source[:, lanes]
+
+    place(w.xg, w.tokens.at[0], w.normed, mine, k)
+    place(w.sg, w.plane_stream, w.stream, mine, k)
     pair[0].wait_recv()
-    outboxes, inboxes, sels = (w.outbox0, w.outbox1), (w.inbox0, w.inbox1), (w.sel0, w.sel1)
-
-    def box(part, i):
-        return remote(
-            outboxes[part].at[lax.rem(e + i, 8)], inboxes[part].at[e], w.box_s.at[part, i], w.box_r.at[part, i],
-            exp=lax.rem(e + i, 8),
-        )
-
-    def box_in(part, i):
+    place(w.xg, w.tokens.at[0], w.pn, 0, kk)
+
+    def relay(d, q, r):
+        columns = pl.ds(q * 512, 512)
+        src, dst, to = (r - 1, r, right) if d == 0 else (lax.rem(9 - r, 8), 8 - r, left)
+        return remote(w.tokens.at[src, :, columns], w.tokens.at[dst, :, columns], w.relay_s.at[d, q, r], w.relay_r.at[d, q, r], ctx=to)
+
+    def relay_round(r):
+        for q in range(2):
+            for d in range(2):
+                if r <= reach(d, q):
+                    relay(d, q, r).wait_recv()
+                if r + 1 <= reach(d, q):
+                    relay(d, q, r + 1).start()
+
+    for q in range(2):
+        for d in range(2):
+            relay(d, q, 1).start()
+
+    def box(i):
+        to = lax.rem(e + i, 8)
+        return remote(w.outbox.at[to], w.inbox.at[e], w.box_s.at[i], w.box_r.at[i], exp=to)
+
+    def box_in(i):
         source = lax.rem(e + 8 - i, 8)
-        return remote(outboxes[part].at[source], inboxes[part].at[source], w.box_s.at[part, i], w.box_r.at[part, i], exp=source)
-
-    for part, (first, groups, height) in enumerate(PARTS):
-        for g in range(groups):
-            lanes = slice((first + g) * 512, (first + g + 1) * 512)
-            xgs[part][pl.ds(their_rows[g], 16), :] = w.pn[:, lanes]
-        chosen = jnp.dot(sels[part][...], xgs[part][...], preferred_element_type=jnp.float32).astype(jnp.bfloat16)
-        outboxes[part][...] = chosen.reshape(8, height, 512)
+        return remote(w.outbox.at[source], w.inbox.at[source], w.box_s.at[i], w.box_r.at[i], exp=source)
+
+    chosen = jnp.dot(w.sel[...], w.xg[...], preferred_element_type=f32).astype(bf)
+    w.outbox[...] = chosen.reshape(8, 48, GROUP)
+    for i in range(1, 8):
+        box(i).start()
+    w.inbox[pl.ds(e, 1)] = w.outbox[pl.ds(e, 1)]
+    relay_round(1)
+    relay_round(2)
+    pair[1].wait_recv()
+    place(w.sg, w.plane_stream, w.ps, 0, kk)
+
+    def gather(d, q, r):
+        columns = pl.ds(q * GROUP, GROUP)
+        src, dst, to = (r - 1, r, right) if d == 0 else (lax.rem(9 - r, 8), 8 - r, left)
+        return remote(w.rows.at[src, :, columns], w.rows.at[dst, :, columns], w.ag_s.at[d, q, r], w.ag_r.at[d, q, r], ctx=to)
+
+    for i in range(1, 8):
+        box_in(i).wait_recv()
+    landed_rows = w.inbox[...].reshape(384, GROUP)
+    for q in range(4):
+        w.rows[0, :, q * GROUP : (q + 1) * GROUP] = jnp.dot(
+            squeeze_map(48, 4, q), landed_rows, preferred_element_type=f32
+        ).astype(bf)
+        for d in range(2):
+            gather(d, q, 1).start()
+    relay_round(3)
+    relay_round(4)
+
+    def plane_box(h, i):
+        to = lax.rem(e + i, 8)
+        return remote(w.plane_out.at[h, to], w.plane_in.at[h, e], w.plane_s.at[h, i], w.plane_r.at[h, i], exp=to)
+
+    def plane_box_in(h, i):
+        source = lax.rem(e + 8 - i, 8)
+        return remote(w.plane_out.at[h, source], w.plane_in.at[h, source], w.plane_s.at[h, i], w.plane_r.at[h, i], exp=source)
+
+    for h in range(2):
+        tokens = w.tokens[:, :, h * 512 : (h + 1) * 512].reshape(256, 512)
+        chosen = jnp.dot(w.plane_sel[...], tokens, preferred_element_type=f32).astype(bf)
+        w.plane_out[h] = chosen.reshape(8, 80, 512)
         for i in range(1, 8):
-            box(part, i).start()
-        inboxes[part][pl.ds(e, 1)] = outboxes[part][pl.ds(e, 1)]
-
-    pair[1].wait_recv()
-    for part, (first, groups, _) in enumerate(PARTS):
-        for g in range(groups):
-            lanes = slice((first + g) * 512, (first + g + 1) * 512)
-            sgs[part][pl.ds(their_rows[g], 16), :] = w.ps[:, lanes]
-
-    def gather(d, q, r):
-        columns = pl.ds(PIECES[q][0], PIECES[q][1])
-        if d == 0:
-            return remote(w.rows.at[r - 1, :, columns], w.rows.at[r, :, columns], w.ag_s.at[d, q, r], w.ag_r.at[d, q, r], ctx=right)
-        return remote(
-            w.rows.at[lax.rem(9 - r, 8), :, columns], w.rows.at[8 - r, :, columns], w.ag_s.at[d, q, r], w.ag_r.at[d, q, r], ctx=left
-        )
-
-    def reach(d, q):
-        return 4 if (q % 2 == 0) == (d == 0) else 3
-
-    for part, (first, groups, height) in enumerate(PARTS):
-        for i in range(1, 8):
-            box_in(part, i).wait_recv()
-        landed_rows = inboxes[part][...].reshape(8 * height, 512)
-        for g in range(groups):
-            w.rows[0, :, (first + g) * 512 : (first + g + 1) * 512] = jnp.dot(
-                squeeze_map(height, groups, g), landed_rows, preferred_element_type=jnp.float32
-            ).astype(jnp.bfloat16)
-        for q in (2 * part, 2 * part + 1):
-            for d in range(2):
-                gather(d, q, 1).start()
+            plane_box(h, i).start()
+        w.plane_in[h, pl.ds(e, 1)] = w.plane_out[h, pl.ds(e, 1)]
     for copy in local:
         copy.wait()
     for copy in pair[2:5]:
@@ -476,136 +512,245 @@
     def swap(slot):
         return remote(w.half.at[slot], w.half_other.at[slot], w.half_s.at[slot], w.half_r.at[slot], ctx=other)
 
-    def first_half(slot):
-        w.half[slot] = jnp.dot(w.rows[slot], w.w_in[...], preferred_element_type=jnp.float32)
+    def ring_half(slot):
+        w.half[slot] = jnp.dot(w.rows[slot], w.w_in[0:RING, :], preferred_element_type=f32)
+
+    ring_half(0)
+
+    def collect(r, carry):
+        for q in range(4):
+            for d in range(2):
+                @pl.when(r <= reach(d, q))
+                def _(d=d, q=q):
+                    gather(d, q, r).wait_recv()
+
+                @pl.when(r + 1 <= reach(d, q))
+                def _(d=d, q=q):
+                    gather(d, q, r + 1).start()
+
+        ring_half(r)
+
+        @pl.when(r < 4)
+        def _():
+            ring_half(8 - r)
+
+        return carry
+
+    lax.fori_loop(1, 5, collect, 0)
+    for h in range(2):
+        for i in range(1, 8):
+            plane_box_in(h, i).wait_recv()
+
+    def plane_half(slot):
+        pick = squeeze_map(80, 8, slot)
+        total = w.half[slot]
+        for h in range(2):
+            mine_now = jnp.dot(pick, w.plane_in[h].reshape(640, 512), preferred_element_type=f32).astype(bf)
+            total = total + jnp.dot(mine_now, w.w_in[RING + h * 512 : RING + (h + 1) * 512, :], preferred_element_type=f32)
+        w.half[slot] = total
         swap(slot).start()
+
+    w.hidden[...] = jnp.zeros((640, 256), f32)
 
     def second_half(slot):
         swap(slot).wait_recv()
         both = w.half[slot] + w.half_other[slot]
         gate = both[:, :256]
-        hidden = (gate / (1.0 + jnp.exp(-gate)) * both[:, 256:]).astype(jnp.bfloat16)
-        w.total[slot] = jnp.dot(hidden, w.w_down[...], preferred_element_type=jnp.float32).astype(jnp.bfloat16)
-
-    first_half(0)
-    second_half(0)
-
-    def pass_on(m, step):
-        columns = pl.ds(SUBS[m][0], SUBS[m][1])
-        slot = step + 1 if m < 2 else 7 - step
-        return remote(
-            w.total.at[slot, :, columns], w.arrived.at[m, step], w.rs_s.at[m, step], w.rs_r.at[m, step], ctx=right if m < 2 else left
-        )
-
-    def turn(r, carry):
-        @pl.when(r <= 4)
+        hidden = (gate / (1.0 + jnp.exp(-gate)) * both[:, 256:]).astype(bf)
+        w.total[slot] = jnp.dot(hidden, w.w_down[:, 0:RING], preferred_element_type=f32).astype(bf)
+        w.hidden[...] = w.hidden[...] + jnp.dot(spread_map(80, 8, slot), hidden, preferred_element_type=f32)
+
+    def scatter(d, q, j):
+        far = reach(d, q) + 1 - j
+        slot, to = (far, left) if d == 0 else (8 - far, right)
+        columns = pl.ds(q * GROUP, GROUP)
+        return remote(w.total.at[slot, :, columns], w.arrived.at[d, q, j - 1], w.rs_s.at[d, q, j - 1], w.rs_r.at[d, q, j - 1], ctx=to)
+
+    def scatter_on(j):
+        for q in range(4):
+            for d in range(2):
+                if j + 1 <= reach(d, q):
+                    far = reach(d, q) - j
+                    slot = far if d == 0 else 8 - far
+                    columns = slice(q * GROUP, (q + 1) * GROUP)
+                    scatter(d, q, j).wait_recv()
+                    w.total[slot, :, columns] = (
+                        w.total[slot, :, columns].astype(f32) + w.arrived[d, q, j - 1].astype(f32)
+                    ).astype(bf)
+                    scatter(d, q, j + 1).start()
+
+    def place_of(i):
+        step = lax.div(i + 1, 2)
+        return jnp.where(lax.rem(i, 2) == 0, 4 + step, 4 - step)
+
+    def work(i, carry):
+        @pl.when(i < 8)
+        def _():
+            plane_half(place_of(i))
+
+        @pl.when(i >= 1)
+        def _():
+            second_half(place_of(i - 1))
+
+        @pl.when(i == 3)
         def _():
             for q in range(4):
                 for d in range(2):
-                    @pl.when(r <= reach(d, q))
-                    def _(d=d, q=q):
-                        gather(d, q, r).wait_recv()
-
-                    @pl.when(r + 1 <= reach(d, q))
-                    def _(d=d, q=q):
-                        gather(d, q, r + 1).start()
-
-            first_half(r)
-
-            @pl.when(r < 4)
-            def _():
-                first_half(8 - r)
-
-            second_half(r)
-
-            @pl.when(r < 4)
-            def _():
-                second_half(8 - r)
-
-        for m in (0, 2, 1, 3):
-            slot = r if m < 2 else 8 - r
-            columns = pl.ds(SUBS[m][0], SUBS[m][1])
-
-            @pl.when(r >= 2)
-            def _(m=m, slot=slot, columns=columns):
-                pass_on(m, r - 2).wait_recv()
-                w.total[slot, :, columns] = (
-                    w.total[slot, :, columns].astype(jnp.float32) + w.arrived[m, r - 2].astype(jnp.float32)
-                ).astype(jnp.bfloat16)
-
-            pass_on(m, r - 1).start()
+                    scatter(d, q, 1).start()
+
         return carry
 
-    lax.fori_loop(1, 8, turn, 0)
-    for m in (0, 2, 1, 3):
-        pass_on(m, 6).wait_recv()
-        columns = slice(SUBS[m][0], SUBS[m][0] + SUBS[m][1])
-        w.summed[:, columns] = (w.total[0, :, columns].astype(jnp.float32) + w.arrived[m, 6].astype(jnp.float32)).astype(jnp.bfloat16)
-
-    rets, backs, mixes, readies = (w.ret0, w.ret1), (w.back0, w.back1), (w.mix0, w.mix1), w.ready
-
-    def give(part, i):
+    lax.fori_loop(0, 9, work, 0)
+
+    def plane_give(h, i):
+        to = lax.rem(e + i, 8)
+        return remote(w.plane_ret.at[h, to], w.plane_back.at[h, e], w.give_s.at[h, i], w.give_r.at[h, i], exp=to)
+
+    def plane_give_in(h, i):
+        source = lax.rem(e + 8 - i, 8)
+        return remote(w.plane_ret.at[h, source], w.plane_back.at[h, source], w.give_s.at[h, i], w.give_r.at[h, i], exp=source)
+
+    hidden = w.hidden[...].astype(bf)
+    for h in range(2):
+        out = jnp.dot(hidden, w.w_down[:, RING + h * 512 : RING + (h + 1) * 512], preferred_element_type=f32).astype(bf)
+        w.plane_ret[h] = out.reshape(8, 80, 512)
+        for i in range(1, 8):
+            plane_give(h, i).start()
+        w.plane_back[h, pl.ds(e, 1)] = w.plane_ret[h, pl.ds(e, 1)]
+
+    def reduce(h, d, q, j):
+        far = reach(d, q) + 1 - j
+        slot, to = (far, left) if d == 0 else (8 - far, right)
+        columns = pl.ds(h * 512 + q * 256, 256)
         return remote(
-            rets[part].at[lax.rem(e + i, 8)], backs[part].at[e], w.back_s.at[part, i], w.back_r.at[part, i], exp=lax.rem(e + i, 8)
+            w.partial.at[slot, :, columns], w.plane_arrived.at[h, d, q, j - 1], w.red_s.at[h, d, q, j - 1],
+            w.red_r.at[h, d, q, j - 1], ctx=to,
         )
 
-    def give_in(part, i):
+    def reduce_start(h):
+        for i in range(1, 8):
+            plane_give_in(h, i).wait_recv()
+        mixed = jnp.dot(w.plane_mix[...], w.plane_back[h].reshape(640, 512), preferred_element_type=f32)
+        mixed = mixed[:256] + mixed[256:]
+        w.plane_own[:, h * 512 : (h + 1) * 512] = mixed[:32]
+        w.partial[:, :, h * 512 : (h + 1) * 512] = mixed.astype(bf).reshape(8, 32, 512)
+        for q in range(2):
+            for d in range(2):
+                reduce(h, d, q, 1).start()
+
+    def reduce_on(h, j):
+        for q in range(2):
+            for d in range(2):
+                if j + 1 <= reach(d, q):
+                    far = reach(d, q) - j
+                    slot = far if d == 0 else 8 - far
+                    columns = slice(h * 512 + q * 256, h * 512 + (q + 1) * 256)
+                    reduce(h, d, q, j).wait_recv()
+                    w.partial[slot, :, columns] = (
+                        w.partial[slot, :, columns].astype(f32) + w.plane_arrived[h, d, q, j - 1].astype(f32)
+                    ).astype(bf)
+                    reduce(h, d, q, j + 1).start()
+
+    def reduce_end(h):
+        for q in range(2):
+            columns = slice(h * 512 + q * 256, h * 512 + (q + 1) * 256)
+            whole = w.plane_own[:, columns] + w.plane_stream[:, columns].astype(f32)
+            for d in range(2):
+                reduce(h, d, q, reach(d, q)).wait_recv()
+                whole = whole + w.plane_arrived[h, d, q, reach(d, q) - 1].astype(f32)
+            whole = whole.astype(bf)
+            for b in range(2):
+                w.ready[b, :, RING + h * 512 + q * 256 : RING + h * 512 + (q + 1) * 256] = whole[b * 16 : (b + 1) * 16]
+
+    def give(i):
+        to = lax.rem(e + i, 8)
+        return remote(w.ret.at[to], w.back.at[e], w.back_s.at[i], w.back_r.at[i], exp=to)
+
+    def give_in(i):
         source = lax.rem(e + 8 - i, 8)
-        return remote(rets[part].at[source], backs[part].at[source], w.back_s.at[part, i], w.back_r.at[part, i], exp=source)
-
-    for part, (first, groups, height) in enumerate(PARTS):
-        spread = jnp.zeros((8 * height, 512), jnp.float32)
-        for g in range(groups):
-            spread = spread + jnp.dot(
-                spread_map(height, groups, g), w.summed[:, (first + g) * 512 : (first + g + 1) * 512],
-                preferred_element_type=jnp.float32,
-            )
-        rets[part][...] = spread.astype(jnp.bfloat16).reshape(8, height, 512)
-        for i in range(1, 8):
-            give(part, i).start()
-        backs[part][pl.ds(e, 1)] = rets[part][pl.ds(e, 1)]
-    for part, (first, groups, height) in enumerate(PARTS):
-        for i in range(1, 8):
-            give_in(part, i).wait_recv()
-        span = groups * 32
-        mixed = jnp.dot(mixes[part][...], backs[part][...].reshape(8 * height, 512), preferred_element_type=jnp.float32)
-        combined = mixed[:span] + mixed[span:]
-        layer_out = (sgs[part][...].astype(jnp.float32) + combined).astype(jnp.bfloat16)
-        for g in range(groups):
-            for b in range(2):
-                readies[b, :, (first + g) * 512 : (first + g + 1) * 512] = layer_out[g * 32 + b * 16 : g * 32 + b * 16 + 16]
-
-    def hand(b, core):
-        return remote(w.ready.at[b], w.landed.at[core], w.fin_s.at[b], w.fin_r.at[core], pipe=over, ctx=2 * z + b)
+        return remote(w.ret.at[source], w.back.at[source], w.back_s.at[i], w.back_r.at[i], exp=source)
+
+    scatter_on(1)
+    scatter_on(2)
+    reduce_start(0)
+    scatter_on(3)
+    reduce_on(0, 1)
+    reduce_start(1)
+    reduce_on(0, 2)
+    spread = jnp.zeros((384, GROUP), f32)
+    for q in range(4):
+        columns = slice(q * GROUP, (q + 1) * GROUP)
+        whole = w.total[0, :, columns].astype(f32)
+        for d in range(2):
+            scatter(d, q, reach(d, q)).wait_recv()
+            whole = whole + w.arrived[d, q, reach(d, q) - 1].astype(f32)
+        spread = spread + jnp.dot(spread_map(48, 4, q), whole.astype(bf), preferred_element_type=f32)
+    w.ret[...] = spread.astype(bf).reshape(8, 48, GROUP)
+    for i in range(1, 8):
+        give(i).start()
+    w.back[pl.ds(e, 1)] = w.ret[pl.ds(e, 1)]
+    reduce_on(0, 3)
+    reduce_on(1, 1)
+    reduce_on(1, 2)
+    reduce_end(0)
+    reduce_on(1, 3)
+    for i in range(1, 8):
+        give_in(i).wait_recv()
+    mixed = jnp.dot(w.mix[...], w.back[...].reshape(384, GROUP), preferred_element_type=f32)
+    layer_out = (w.sg[...].astype(f32) + (mixed[:128] + mixed[128:])).astype(bf)
+    for g in range(4):
+        for b in range(2):
+            w.ready[b, :, g * GROUP : (g + 1) * GROUP] = layer_out[g * 32 + b * 16 : g * 32 + b * 16 + 16]
+
+    def hand(part, b, core):
+        columns = pl.ds(0, RING) if part == 0 else pl.ds(RING, PLANE)
+        return remote(
+            w.ready.at[b, :, columns], w.landed.at[core, :, columns], w.fin_s.at[part, b], w.fin_r.at[part, core],
+            pipe=over, ctx=2 * z + b,
+        )
 
     for b in range(2):
-        hand(b, k).start()
+        hand(0, b, k).start()
+    reduce_end(1)
     for b in range(2):
-        hand(b, b).wait_recv()
+        hand(1, b, k).start()
+    for part in range(2):
+        for b in range(2):
+            hand(part, b, b).wait_recv()
+    for b in range(2):
         out_ref[:, b * HALF : (b + 1) * HALF] = w.landed[b]
 
-    for b in range(2):
-        hand(b, k).wait_send()
+    for part in range(2):
+        for b in range(2):
+            hand(part, b, k).wait_send()
     for copy in pair:
         copy.wait_send()
-    for part in range(2):
-        for i in range(1, 8):
-            box(part, i).wait_send()
-            give(part, i).wait_send()
-    for q in range(4):
-        for d in range(2):
-            def done(r, carry, d=d, q=q):
-                gather(d, q, r).wait_send()
-                return carry
-
-            lax.fori_loop(1, reach(d, q) + 1, done, 0)
-
-    def sent(step, carry):
-        for m in range(4):
-            pass_on(m, step).wait_send()
+
+    def sent(i, carry):
+        box(i).wait_send()
+        give(i).wait_send()
+        spread_table(i).wait_send()
+        for h in range(2):
+            plane_box(h, i).wait_send()
+            plane_give(h, i).wait_send()
         return carry
 
-    lax.fori_loop(0, 7, sent, 0)
+    lax.fori_loop(1, 8, sent, 0)
+
+    def gone(r, carry):
+        for q in range(4):
+            for d in range(2):
+                @pl.when(r <= reach(d, q))
+                def _(d=d, q=q):
+                    gather(d, q, r).wait_send()
+                    scatter(d, q, r).wait_send()
+                    if q < 2:
+                        relay(d, q, r).wait_send()
+                        for h in range(2):
+                            reduce(h, d, q, r).wait_send()
+        return carry
+
+    lax.fori_loop(1, 5, gone, 0)
 
     def swapped(slot, carry):
         swap(slot).wait_send()
@@ -622,23 +767,27 @@
     "proj": ((896, 1024), BF), "proj_all": ((1024, 896), BF), "product": ((8, 128, 896), F32),
     "fold_out": ((8, 64, 896), BF), "fold_in": ((8, 64, 896), BF), "cross_out": ((8, 64, 896), BF),
     "cross_in": ((8, 3, 16, 896), BF), "part_out": ((8, 16, 896), BF), "parts": ((8, 16, 896), BF), "stream": ((16, D), BF),
-    "table": ((2, 16, 128), F32), "sel0": ((384, 128), BF), "sel1": ((256, 96), BF), "mix0": ((256, 384), BF), "mix1": ((192, 256), BF),
-    "normed": ((16, D), BF), "pn": ((16, HALF), BF), "ps": ((16, HALF), BF),
-    "xg0": ((128, 512), BF), "xg1": ((96, 512), BF), "sg0": ((128, 512), BF), "sg1": ((96, 512), BF),
-    "outbox0": ((8, 48, 512), BF), "outbox1": ((8, 32, 512), BF), "inbox0": ((8, 48, 512), BF), "inbox1": ((8, 32, 512), BF),
-    "w_in": ((HALF, 512), BF), "w_down": ((256, HALF), BF), "rows": ((8, 80, HALF), BF),
-    "half": ((8, 80, 512), F32), "half_other": ((8, 80, 512), F32), "total": ((8, 80, HALF), BF),
-    "arrived": ((4, 7, 80, 896), BF), "summed": ((80, HALF), BF),
-    "ret0": ((8, 48, 512), BF), "ret1": ((8, 32, 512), BF), "back0": ((8, 48, 512), BF), "back1": ((8, 32, 512), BF),
-    "ready": ((2, 16, HALF), BF), "landed": ((2, 16, HALF), BF),
+    "table": ((8, 2, 16, 128), F32), "sel": ((384, 128), BF), "mix": ((256, 384), BF),
+    "plane_sel": ((640, 256), BF), "plane_mix": ((512, 640), BF),
+    "normed": ((16, D), BF), "pn": ((16, HALF), BF), "ps": ((16, HALF), BF), "tokens": ((8, 32, PLANE), BF),
+    "xg": ((128, GROUP), BF), "sg": ((128, GROUP), BF), "plane_stream": ((32, PLANE), BF),
+    "outbox": ((8, 48, GROUP), BF), "inbox": ((8, 48, GROUP), BF), "ret": ((8, 48, GROUP), BF), "back": ((8, 48, GROUP), BF),
+    "plane_out": ((2, 8, 80, 512), BF), "plane_in": ((2, 8, 80, 512), BF),
+    "plane_ret": ((2, 8, 80, 512), BF), "plane_back": ((2, 8, 80, 512), BF),
+    "w_in": ((HALF, 512), BF), "w_down": ((256, HALF), BF), "rows": ((8, 80, RING), BF),
+    "half": ((8, 80, 512), F32), "half_other": ((8, 80, 512), F32), "hidden": ((640, 256), F32), "total": ((8, 80, RING), BF),
+    "arrived": ((2, 4, 4, 80, GROUP), BF), "partial": ((8, 32, PLANE), BF), "plane_own": ((32, PLANE), F32),
+    "plane_arrived": ((2, 2, 2, 4, 32, 256), BF), "ready": ((2, 16, HALF), BF), "landed": ((2, 16, HALF), BF),
     "load": ((9,), None), "chain_s": ((5, 4), None), "chain_r": ((5, 4), None), "share_s": ((5,), None), "share_r": ((5,), None),
     "proj_s": ((1,), None), "proj_r": ((1,), None), "head_s": ((2, 2, 5), None), "head_r": ((2, 2, 5), None),
     "fold_s": ((8,), None), "fold_r": ((8,), None), "cross_s": ((8, 3), None), "cross_r": ((8, 3), None),
     "part_s": ((8,), None), "part_r": ((8,), None),
-    "pair_s": ((6,), None), "pair_r": ((6,), None), "loc": ((3,), None), "box_s": ((2, 8), None), "box_r": ((2, 8), None),
+    "pair_s": ((6,), None), "pair_r": ((6,), None), "loc": ((3,), None), "table_s": ((8,), None), "table_r": ((8,), None),
+    "box_s": ((8,), None), "box_r": ((8,), None), "relay_s": ((2, 2, 5), None), "relay_r": ((2, 2, 5), None),
+    "plane_s": ((2, 8), None), "plane_r": ((2, 8), None), "give_s": ((2, 8), None), "give_r": ((2, 8), None),
     "ag_s": ((2, 4, 5), None), "ag_r": ((2, 4, 5), None), "half_s": ((8,), None), "half_r": ((8,), None),
-    "rs_s": ((4, 7), None), "rs_r": ((4, 7), None), "back_s": ((2, 8), None), "back_r": ((2, 8), None),
-    "fin_s": ((2,), None), "fin_r": ((2,), None),
+    "rs_s": ((2, 4, 4), None), "rs_r": ((2, 4, 4), None), "red_s": ((2, 2, 2, 4), None), "red_r": ((2, 2, 2, 4), None),
+    "back_s": ((8,), None), "back_r": ((8,), None), "fin_s": ((2, 2), None), "fin_r": ((2, 2), None),
 }
 
 

time: 193 us -> 186 us (0.964)
  Pallas kernels: 191 us -> 184 us
    pallas_call x1, Pallas kernels: 191 us -> 184 us  [on_device(): pl.pallas_call(layer_kernel, out_shape=jax.ShapeDtypeStruct((16, D), BF),...]
where the time goes in v4:
time: 186 us; the launch traced here: 185 us
  Pallas kernels  184 us (99%)
    pallas_call x1, Pallas kernels, on_device(): pl.pallas_call(layer_kernel, out_shape=jax.ShapeDtypeStruct((16, D), BF),...  184 us

profile of v4, /device:TPU:1, one launch (start us, length us, event | category | flops | bytes accessed | tf_op | source)
XLA Modules:
  0.0 185.4 jit_solution(6903792327915899172)
XLA Ops:
  0.0 183.8 %layer.1 = bf16[16,7168]{1,0:T(8,128)(2,1)} custom-call(bf16[8,576,128]{2,1,0:T(8,128)(2,1)} %bitcast.25, bf16[576,128]{1,0:T(8,128)(2,1)} %bitcast.29, s32[1,128]{1,0:T(1,128)} %doc_ref.1, s32[2,16]{1,0:T(2,128)} %bitcast.30, f32[2,16]{1,0:T(2,128)} %bitcast.31, bf16[16,7168]{1,0:T(8,128)(2,1)} %bitcast.28, f32[1,7168]{1,0:T(1,128)} %gain_ref.1, ...), custom_call_target="tpu_custom_call" | custom-call | flops 8000000000 | bytes 10000000 | tf_op jit(solution)/shard_map/layer/pallas_call | solution.py:799
  183.8 1.6 copy.14

commit v5 on v4

--- a/solution.py
+++ b/solution.py
@@ -56,9 +56,12 @@
     return jnp.where(row == want, 1.0, 0.0).astype(dtype)
 
 
-RING = 2560
-GROUP = 640
+RING = 2304
+GROUP = 384
+PIECES = RING // GROUP
 PLANE = HALF - RING
+WIDE = PLANE // 2
+SUMS = (((0, 384), (384, 256)), ((640, 256), (896, 384)))
 
 
 def reach(d, q):
@@ -174,7 +177,6 @@
     own_proj.wait()
     pair_proj.wait_recv()
     w.proj_all[...] = jnp.transpose(w.proj[...])
-    make_tables()
 
     y_mine = pl.multiple_of(y * 64, 64)
     y_theirs = pl.multiple_of((1 - y) * 64, 64)
@@ -247,6 +249,7 @@
             def _(act=act, now=now):
                 act(8 - now)
 
+        make_tables(r)
         return carry
 
     lax.fori_loop(0, 7, turn, 0)
@@ -320,38 +323,37 @@
     w.table[0, pl.ds(k, 1)] = table[None]
 
 
-def matrices(w):
-    bf, f32 = jnp.bfloat16, jnp.float32
-    chip = jnp.concatenate([w.table[0].reshape(32, 128)] * 4, axis=0)
-    column = w.table[...].reshape(256, 128)
-    for columns, sel, mix, groups, height in ((chip, w.sel, w.mix, 4, 48), (column, w.plane_sel, w.plane_mix, 8, 80)):
-        span, count = groups * 32, 8 * height
-        lanes = jnp.transpose(columns)
-
-        def decode(shape, axis):
-            row = lax.broadcasted_iota(jnp.int32, shape, axis).astype(f32)
-            expert = jnp.floor((row + 0.5) * (1.0 / height))
-            inner = row - expert * height
-            group = jnp.floor((inner + 0.5) * 0.1)
-            within = inner - group * 10.0
-            block = jnp.where(within >= 5.0, 1.0, 0.0)
-            slot = jnp.where(group < groups, expert * 8.0 + within - block * 5.0, -1.0)
-            owner = group * 2.0 + block
-            return slot, owner
-
-        slot, owner = decode((count, 1), 0)
-        token = lax.shift_right_logical(lax.broadcasted_iota(jnp.int32, (count, span), 1), 4).astype(f32)
-        hit = (owner == token) & ((slot == lanes[0:1, :]) | (slot == lanes[1:2, :]))
-        sel[...] = jnp.where(hit, 1.0, 0.0).astype(bf)
-        slot, owner = decode((1, count), 1)
-        token = lax.shift_right_logical(lax.broadcasted_iota(jnp.int32, (span, count), 0), 4).astype(f32)
-        slot = jnp.where(owner == token, slot, -1.0)
-        weight = jnp.zeros((span, count), f32)
-        for i in range(2):
-            weight = weight + jnp.where(slot == columns[:, i : i + 1], columns[:, i + 2 : i + 3], 0.0)
-        high = weight.astype(bf)
-        mix[0:span, :] = high
-        mix[span : 2 * span, :] = (weight - high.astype(f32)).astype(bf)
+def decode(shape, axis, groups, height):
+    row = lax.broadcasted_iota(jnp.int32, shape, axis).astype(jnp.float32)
+    expert = jnp.floor((row + 0.5) * (1.0 / height))
+    inner = row - expert * height
+    group = jnp.floor((inner + 0.5) * 0.1)
+    within = inner - group * 10.0
+    block = jnp.where(within >= 5.0, 1.0, 0.0)
+    slot = jnp.where(group < groups, expert * 8.0 + within - block * 5.0, -1.0)
+    return slot, group * 2.0 + block
+
+
+def choose_matrix(columns, sel, groups, height):
+    span, count = groups * 32, 8 * height
+    lanes = jnp.transpose(columns)
+    slot, owner = decode((count, 1), 0, groups, height)
+    token = lax.shift_right_logical(lax.broadcasted_iota(jnp.int32, (count, span), 1), 4).astype(jnp.float32)
+    hit = (owner == token) & ((slot == lanes[0:1, :span]) | (slot == lanes[1:2, :span]))
+    sel[...] = jnp.where(hit, 1.0, 0.0).astype(jnp.bfloat16)
+
+
+def weigh_matrix(columns, mix, groups, height):
+    span, count = groups * 32, 8 * height
+    slot, owner = decode((1, count), 1, groups, height)
+    token = lax.shift_right_logical(lax.broadcasted_iota(jnp.int32, (span, count), 0), 4).astype(jnp.float32)
+    slot = jnp.where(owner == token, slot, -1.0)
+    weight = jnp.zeros((span, count), jnp.float32)
+    for i in range(2):
+        weight = weight + jnp.where(slot == columns[:span, i : i + 1], columns[:span, i + 2 : i + 3], 0.0)
+    high = weight.astype(jnp.bfloat16)
+    mix[0:span, :] = high
+    mix[span : 2 * span, :] = (weight - high.astype(jnp.float32)).astype(jnp.bfloat16)
 
 
 def layer_kernel(
@@ -413,10 +415,22 @@
         for i in range(1, 8):
             spread_table(i).start()
 
-    def make_tables():
-        for i in range(1, 8):
-            spread_table(i).wait_recv()
-        matrices(w)
+    def chip_table():
+        return jnp.concatenate([w.table[0].reshape(32, 128)] * 4, axis=0)
+
+    def column_table():
+        return w.table[...].reshape(256, 128)
+
+    def make_tables(r):
+        @pl.when(r == 1)
+        def _():
+            choose_matrix(chip_table(), w.sel, 3, 32)
+
+        @pl.when(r == 2)
+        def _():
+            for i in range(1, 8):
+                spread_table(i).wait_recv()
+            choose_matrix(column_table(), w.plane_sel, 8, 80)
 
     settle = attend(w, q_ref, lat_ref, doc_ref, vu_ref, op_ref, residual_ref, start_rest, share_tables, make_tables)
     wide = w.stream[...].astype(f32)
@@ -426,9 +440,9 @@
         copy.start()
 
     def place(target, plane_target, source, start, core):
-        for g in range(4):
+        for g in range(PIECES):
             lanes = pl.ds(start + g * GROUP if isinstance(start, int) else pl.multiple_of(start + g * GROUP, 128), GROUP)
-            target[pl.ds(pl.multiple_of(g * 32 + core * 16, 16), 16), :] = source[:, lanes]
+            target[g // 3, pl.ds(pl.multiple_of(g % 3 * 32 + core * 16, 16), 16), :] = source[:, lanes]
         lanes = pl.ds(start + RING if isinstance(start, int) else pl.multiple_of(start + RING, 128), PLANE)
         plane_target[pl.ds(pl.multiple_of(core * 16, 16), 16), :] = source[:, lanes]
 
@@ -438,7 +452,7 @@
     place(w.xg, w.tokens.at[0], w.pn, 0, kk)
 
     def relay(d, q, r):
-        columns = pl.ds(q * 512, 512)
+        columns = pl.ds(q * WIDE, WIDE)
         src, dst, to = (r - 1, r, right) if d == 0 else (lax.rem(9 - r, 8), 8 - r, left)
         return remote(w.tokens.at[src, :, columns], w.tokens.at[dst, :, columns], w.relay_s.at[d, q, r], w.relay_r.at[d, q, r], ctx=to)
 
@@ -454,39 +468,41 @@
         for d in range(2):
             relay(d, q, 1).start()
 
-    def box(i):
+    def box(part, i):
         to = lax.rem(e + i, 8)
-        return remote(w.outbox.at[to], w.inbox.at[e], w.box_s.at[i], w.box_r.at[i], exp=to)
-
-    def box_in(i):
+        return remote(w.outbox.at[part, to], w.inbox.at[part, e], w.box_s.at[part, i], w.box_r.at[part, i], exp=to)
+
+    def box_in(part, i):
         source = lax.rem(e + 8 - i, 8)
-        return remote(w.outbox.at[source], w.inbox.at[source], w.box_s.at[i], w.box_r.at[i], exp=source)
-
-    chosen = jnp.dot(w.sel[...], w.xg[...], preferred_element_type=f32).astype(bf)
-    w.outbox[...] = chosen.reshape(8, 48, GROUP)
-    for i in range(1, 8):
-        box(i).start()
-    w.inbox[pl.ds(e, 1)] = w.outbox[pl.ds(e, 1)]
+        return remote(
+            w.outbox.at[part, source], w.inbox.at[part, source], w.box_s.at[part, i], w.box_r.at[part, i], exp=source
+        )
+
+    for part in range(2):
+        chosen = jnp.dot(w.sel[...], w.xg[part], preferred_element_type=f32).astype(bf)
+        w.outbox[part] = chosen.reshape(8, 32, GROUP)
+        for i in range(1, 8):
+            box(part, i).start()
+        w.inbox[part, pl.ds(e, 1)] = w.outbox[part, pl.ds(e, 1)]
     relay_round(1)
-    relay_round(2)
-    pair[1].wait_recv()
-    place(w.sg, w.plane_stream, w.ps, 0, kk)
 
     def gather(d, q, r):
         columns = pl.ds(q * GROUP, GROUP)
         src, dst, to = (r - 1, r, right) if d == 0 else (lax.rem(9 - r, 8), 8 - r, left)
         return remote(w.rows.at[src, :, columns], w.rows.at[dst, :, columns], w.ag_s.at[d, q, r], w.ag_r.at[d, q, r], ctx=to)
 
-    for i in range(1, 8):
-        box_in(i).wait_recv()
-    landed_rows = w.inbox[...].reshape(384, GROUP)
-    for q in range(4):
-        w.rows[0, :, q * GROUP : (q + 1) * GROUP] = jnp.dot(
-            squeeze_map(48, 4, q), landed_rows, preferred_element_type=f32
-        ).astype(bf)
-        for d in range(2):
-            gather(d, q, 1).start()
-    relay_round(3)
+    for part in range(2):
+        for i in range(1, 8):
+            box_in(part, i).wait_recv()
+        landed_rows = w.inbox[part].reshape(256, GROUP)
+        for g in range(3):
+            q = part * 3 + g
+            w.rows[0, :, q * GROUP : (q + 1) * GROUP] = jnp.dot(
+                squeeze_map(32, 3, g), landed_rows, preferred_element_type=f32
+            ).astype(bf)
+            for d in range(2):
+                gather(d, q, 1).start()
+        relay_round(2 + part)
     relay_round(4)
 
     def plane_box(h, i):
@@ -498,67 +514,73 @@
         return remote(w.plane_out.at[h, source], w.plane_in.at[h, source], w.plane_s.at[h, i], w.plane_r.at[h, i], exp=source)
 
     for h in range(2):
-        tokens = w.tokens[:, :, h * 512 : (h + 1) * 512].reshape(256, 512)
+        tokens = w.tokens[:, :, h * WIDE : (h + 1) * WIDE].reshape(256, WIDE)
         chosen = jnp.dot(w.plane_sel[...], tokens, preferred_element_type=f32).astype(bf)
-        w.plane_out[h] = chosen.reshape(8, 80, 512)
+        w.plane_out[h] = chosen.reshape(8, 80, WIDE)
         for i in range(1, 8):
             plane_box(h, i).start()
         w.plane_in[h, pl.ds(e, 1)] = w.plane_out[h, pl.ds(e, 1)]
+    pair[1].wait_recv()
+    place(w.sg, w.plane_stream, w.ps, 0, kk)
     for copy in local:
         copy.wait()
     for copy in pair[2:5]:
         copy.wait_recv()
 
-    def swap(slot):
-        return remote(w.half.at[slot], w.half_other.at[slot], w.half_s.at[slot], w.half_r.at[slot], ctx=other)
+    BATCHES = ((0, 4), (5, 3), (4, 1))
+
+    def swap(n):
+        slots = pl.ds(*BATCHES[n])
+        return remote(w.half.at[slots], w.half_other.at[slots], w.half_s.at[n], w.half_r.at[n], ctx=other)
 
     def ring_half(slot):
-        w.half[slot] = jnp.dot(w.rows[slot], w.w_in[0:RING, :], preferred_element_type=f32)
-
-    ring_half(0)
-
-    def collect(r, carry):
-        for q in range(4):
-            for d in range(2):
-                @pl.when(r <= reach(d, q))
-                def _(d=d, q=q):
-                    gather(d, q, r).wait_recv()
-
-                @pl.when(r + 1 <= reach(d, q))
-                def _(d=d, q=q):
-                    gather(d, q, r + 1).start()
-
-        ring_half(r)
-
-        @pl.when(r < 4)
-        def _():
-            ring_half(8 - r)
-
-        return carry
-
-    lax.fori_loop(1, 5, collect, 0)
-    for h in range(2):
-        for i in range(1, 8):
-            plane_box_in(h, i).wait_recv()
-
-    def plane_half(slot):
-        pick = squeeze_map(80, 8, slot)
-        total = w.half[slot]
-        for h in range(2):
-            mine_now = jnp.dot(pick, w.plane_in[h].reshape(640, 512), preferred_element_type=f32).astype(bf)
-            total = total + jnp.dot(mine_now, w.w_in[RING + h * 512 : RING + (h + 1) * 512, :], preferred_element_type=f32)
-        w.half[slot] = total
-        swap(slot).start()
-
-    w.hidden[...] = jnp.zeros((640, 256), f32)
-
-    def second_half(slot):
-        swap(slot).wait_recv()
-        both = w.half[slot] + w.half_other[slot]
+        w.half[slot] = w.half[slot] + jnp.dot(w.rows[slot], w.w_in[0:RING, :], preferred_element_type=f32)
+
+    def second_half(n):
+        first, count = BATCHES[n]
+        swap(n).wait_recv()
+        slots = slice(first, first + count)
+        both = (w.half[slots] + w.half_other[slots]).reshape(count * 80, 512)
         gate = both[:, :256]
         hidden = (gate / (1.0 + jnp.exp(-gate)) * both[:, 256:]).astype(bf)
-        w.total[slot] = jnp.dot(hidden, w.w_down[:, 0:RING], preferred_element_type=f32).astype(bf)
-        w.hidden[...] = w.hidden[...] + jnp.dot(spread_map(80, 8, slot), hidden, preferred_element_type=f32)
+        w.hidden[first * 80 : (first + count) * 80, :] = hidden
+        for part in range(2):
+            columns = slice(part * 3 * GROUP, (part + 1) * 3 * GROUP)
+            out = jnp.dot(hidden, w.w_down[:, columns], preferred_element_type=f32).astype(bf)
+            w.total[slots, :, columns] = out.reshape(count, 80, 3 * GROUP)
+
+    w.half[...] = jnp.zeros((8, 80, 512), f32)
+    ring_half(0)
+    for r in range(1, 5):
+        for q in range(PIECES):
+            for d in range(2):
+                if r <= reach(d, q):
+                    gather(d, q, r).wait_recv()
+                if r + 1 <= reach(d, q):
+                    gather(d, q, r + 1).start()
+        ring_half(r)
+        if r < 4:
+            ring_half(8 - r)
+        if r == 1:
+            weigh_matrix(chip_table(), w.mix, 3, 32)
+            for slot in range(8):
+                w.turn[slot * 80 : (slot + 1) * 80, :] = squeeze_map(80, 8, slot)
+        if r == 2:
+            weigh_matrix(column_table(), w.plane_mix, 8, 80)
+        if r == 3:
+            for h in range(2):
+                for i in range(1, 8):
+                    plane_box_in(h, i).wait_recv()
+                turned = jnp.dot(w.turn[...], w.plane_in[h].reshape(640, WIDE), preferred_element_type=f32).astype(bf)
+                lanes = slice(RING + h * WIDE, RING + (h + 1) * WIDE)
+                more = jnp.dot(turned, w.w_in[lanes, :], preferred_element_type=f32)
+                w.half[...] = w.half[...] + more.reshape(8, 80, 512)
+            swap(0).start()
+            swap(1).start()
+            second_half(0)
+            second_half(1)
+    swap(2).start()
+    second_half(2)
 
     def scatter(d, q, j):
         far = reach(d, q) + 1 - j
@@ -567,7 +589,7 @@
         return remote(w.total.at[slot, :, columns], w.arrived.at[d, q, j - 1], w.rs_s.at[d, q, j - 1], w.rs_r.at[d, q, j - 1], ctx=to)
 
     def scatter_on(j):
-        for q in range(4):
+        for q in range(PIECES):
             for d in range(2):
                 if j + 1 <= reach(d, q):
                     far = reach(d, q) - j
@@ -579,28 +601,9 @@
                     ).astype(bf)
                     scatter(d, q, j + 1).start()
 
-    def place_of(i):
-        step = lax.div(i + 1, 2)
-        return jnp.where(lax.rem(i, 2) == 0, 4 + step, 4 - step)
-
-    def work(i, carry):
-        @pl.when(i < 8)
-        def _():
-            plane_half(place_of(i))
-
-        @pl.when(i >= 1)
-        def _():
-            second_half(place_of(i - 1))
-
-        @pl.when(i == 3)
-        def _():
-            for q in range(4):
-                for d in range(2):
-                    scatter(d, q, 1).start()
-
-        return carry
-
-    lax.fori_loop(0, 9, work, 0)
+    for q in range(PIECES):
+        for d in range(2):
+            scatter(d, q, 1).start()
 
     def plane_give(h, i):
         to = lax.rem(e + i, 8)
@@ -610,10 +613,10 @@
         source = lax.rem(e + 8 - i, 8)
         return remote(w.plane_ret.at[h, source], w.plane_back.at[h, source], w.give_s.at[h, i], w.give_r.at[h, i], exp=source)
 
-    hidden = w.hidden[...].astype(bf)
+    hidden = jnp.dot(w.turn[...], w.hidden[...], preferred_element_type=f32).astype(bf)
     for h in range(2):
-        out = jnp.dot(hidden, w.w_down[:, RING + h * 512 : RING + (h + 1) * 512], preferred_element_type=f32).astype(bf)
-        w.plane_ret[h] = out.reshape(8, 80, 512)
+        out = jnp.dot(hidden, w.w_down[:, RING + h * WIDE : RING + (h + 1) * WIDE], preferred_element_type=f32).astype(bf)
+        w.plane_ret[h] = out.reshape(8, 80, WIDE)
         for i in range(1, 8):
             plane_give(h, i).start()
         w.plane_back[h, pl.ds(e, 1)] = w.plane_ret[h, pl.ds(e, 1)]
@@ -621,19 +624,19 @@
     def reduce(h, d, q, j):
         far = reach(d, q) + 1 - j
         slot, to = (far, left) if d == 0 else (8 - far, right)
-        columns = pl.ds(h * 512 + q * 256, 256)
+        columns = pl.ds(*SUMS[h][q])
         return remote(
-            w.partial.at[slot, :, columns], w.plane_arrived.at[h, d, q, j - 1], w.red_s.at[h, d, q, j - 1],
+            w.partial.at[slot, :, columns], w.plane_arrived.at[h, d, q, j - 1, :, pl.ds(0, SUMS[h][q][1])], w.red_s.at[h, d, q, j - 1],
             w.red_r.at[h, d, q, j - 1], ctx=to,
         )
 
     def reduce_start(h):
         for i in range(1, 8):
             plane_give_in(h, i).wait_recv()
-        mixed = jnp.dot(w.plane_mix[...], w.plane_back[h].reshape(640, 512), preferred_element_type=f32)
+        mixed = jnp.dot(w.plane_mix[...], w.plane_back[h].reshape(640, WIDE), preferred_element_type=f32)
         mixed = mixed[:256] + mixed[256:]
-        w.plane_own[:, h * 512 : (h + 1) * 512] = mixed[:32]
-        w.partial[:, :, h * 512 : (h + 1) * 512] = mixed.astype(bf).reshape(8, 32, 512)
+        w.plane_own[:, h * WIDE : (h + 1) * WIDE] = mixed[:32]
+        w.partial[:, :, h * WIDE : (h + 1) * WIDE] = mixed.astype(bf).reshape(8, 32, WIDE)
         for q in range(2):
             for d in range(2):
                 reduce(h, d, q, 1).start()
@@ -644,31 +647,67 @@
                 if j + 1 <= reach(d, q):
                     far = reach(d, q) - j
                     slot = far if d == 0 else 8 - far
-                    columns = slice(h * 512 + q * 256, h * 512 + (q + 1) * 256)
+                    start, width = SUMS[h][q]
+                    columns = slice(start, start + width)
                     reduce(h, d, q, j).wait_recv()
                     w.partial[slot, :, columns] = (
-                        w.partial[slot, :, columns].astype(f32) + w.plane_arrived[h, d, q, j - 1].astype(f32)
+                        w.partial[slot, :, columns].astype(f32) + w.plane_arrived[h, d, q, j - 1, :, 0:width].astype(f32)
                     ).astype(bf)
                     reduce(h, d, q, j + 1).start()
 
     def reduce_end(h):
         for q in range(2):
-            columns = slice(h * 512 + q * 256, h * 512 + (q + 1) * 256)
+            start, width = SUMS[h][q]
+            columns = slice(start, start + width)
             whole = w.plane_own[:, columns] + w.plane_stream[:, columns].astype(f32)
             for d in range(2):
                 reduce(h, d, q, reach(d, q)).wait_recv()
-                whole = whole + w.plane_arrived[h, d, q, reach(d, q) - 1].astype(f32)
+                whole = whole + w.plane_arrived[h, d, q, reach(d, q) - 1, :, 0:width].astype(f32)
             whole = whole.astype(bf)
             for b in range(2):
-                w.ready[b, :, RING + h * 512 + q * 256 : RING + h * 512 + (q + 1) * 256] = whole[b * 16 : (b + 1) * 16]
-
-    def give(i):
+                w.ready[b, :, RING + start : RING + start + width] = whole[b * 16 : (b + 1) * 16]
+
+    def give(part, i):
         to = lax.rem(e + i, 8)
-        return remote(w.ret.at[to], w.back.at[e], w.back_s.at[i], w.back_r.at[i], exp=to)
-
-    def give_in(i):
+        return remote(w.ret.at[part, to], w.back.at[part, e], w.back_s.at[part, i], w.back_r.at[part, i], exp=to)
+
+    def give_in(part, i):
         source = lax.rem(e + 8 - i, 8)
-        return remote(w.ret.at[source], w.back.at[source], w.back_s.at[i], w.back_r.at[i], exp=source)
+        return remote(w.ret.at[part, source], w.back.at[part, source], w.back_s.at[part, i], w.back_r.at[part, i], exp=source)
+
+    def send_back(part):
+        spread = jnp.zeros((256, GROUP), f32)
+        for g in range(3):
+            q = part * 3 + g
+            columns = slice(q * GROUP, (q + 1) * GROUP)
+            whole = w.total[0, :, columns].astype(f32)
+            for d in range(2):
+                scatter(d, q, reach(d, q)).wait_recv()
+                whole = whole + w.arrived[d, q, reach(d, q) - 1].astype(f32)
+            spread = spread + jnp.dot(spread_map(32, 3, g), whole.astype(bf), preferred_element_type=f32)
+        w.ret[part] = spread.astype(bf).reshape(8, 32, GROUP)
+        for i in range(1, 8):
+            give(part, i).start()
+        w.back[part, pl.ds(e, 1)] = w.ret[part, pl.ds(e, 1)]
+
+    def hand(part, b, core):
+        columns = pl.ds(part * 3 * GROUP, 3 * GROUP) if part < 2 else pl.ds(RING, PLANE)
+        return remote(
+            w.ready.at[b, :, columns], w.landed.at[core, :, columns], w.fin_s.at[part, b], w.fin_r.at[part, core],
+            pipe=over, ctx=2 * z + b,
+        )
+
+    def finish_ring(part):
+        for i in range(1, 8):
+            give_in(part, i).wait_recv()
+        mixed = jnp.dot(w.mix[...], w.back[part].reshape(256, GROUP), preferred_element_type=f32)
+        layer_out = (w.sg[part].astype(f32) + (mixed[:96] + mixed[96:])).astype(bf)
+        for g in range(3):
+            start = (part * 3 + g) * GROUP
+            for b in range(2):
+                w.ready[b, :, start : start + GROUP] = layer_out[g * 32 + b * 16 : g * 32 + b * 16 + 16]
+        for b in range(2):
+            hand(part, b, k).start()
 
     scatter_on(1)
     scatter_on(2)
@@ -677,68 +716,43 @@
     reduce_on(0, 1)
     reduce_start(1)
     reduce_on(0, 2)
-    spread = jnp.zeros((384, GROUP), f32)
-    for q in range(4):
-        columns = slice(q * GROUP, (q + 1) * GROUP)
-        whole = w.total[0, :, columns].astype(f32)
-        for d in range(2):
-            scatter(d, q, reach(d, q)).wait_recv()
-            whole = whole + w.arrived[d, q, reach(d, q) - 1].astype(f32)
-        spread = spread + jnp.dot(spread_map(48, 4, q), whole.astype(bf), preferred_element_type=f32)
-    w.ret[...] = spread.astype(bf).reshape(8, 48, GROUP)
-    for i in range(1, 8):
-        give(i).start()
-    w.back[pl.ds(e, 1)] = w.ret[pl.ds(e, 1)]
     reduce_on(0, 3)
     reduce_on(1, 1)
+    send_back(0)
+    send_back(1)
     reduce_on(1, 2)
     reduce_end(0)
     reduce_on(1, 3)
-    for i in range(1, 8):
-        give_in(i).wait_recv()
-    mixed = jnp.dot(w.mix[...], w.back[...].reshape(384, GROUP), preferred_element_type=f32)
-    layer_out = (w.sg[...].astype(f32) + (mixed[:128] + mixed[128:])).astype(bf)
-    for g in range(4):
-        for b in range(2):
-            w.ready[b, :, g * GROUP : (g + 1) * GROUP] = layer_out[g * 32 + b * 16 : g * 32 + b * 16 + 16]
-
-    def hand(part, b, core):
-        columns = pl.ds(0, RING) if part == 0 else pl.ds(RING, PLANE)
-        return remote(
-            w.ready.at[b, :, columns], w.landed.at[core, :, columns], w.fin_s.at[part, b], w.fin_r.at[part, core],
-            pipe=over, ctx=2 * z + b,
-        )
-
-    for b in range(2):
-        hand(0, b, k).start()
+    finish_ring(0)
     reduce_end(1)
     for b in range(2):
-        hand(1, b, k).start()
-    for part in range(2):
+        hand(2, b, k).start()
+    finish_ring(1)
+    for part in range(3):
         for b in range(2):
             hand(part, b, b).wait_recv()
     for b in range(2):
         out_ref[:, b * HALF : (b + 1) * HALF] = w.landed[b]
 
-    for part in range(2):
+    for part in range(3):
         for b in range(2):
             hand(part, b, k).wait_send()
     for copy in pair:
         copy.wait_send()
 
     def sent(i, carry):
-        box(i).wait_send()
-        give(i).wait_send()
         spread_table(i).wait_send()
         for h in range(2):
             plane_box(h, i).wait_send()
             plane_give(h, i).wait_send()
+            box(h, i).wait_send()
+            give(h, i).wait_send()
         return carry
 
     lax.fori_loop(1, 8, sent, 0)
 
     def gone(r, carry):
-        for q in range(4):
+        for q in range(PIECES):
             for d in range(2):
                 @pl.when(r <= reach(d, q))
                 def _(d=d, q=q):
@@ -752,11 +766,8 @@
 
     lax.fori_loop(1, 5, gone, 0)
 
-    def swapped(slot, carry):
-        swap(slot).wait_send()
-        return carry
-
-    lax.fori_loop(0, 8, swapped, 0)
+    for n in range(3):
+        swap(n).wait_send()
     settle()
 
 
@@ -767,27 +778,27 @@
     "proj": ((896, 1024), BF), "proj_all": ((1024, 896), BF), "product": ((8, 128, 896), F32),
     "fold_out": ((8, 64, 896), BF), "fold_in": ((8, 64, 896), BF), "cross_out": ((8, 64, 896), BF),
     "cross_in": ((8, 3, 16, 896), BF), "part_out": ((8, 16, 896), BF), "parts": ((8, 16, 896), BF), "stream": ((16, D), BF),
-    "table": ((8, 2, 16, 128), F32), "sel": ((384, 128), BF), "mix": ((256, 384), BF),
+    "table": ((8, 2, 16, 128), F32), "sel": ((256, 96), BF), "mix": ((192, 256), BF), "turn": ((640, 640), BF),
     "plane_sel": ((640, 256), BF), "plane_mix": ((512, 640), BF),
     "normed": ((16, D), BF), "pn": ((16, HALF), BF), "ps": ((16, HALF), BF), "tokens": ((8, 32, PLANE), BF),
-    "xg": ((128, GROUP), BF), "sg": ((128, GROUP), BF), "plane_stream": ((32, PLANE), BF),
-    "outbox": ((8, 48, GROUP), BF), "inbox": ((8, 48, GROUP), BF), "ret": ((8, 48, GROUP), BF), "back": ((8, 48, GROUP), BF),
-    "plane_out": ((2, 8, 80, 512), BF), "plane_in": ((2, 8, 80, 512), BF),
-    "plane_ret": ((2, 8, 80, 512), BF), "plane_back": ((2, 8, 80, 512), BF),
+    "xg": ((2, 96, GROUP), BF), "sg": ((2, 96, GROUP), BF), "plane_stream": ((32, PLANE), BF),
+    "outbox": ((2, 8, 32, GROUP), BF), "inbox": ((2, 8, 32, GROUP), BF), "ret": ((2, 8, 32, GROUP), BF),
+    "back": ((2, 8, 32, GROUP), BF), "plane_out": ((2, 8, 80, WIDE), BF), "plane_in": ((2, 8, 80, WIDE), BF),
+    "plane_ret": ((2, 8, 80, WIDE), BF), "plane_back": ((2, 8, 80, WIDE), BF),
     "w_in": ((HALF, 512), BF), "w_down": ((256, HALF), BF), "rows": ((8, 80, RING), BF),
-    "half": ((8, 80, 512), F32), "half_other": ((8, 80, 512), F32), "hidden": ((640, 256), F32), "total": ((8, 80, RING), BF),
-    "arrived": ((2, 4, 4, 80, GROUP), BF), "partial": ((8, 32, PLANE), BF), "plane_own": ((32, PLANE), F32),
-    "plane_arrived": ((2, 2, 2, 4, 32, 256), BF), "ready": ((2, 16, HALF), BF), "landed": ((2, 16, HALF), BF),
+    "half": ((8, 80, 512), F32), "half_other": ((8, 80, 512), F32), "hidden": ((640, 256), BF), "total": ((8, 80, RING), BF),
+    "arrived": ((2, PIECES, 4, 80, GROUP), BF), "partial": ((8, 32, PLANE), BF), "plane_own": ((32, PLANE), F32),
+    "plane_arrived": ((2, 2, 2, 4, 32, 384), BF), "ready": ((2, 16, HALF), BF), "landed": ((2, 16, HALF), BF),
     "load": ((9,), None), "chain_s": ((5, 4), None), "chain_r": ((5, 4), None), "share_s": ((5,), None), "share_r": ((5,), None),
     "proj_s": ((1,), None), "proj_r": ((1,), None), "head_s": ((2, 2, 5), None), "head_r": ((2, 2, 5), None),
     "fold_s": ((8,), None), "fold_r": ((8,), None), "cross_s": ((8, 3), None), "cross_r": ((8, 3), None),
     "part_s": ((8,), None), "part_r": ((8,), None),
     "pair_s": ((6,), None), "pair_r": ((6,), None), "loc": ((3,), None), "table_s": ((8,), None), "table_r": ((8,), None),
-    "box_s": ((8,), None), "box_r": ((8,), None), "relay_s": ((2, 2, 5), None), "relay_r": ((2, 2, 5), None),
+    "box_s": ((2, 8), None), "box_r": ((2, 8), None), "relay_s": ((2, 2, 5), None), "relay_r": ((2, 2, 5), None),
     "plane_s": ((2, 8), None), "plane_r": ((2, 8), None), "give_s": ((2, 8), None), "give_r": ((2, 8), None),
-    "ag_s": ((2, 4, 5), None), "ag_r": ((2, 4, 5), None), "half_s": ((8,), None), "half_r": ((8,), None),
-    "rs_s": ((2, 4, 4), None), "rs_r": ((2, 4, 4), None), "red_s": ((2, 2, 2, 4), None), "red_r": ((2, 2, 2, 4), None),
-    "back_s": ((8,), None), "back_r": ((8,), None), "fin_s": ((2, 2), None), "fin_r": ((2, 2), None),
+    "ag_s": ((2, PIECES, 5), None), "ag_r": ((2, PIECES, 5), None), "half_s": ((3,), None), "half_r": ((3,), None),
+    "rs_s": ((2, PIECES, 4), None), "rs_r": ((2, PIECES, 4), None), "red_s": ((2, 2, 2, 4), None), "red_r": ((2, 2, 2, 4), None),
+    "back_s": ((2, 8), None), "back_r": ((2, 8), None), "fin_s": ((3, 2), None), "fin_r": ((3, 2), None),
 }
 
 

time: 186 us -> 181 us (0.973)
  Pallas kernels: 184 us -> 179 us
    pallas_call x1, Pallas kernels: 184 us -> 179 us  [on_device(): pl.pallas_call(layer_kernel, out_shape=jax.ShapeDtypeStruct((16, D), BF),...]
where the time goes in v5:
time: 181 us
  Pallas kernels  179 us (99%)
    pallas_call x1, Pallas kernels, on_device(): pl.pallas_call(layer_kernel, out_shape=jax.ShapeDtypeStruct((16, D), BF),...  179 us

profile of v5, /device:TPU:1, one launch (start us, length us, event | category | flops | bytes accessed | tf_op | source)
XLA Modules:
  0.0 180.9 jit_solution(11805841261738414350)
XLA Ops:
  0.0 179.3 %layer.1 = bf16[16,7168]{1,0:T(8,128)(2,1)} custom-call(bf16[8,576,128]{2,1,0:T(8,128)(2,1)} %bitcast.25, bf16[576,128]{1,0:T(8,128)(2,1)} %bitcast.29, s32[1,128]{1,0:T(1,128)} %doc_ref.1, s32[2,16]{1,0:T(2,128)} %bitcast.30, f32[2,16]{1,0:T(2,128)} %bitcast.31, bf16[16,7168]{1,0:T(8,128)(2,1)} %bitcast.28, f32[1,7168]{1,0:T(1,128)} %gain_ref.1, ...), custom_call_target="tpu_custom_call" | custom-call | flops 8000000000 | bytes 10000000 | tf_op jit(solution)/shard_map/layer/pallas_call | solution.py:810
  179.3 1.6 copy.14

commit v6 on v5

--- a/solution.py
+++ b/solution.py
@@ -60,15 +60,16 @@
 GROUP = 384
 PIECES = RING // GROUP
 PLANE = HALF - RING
-WIDE = PLANE // 2
-SUMS = (((0, 384), (384, 256)), ((640, 256), (896, 384)))
+SHARES = ((0, 896), (896, 384))
+HANDS = ((0, 3 * GROUP), (3 * GROUP, 3 * GROUP), (RING, 896), (RING + 896, 384))
+SUMS = ((0, 512), (512, 384))
 
 
 def reach(d, q):
     return 4 if q % 2 == d else 3
 
 
-def attend(w, q_ref, lat_ref, doc_ref, vu_ref, op_ref, residual_ref, start_rest, share_tables, make_tables):
+def attend(w, q_ref, lat_ref, doc_ref, vu_ref, op_ref, residual_ref, start_rest, make_tables):
     p, c, e = lax.axis_index("pipe"), lax.axis_index("ctx"), lax.axis_index("exp")
     k = lax.rem(c, 2)
     z = lax.div(c, 2)
@@ -153,7 +154,6 @@
         return carry
 
     lax.fori_loop(0, 5, visit, 0)
-    share_tables()
 
     for copy in up_loads:
         copy.wait()
@@ -205,6 +205,26 @@
         w.product[slot] = jnp.dot(w.heads[slot], w.proj_all[...], preferred_element_type=f32)
         w.fold_out[slot] = w.product[slot, pl.ds(y_theirs, 64), :].astype(bf)
         fold(slot).start()
+
+    def direct(i):
+        to = lax.rem(e + i, 8)
+        return remote(
+            w.direct_out.at[pl.ds(pl.multiple_of(to * 16, 16), 16)], w.direct_in.at[i - 1], w.direct_s.at[i], w.direct_r.at[i], exp=to
+        )
+
+    def project_last():
+        w.product[4] = jnp.dot(w.heads[4], w.proj_all[...], preferred_element_type=f32)
+        w.direct_out[...] = w.product[4].astype(bf)
+        for i in range(1, 8):
+            direct(i).start()
+
+    def sum_last():
+        whole = w.product[4, pl.ds(pl.multiple_of(e * 16, 16), 16), :]
+        for i in range(1, 8):
+            direct(i).wait_recv()
+            whole = whole + w.direct_in[i - 1].astype(f32)
+        w.part_out[4] = whole.astype(bf)
+        deliver(4).start()
 
     def over_y(slot):
         fold(slot).wait_recv()
@@ -238,16 +258,24 @@
                     def _(d=d, q=q):
                         gather(d, q, r + 1).start()
 
+        @pl.when(r == 4)
+        def _():
+            project_last()
+
         for stage, act in enumerate((project, over_y, over_x)):
             now = r - stage
 
-            @pl.when((now >= 0) & (now <= 4))
+            @pl.when((now >= 0) & (now <= 3))
             def _(act=act, now=now):
                 act(now)
 
             @pl.when((now >= 1) & (now <= 3))
             def _(act=act, now=now):
                 act(8 - now)
+
+        @pl.when(r == 5)
+        def _():
+            sum_last()
 
         make_tables(r)
         return carry
@@ -283,10 +311,15 @@
 
                 lax.fori_loop(1, reach(d, q) + 1, gathered, 0)
 
+        for i in range(1, 8):
+            direct(i).wait_send()
+
         def folded(slot, carry):
-            fold(slot).wait_send()
-            for i in range(1, 4):
-                cross(slot, i).wait_send()
+            @pl.when(slot != 4)
+            def _():
+                fold(slot).wait_send()
+                for i in range(1, 4):
+                    cross(slot, i).wait_send()
 
             @pl.when(slot >= 1)
             def _():
@@ -320,7 +353,7 @@
     for i in range(2):
         table = jnp.where(lane == i, ids[i] * 8.0 + ranks[i], table)
         table = jnp.where(lane == i + 2, weights[i], table)
-    w.table[0, pl.ds(k, 1)] = table[None]
+    w.table[pl.ds(k, 1)] = table[None]
 
 
 def decode(shape, axis, groups, height):
@@ -380,7 +413,6 @@
     doc_row = jnp.broadcast_to(doc_ref[...].astype(f32), (128, 128))
     w.keys[0, KV:, pl.ds(my_lane, 128)] = doc_row[0:16].astype(bf)
     w.query_doc[...] = jnp.broadcast_to(column_of(doc_row), (128, 128))
-    tables(w, ids_ref, weights_ref, k)
     meet(
         [{"ctx": other}, {"pipe": over}, {"pipe": over, "ctx": other}]
         + [{"ctx": 2 * lax.rem(z + i, 8) + k} for i in range(1, 8)]
@@ -398,9 +430,10 @@
         remote(up_ref.at[pl.ds(theirs, HALF), :], w.w_in.at[:, pl.ds(up_lane, 128)], w.pair_s.at[3], w.pair_r.at[3], ctx=other),
         remote(down_ref.at[:, pl.ds(theirs, HALF)], w.w_down.at[pl.ds(my_lane, 128), :], w.pair_s.at[4], w.pair_r.at[4], ctx=other),
     ]
-    pair.append(remote(w.table.at[0, k], w.table.at[0, k], w.pair_s.at[5], w.pair_r.at[5], ctx=other))
+    pair.append(remote(w.table.at[k], w.table.at[k], w.pair_s.at[5], w.pair_r.at[5], ctx=other))
 
     def start_rest():
+        tables(w, ids_ref, weights_ref, k)
         pair[5].start()
         for copy in local:
             copy.start()
@@ -408,31 +441,32 @@
             copy.start()
 
     def spread_table(i):
-        return remote(w.table.at[0], w.table.at[i], w.table_s.at[i], w.table_r.at[i], ctx=2 * lax.rem(z + i, 8) + k)
-
-    def share_tables():
-        pair[5].wait_recv()
-        for i in range(1, 8):
-            spread_table(i).start()
+        return remote(w.brief.at[0], w.brief.at[i], w.table_s.at[i], w.table_r.at[i], ctx=2 * lax.rem(z + i, 8) + k)
 
     def chip_table():
-        return jnp.concatenate([w.table[0].reshape(32, 128)] * 4, axis=0)
-
-    def column_table():
-        return w.table[...].reshape(256, 128)
+        return jnp.concatenate([w.table[...].reshape(32, 128)] * 4, axis=0)
 
     def make_tables(r):
-        @pl.when(r == 1)
+        @pl.when(r == 3)
+        def _():
+            pair[5].wait_recv()
+            w.brief[0] = jnp.transpose(chip_table())[0:8]
+            for i in range(1, 8):
+                spread_table(i).start()
+
+        @pl.when(r == 4)
         def _():
             choose_matrix(chip_table(), w.sel, 3, 32)
 
-        @pl.when(r == 2)
+        @pl.when(r == 6)
         def _():
             for i in range(1, 8):
                 spread_table(i).wait_recv()
-            choose_matrix(column_table(), w.plane_sel, 8, 80)
-
-    settle = attend(w, q_ref, lat_ref, doc_ref, vu_ref, op_ref, residual_ref, start_rest, share_tables, make_tables)
+            for i in range(8):
+                w.column[i * 32 : (i + 1) * 32, :] = jnp.transpose(jnp.concatenate([w.brief[i]] * 16, axis=0))[0:32]
+            choose_matrix(w.column[...], w.plane_sel, 8, 80)
+
+    settle = attend(w, q_ref, lat_ref, doc_ref, vu_ref, op_ref, residual_ref, start_rest, make_tables)
     wide = w.stream[...].astype(f32)
     mean_square = jnp.mean(wide * wide, axis=1, keepdims=True)
     w.normed[...] = (wide * lax.rsqrt(mean_square + epsilon) * gain_ref[...]).astype(bf)
@@ -452,7 +486,7 @@
     place(w.xg, w.tokens.at[0], w.pn, 0, kk)
 
     def relay(d, q, r):
-        columns = pl.ds(q * WIDE, WIDE)
+        columns = pl.ds(q * (PLANE // 2), PLANE // 2)
         src, dst, to = (r - 1, r, right) if d == 0 else (lax.rem(9 - r, 8), 8 - r, left)
         return remote(w.tokens.at[src, :, columns], w.tokens.at[dst, :, columns], w.relay_s.at[d, q, r], w.relay_r.at[d, q, r], ctx=to)
 
@@ -505,21 +539,24 @@
         relay_round(2 + part)
     relay_round(4)
 
+    plane_out, plane_in = (w.plane_out0, w.plane_out1), (w.plane_in0, w.plane_in1)
+    plane_ret, plane_back = (w.plane_ret0, w.plane_ret1), (w.plane_back0, w.plane_back1)
+
     def plane_box(h, i):
         to = lax.rem(e + i, 8)
-        return remote(w.plane_out.at[h, to], w.plane_in.at[h, e], w.plane_s.at[h, i], w.plane_r.at[h, i], exp=to)
+        return remote(plane_out[h].at[to], plane_in[h].at[e], w.plane_s.at[h, i], w.plane_r.at[h, i], exp=to)
 
     def plane_box_in(h, i):
         source = lax.rem(e + 8 - i, 8)
-        return remote(w.plane_out.at[h, source], w.plane_in.at[h, source], w.plane_s.at[h, i], w.plane_r.at[h, i], exp=source)
-
-    for h in range(2):
-        tokens = w.tokens[:, :, h * WIDE : (h + 1) * WIDE].reshape(256, WIDE)
+        return remote(plane_out[h].at[source], plane_in[h].at[source], w.plane_s.at[h, i], w.plane_r.at[h, i], exp=source)
+
+    for h, (start, width) in enumerate(SHARES):
+        tokens = w.tokens[:, :, start : start + width].reshape(256, width)
         chosen = jnp.dot(w.plane_sel[...], tokens, preferred_element_type=f32).astype(bf)
-        w.plane_out[h] = chosen.reshape(8, 80, WIDE)
+        plane_out[h][...] = chosen.reshape(8, 80, width)
         for i in range(1, 8):
             plane_box(h, i).start()
-        w.plane_in[h, pl.ds(e, 1)] = w.plane_out[h, pl.ds(e, 1)]
+        plane_in[h][pl.ds(e, 1)] = plane_out[h][pl.ds(e, 1)]
     pair[1].wait_recv()
     place(w.sg, w.plane_stream, w.ps, 0, kk)
     for copy in local:
@@ -566,13 +603,13 @@
             for slot in range(8):
                 w.turn[slot * 80 : (slot + 1) * 80, :] = squeeze_map(80, 8, slot)
         if r == 2:
-            weigh_matrix(column_table(), w.plane_mix, 8, 80)
+            weigh_matrix(w.column[...], w.plane_mix, 8, 80)
         if r == 3:
-            for h in range(2):
+            for h, (start, width) in enumerate(SHARES):
                 for i in range(1, 8):
                     plane_box_in(h, i).wait_recv()
-                turned = jnp.dot(w.turn[...], w.plane_in[h].reshape(640, WIDE), preferred_element_type=f32).astype(bf)
-                lanes = slice(RING + h * WIDE, RING + (h + 1) * WIDE)
+                turned = jnp.dot(w.turn[...], plane_in[h][...].reshape(640, width), preferred_element_type=f32).astype(bf)
+                lanes = slice(RING + start, RING + start + width)
                 more = jnp.dot(turned, w.w_in[lanes, :], preferred_element_type=f32)
                 w.half[...] = w.half[...] + more.reshape(8, 80, 512)
             swap(0).start()
@@ -607,65 +644,91 @@
 
     def plane_give(h, i):
         to = lax.rem(e + i, 8)
-        return remote(w.plane_ret.at[h, to], w.plane_back.at[h, e], w.give_s.at[h, i], w.give_r.at[h, i], exp=to)
+        return remote(plane_ret[h].at[to], plane_back[h].at[e], w.give_s.at[h, i], w.give_r.at[h, i], exp=to)
 
     def plane_give_in(h, i):
         source = lax.rem(e + 8 - i, 8)
-        return remote(w.plane_ret.at[h, source], w.plane_back.at[h, source], w.give_s.at[h, i], w.give_r.at[h, i], exp=source)
+        return remote(plane_ret[h].at[source], plane_back[h].at[source], w.give_s.at[h, i], w.give_r.at[h, i], exp=source)
 
     hidden = jnp.dot(w.turn[...], w.hidden[...], preferred_element_type=f32).astype(bf)
-    for h in range(2):
-        out = jnp.dot(hidden, w.w_down[:, RING + h * WIDE : RING + (h + 1) * WIDE], preferred_element_type=f32).astype(bf)
-        w.plane_ret[h] = out.reshape(8, 80, WIDE)
+    for h, (start, width) in enumerate(SHARES):
+        out = jnp.dot(hidden, w.w_down[:, RING + start : RING + start + width], preferred_element_type=f32).astype(bf)
+        plane_ret[h][...] = out.reshape(8, 80, width)
         for i in range(1, 8):
             plane_give(h, i).start()
-        w.plane_back[h, pl.ds(e, 1)] = w.plane_ret[h, pl.ds(e, 1)]
-
-    def reduce(h, d, q, j):
+        plane_back[h][pl.ds(e, 1)] = plane_ret[h][pl.ds(e, 1)]
+
+    def reduce(d, q, j):
         far = reach(d, q) + 1 - j
         slot, to = (far, left) if d == 0 else (8 - far, right)
-        columns = pl.ds(*SUMS[h][q])
+        start, width = SUMS[q]
         return remote(
-            w.partial.at[slot, :, columns], w.plane_arrived.at[h, d, q, j - 1, :, pl.ds(0, SUMS[h][q][1])], w.red_s.at[h, d, q, j - 1],
-            w.red_r.at[h, d, q, j - 1], ctx=to,
+            w.partial.at[slot, :, pl.ds(start, width)], w.plane_arrived.at[d, q, j - 1, :, pl.ds(0, width)],
+            w.red_s.at[d, q, j - 1], w.red_r.at[d, q, j - 1], ctx=to,
         )
 
+    def straight(slot):
+        start, width = SHARES[1]
+        return remote(
+            w.partial.at[slot, :, pl.ds(start, width)], w.straight_in.at[slot], w.straight_s.at[slot], w.straight_r.at[slot],
+            ctx=2 * lax.rem(z + 8 - slot, 8) + k,
+        )
+
     def reduce_start(h):
+        start, width = SHARES[h]
         for i in range(1, 8):
             plane_give_in(h, i).wait_recv()
-        mixed = jnp.dot(w.plane_mix[...], w.plane_back[h].reshape(640, WIDE), preferred_element_type=f32)
+        mixed = jnp.dot(w.plane_mix[...], plane_back[h][...].reshape(640, width), preferred_element_type=f32)
         mixed = mixed[:256] + mixed[256:]
-        w.plane_own[:, h * WIDE : (h + 1) * WIDE] = mixed[:32]
-        w.partial[:, :, h * WIDE : (h + 1) * WIDE] = mixed.astype(bf).reshape(8, 32, WIDE)
-        for q in range(2):
-            for d in range(2):
-                reduce(h, d, q, 1).start()
-
-    def reduce_on(h, j):
-        for q in range(2):
+        w.plane_own[:, start : start + width] = mixed[:32]
+        w.partial[:, :, start : start + width] = mixed.astype(bf).reshape(8, 32, width)
+        if h == 0:
+            for q in range(2):
+                for d in range(2):
+                    reduce(d, q, 1).start()
+        else:
+            for slot in (4, 3, 5, 2, 6, 1, 7):
+                straight(slot).start()
+
+    def reduce_on(j):
+        for q, (start, width) in enumerate(SUMS):
             for d in range(2):
                 if j + 1 <= reach(d, q):
                     far = reach(d, q) - j
                     slot = far if d == 0 else 8 - far
-                    start, width = SUMS[h][q]
                     columns = slice(start, start + width)
-                    reduce(h, d, q, j).wait_recv()
+                    reduce(d, q, j).wait_recv()
                     w.partial[slot, :, columns] = (
-                        w.partial[slot, :, columns].astype(f32) + w.plane_arrived[h, d, q, j - 1, :, 0:width].astype(f32)
+                        w.partial[slot, :, columns].astype(f32) + w.plane_arrived[d, q, j - 1, :, 0:width].astype(f32)
                     ).astype(bf)
-                    reduce(h, d, q, j + 1).start()
-
-    def reduce_end(h):
-        for q in range(2):
-            start, width = SUMS[h][q]
+                    reduce(d, q, j + 1).start()
+
+    def keep(whole, start, width):
+        whole = whole.astype(bf)
+        for b in range(2):
+            w.ready[b, :, RING + start : RING + start + width] = whole[b * 16 : (b + 1) * 16]
+
+    def reduce_end():
+        for q, (start, width) in enumerate(SUMS):
             columns = slice(start, start + width)
             whole = w.plane_own[:, columns] + w.plane_stream[:, columns].astype(f32)
             for d in range(2):
-                reduce(h, d, q, reach(d, q)).wait_recv()
-                whole = whole + w.plane_arrived[h, d, q, reach(d, q) - 1, :, 0:width].astype(f32)
-            whole = whole.astype(bf)
-            for b in range(2):
-                w.ready[b, :, RING + start : RING + start + width] = whole[b * 16 : (b + 1) * 16]
+                reduce(d, q, reach(d, q)).wait_recv()
+                whole = whole + w.plane_arrived[d, q, reach(d, q) - 1, :, 0:width].astype(f32)
+            keep(whole, start, width)
+        for b in range(2):
+            hand(2, b, k).start()
+
+    def straight_end():
+        start, width = SHARES[1]
+        columns = slice(start, start + width)
+        whole = w.plane_own[:, columns] + w.plane_stream[:, columns].astype(f32)
+        for slot in range(1, 8):
+            straight(slot).wait_recv()
+            whole = whole + w.straight_in[slot].astype(f32)
+        keep(whole, start, width)
+        for b in range(2):
+            hand(3, b, k).start()
 
     def give(part, i):
         to = lax.rem(e + i, 8)
@@ -691,7 +754,8 @@
         w.back[part, pl.ds(e, 1)] = w.ret[part, pl.ds(e, 1)]
 
     def hand(part, b, core):
-        columns = pl.ds(part * 3 * GROUP, 3 * GROUP) if part < 2 else pl.ds(RING, PLANE)
+        start, width = HANDS[part]
+        columns = pl.ds(start, width)
         return remote(
             w.ready.at[b, :, columns], w.landed.at[core, :, columns], w.fin_s.at[part, b], w.fin_r.at[part, core],
             pipe=over, ctx=2 * z + b,
@@ -713,28 +777,23 @@
     scatter_on(2)
     reduce_start(0)
     scatter_on(3)
-    reduce_on(0, 1)
-    reduce_start(1)
-    reduce_on(0, 2)
-    reduce_on(0, 3)
-    reduce_on(1, 1)
+    reduce_on(1)
     send_back(0)
     send_back(1)
-    reduce_on(1, 2)
-    reduce_end(0)
-    reduce_on(1, 3)
+    reduce_on(2)
+    reduce_start(1)
+    reduce_on(3)
     finish_ring(0)
-    reduce_end(1)
-    for b in range(2):
-        hand(2, b, k).start()
+    reduce_end()
     finish_ring(1)
-    for part in range(3):
+    straight_end()
+    for part in range(4):
         for b in range(2):
             hand(part, b, b).wait_recv()
     for b in range(2):
         out_ref[:, b * HALF : (b + 1) * HALF] = w.landed[b]
 
-    for part in range(3):
+    for part in range(4):
         for b in range(2):
             hand(part, b, k).wait_send()
     for copy in pair:
@@ -742,6 +801,7 @@
 
     def sent(i, carry):
         spread_table(i).wait_send()
+        straight(i).wait_send()
         for h in range(2):
             plane_box(h, i).wait_send()
             plane_give(h, i).wait_send()
@@ -760,8 +820,7 @@
                     scatter(d, q, r).wait_send()
                     if q < 2:
                         relay(d, q, r).wait_send()
-                        for h in range(2):
-                            reduce(h, d, q, r).wait_send()
+                        reduce(d, q, r).wait_send()
         return carry
 
     lax.fori_loop(1, 5, gone, 0)
@@ -777,28 +836,30 @@
     "sums": ((1024, 128), F32), "mixed": ((1024, LAT), F32), "value_up": ((8, LAT, 128), BF), "heads": ((8, 128, 1024), BF),
     "proj": ((896, 1024), BF), "proj_all": ((1024, 896), BF), "product": ((8, 128, 896), F32),
     "fold_out": ((8, 64, 896), BF), "fold_in": ((8, 64, 896), BF), "cross_out": ((8, 64, 896), BF),
-    "cross_in": ((8, 3, 16, 896), BF), "part_out": ((8, 16, 896), BF), "parts": ((8, 16, 896), BF), "stream": ((16, D), BF),
-    "table": ((8, 2, 16, 128), F32), "sel": ((256, 96), BF), "mix": ((192, 256), BF), "turn": ((640, 640), BF),
+    "cross_in": ((8, 3, 16, 896), BF), "direct_out": ((128, 896), BF), "direct_in": ((7, 16, 896), BF), "part_out": ((8, 16, 896), BF), "parts": ((8, 16, 896), BF), "stream": ((16, D), BF),
+    "table": ((2, 16, 128), F32), "brief": ((8, 8, 128), F32), "column": ((256, 128), F32), "sel": ((256, 96), BF), "mix": ((192, 256), BF), "turn": ((640, 640), BF),
     "plane_sel": ((640, 256), BF), "plane_mix": ((512, 640), BF),
     "normed": ((16, D), BF), "pn": ((16, HALF), BF), "ps": ((16, HALF), BF), "tokens": ((8, 32, PLANE), BF),
     "xg": ((2, 96, GROUP), BF), "sg": ((2, 96, GROUP), BF), "plane_stream": ((32, PLANE), BF),
     "outbox": ((2, 8, 32, GROUP), BF), "inbox": ((2, 8, 32, GROUP), BF), "ret": ((2, 8, 32, GROUP), BF),
-    "back": ((2, 8, 32, GROUP), BF), "plane_out": ((2, 8, 80, WIDE), BF), "plane_in": ((2, 8, 80, WIDE), BF),
-    "plane_ret": ((2, 8, 80, WIDE), BF), "plane_back": ((2, 8, 80, WIDE), BF),
+    "back": ((2, 8, 32, GROUP), BF), "plane_out0": ((8, 80, 896), BF), "plane_in0": ((8, 80, 896), BF),
+    "plane_ret0": ((8, 80, 896), BF), "plane_back0": ((8, 80, 896), BF), "plane_out1": ((8, 80, 384), BF),
+    "plane_in1": ((8, 80, 384), BF), "plane_ret1": ((8, 80, 384), BF), "plane_back1": ((8, 80, 384), BF),
+    "straight_in": ((8, 32, 384), BF),
     "w_in": ((HALF, 512), BF), "w_down": ((256, HALF), BF), "rows": ((8, 80, RING), BF),
     "half": ((8, 80, 512), F32), "half_other": ((8, 80, 512), F32), "hidden": ((640, 256), BF), "total": ((8, 80, RING), BF),
     "arrived": ((2, PIECES, 4, 80, GROUP), BF), "partial": ((8, 32, PLANE), BF), "plane_own": ((32, PLANE), F32),
-    "plane_arrived": ((2, 2, 2, 4, 32, 384), BF), "ready": ((2, 16, HALF), BF), "landed": ((2, 16, HALF), BF),
+    "plane_arrived": ((2, 2, 4, 32, 512), BF), "ready": ((2, 16, HALF), BF), "landed": ((2, 16, HALF), BF),
     "load": ((9,), None), "chain_s": ((5, 4), None), "chain_r": ((5, 4), None), "share_s": ((5,), None), "share_r": ((5,), None),
     "proj_s": ((1,), None), "proj_r": ((1,), None), "head_s": ((2, 2, 5), None), "head_r": ((2, 2, 5), None),
     "fold_s": ((8,), None), "fold_r": ((8,), None), "cross_s": ((8, 3), None), "cross_r": ((8, 3), None),
-    "part_s": ((8,), None), "part_r": ((8,), None),
+    "part_s": ((8,), None), "part_r": ((8,), None), "direct_s": ((8,), None), "direct_r": ((8,), None),
     "pair_s": ((6,), None), "pair_r": ((6,), None), "loc": ((3,), None), "table_s": ((8,), None), "table_r": ((8,), None),
     "box_s": ((2, 8), None), "box_r": ((2, 8), None), "relay_s": ((2, 2, 5), None), "relay_r": ((2, 2, 5), None),
     "plane_s": ((2, 8), None), "plane_r": ((2, 8), None), "give_s": ((2, 8), None), "give_r": ((2, 8), None),
     "ag_s": ((2, PIECES, 5), None), "ag_r": ((2, PIECES, 5), None), "half_s": ((3,), None), "half_r": ((3,), None),
-    "rs_s": ((2, PIECES, 4), None), "rs_r": ((2, PIECES, 4), None), "red_s": ((2, 2, 2, 4), None), "red_r": ((2, 2, 2, 4), None),
-    "back_s": ((2, 8), None), "back_r": ((2, 8), None), "fin_s": ((3, 2), None), "fin_r": ((3, 2), None),
+    "rs_s": ((2, PIECES, 4), None), "rs_r": ((2, PIECES, 4), None), "red_s": ((2, 2, 4), None), "red_r": ((2, 2, 4), None), "straight_s": ((8,), None), "straight_r": ((8,), None),
+    "back_s": ((2, 8), None), "back_r": ((2, 8), None), "fin_s": ((4, 2), None), "fin_r": ((4, 2), None),
 }
 
 

time: 181 us -> 175 us (0.967)
  Pallas kernels: 179 us -> 173 us
    pallas_call x1, Pallas kernels: 179 us -> 173 us  [on_device(): pl.pallas_call(layer_kernel, out_shape=jax.ShapeDtypeStruct((16, D), BF),...]
where the time goes in v6:
time: 175 us
  Pallas kernels  173 us (99%)
    pallas_call x1, Pallas kernels, on_device(): pl.pallas_call(layer_kernel, out_shape=jax.ShapeDtypeStruct((16, D), BF),...  173 us

profile of v6, /device:TPU:1, one launch (start us, length us, event | category | flops | bytes accessed | tf_op | source)
XLA Modules:
  0.0 174.6 jit_solution(3294737903458234931)
XLA Ops:
  0.0 172.9 %layer.1 = bf16[16,7168]{1,0:T(8,128)(2,1)} custom-call(bf16[8,576,128]{2,1,0:T(8,128)(2,1)} %bitcast.25, bf16[576,128]{1,0:T(8,128)(2,1)} %bitcast.29, s32[1,128]{1,0:T(1,128)} %doc_ref.1, s32[2,16]{1,0:T(2,128)} %bitcast.30, f32[2,16]{1,0:T(2,128)} %bitcast.31, bf16[16,7168]{1,0:T(8,128)(2,1)} %bitcast.28, f32[1,7168]{1,0:T(1,128)} %gain_ref.1, ...), custom_call_target="tpu_custom_call" | custom-call | flops 8000000000 | bytes 10000000 | tf_op jit(solution)/shard_map/layer/pallas_call | solution.py:871
  172.9 1.6 copy.14

commit v7 on v6

--- a/solution.py
+++ b/solution.py
@@ -31,6 +31,10 @@
         device_id=device,
         device_id_type=MESH,
     )
+
+
+def take(ref, sem):
+    pltpu.make_async_copy(ref, ref, sem).wait()
 
 
 def meet(peers):
@@ -87,24 +91,24 @@
     def chain(s, q):
         piece = pl.ds(*KEY_PIECES[q])
         return remote(
-            w.keys.at[s - 1, piece, my_lanes], w.keys.at[s, piece, my_lanes], w.chain_s.at[s, q], w.chain_r.at[s, q], ctx=right
+            w.keys.at[s - 1, piece, my_lanes], w.keys.at[s, piece, my_lanes], w.chain_s.at[0], w.chain_r.at[s - 1, q], ctx=right
         )
 
     def share(s):
-        return remote(w.keys.at[s, :, my_lanes], w.keys.at[s, :, my_lanes], w.share_s.at[s], w.share_r.at[s], ctx=other)
+        return remote(w.keys.at[s, :, my_lanes], w.keys.at[s, :, my_lanes], w.share_s.at[0], w.share_r.at[s], ctx=other)
 
     def share_in(s):
-        return remote(w.keys.at[s, :, their_lanes], w.keys.at[s, :, their_lanes], w.share_s.at[s], w.share_r.at[s], ctx=other)
+        return remote(w.keys.at[s, :, their_lanes], w.keys.at[s, :, their_lanes], w.share_s.at[0], w.share_r.at[s], ctx=other)
 
     for q in range(4):
         chain(1, q).start()
     share(0).start()
-    own_proj = pltpu.make_async_copy(op_ref, w.proj.at[my_columns], w.load.at[8])
+    own_proj = pltpu.make_async_copy(op_ref, w.proj.at[my_columns], w.load.at[1])
     own_proj.start()
     pair_proj = remote(op_ref, w.proj.at[my_columns], w.proj_s.at[0], w.proj_r.at[0], ctx=other)
     pair_proj.start()
     up_loads = [
-        pltpu.make_async_copy(vu_ref.at[h], w.value_up.at[h], w.load.at[h]) for h in range(8)
+        pltpu.make_async_copy(vu_ref.at[h], w.value_up.at[h], w.load.at[0]) for h in range(8)
     ]
     for copy in up_loads:
         copy.start()
@@ -118,19 +122,7 @@
     contract_last = (((1,), (1,)), ((), ()))
     query_pos = c * 128 + lax.broadcasted_iota(jnp.int32, (128, 256), 0)
 
-    def visit(s, carry):
-        @pl.when(s >= 1)
-        def _():
-            for q in range(4):
-                chain(s, q).wait_recv()
-
-                @pl.when(s < 4)
-                def _(q=q):
-                    chain(s + 1, q).start()
-
-            share(s).start()
-
-        share_in(s).wait_recv()
+    def attend_to(s):
         key_doc = w.keys[s, KV:, :].astype(f32)[0:1]
         key_pos = lax.rem(z + 8 - s, 8) * 256 + lax.broadcasted_iota(jnp.int32, (128, 256), 1)
         query_doc = jnp.concatenate([w.query_doc[...]] * 2, axis=1)
@@ -151,19 +143,35 @@
             return carry
 
         lax.fori_loop(0, 2, some, 0)
+
+    def visit(s, carry):
+        def pass_keys(pieces):
+            for q in pieces:
+                chain(s, q).wait_recv()
+
+                @pl.when(s < 4)
+                def _(q=q):
+                    chain(s + 1, q).start()
+
+        pass_keys((0, 1))
+        share_in(s - 1).wait_recv()
+        attend_to(s - 1)
+        pass_keys((2, 3))
+        share(s).start()
         return carry
 
-    lax.fori_loop(0, 5, visit, 0)
-
-    for copy in up_loads:
-        copy.wait()
+    lax.fori_loop(1, 5, visit, 0)
+    share_in(4).wait_recv()
+    attend_to(4)
+
+    take(w.value_up, w.load.at[0])
 
     def gather(d, q, r):
         piece = pl.ds(q * 64, 64)
         if d == 0:
-            return remote(w.heads.at[r - 1, piece], w.heads.at[r, piece], w.head_s.at[d, q, r], w.head_r.at[d, q, r], ctx=right)
+            return remote(w.heads.at[r - 1, piece], w.heads.at[r, piece], w.head_s.at[0], w.head_r.at[d, q, r - 1], ctx=right)
         return remote(
-            w.heads.at[lax.rem(9 - r, 8), piece], w.heads.at[8 - r, piece], w.head_s.at[d, q, r], w.head_r.at[d, q, r], ctx=left
+            w.heads.at[lax.rem(9 - r, 8), piece], w.heads.at[8 - r, piece], w.head_s.at[0], w.head_r.at[d, q, r - 1], ctx=left
         )
 
     for h in range(8):
@@ -183,23 +191,19 @@
     x_mine = pl.multiple_of(x * 16, 16)
 
     def fold(slot):
-        return remote(w.fold_out.at[slot], w.fold_in.at[slot], w.fold_s.at[slot], w.fold_r.at[slot], exp=lax.rem(e + 4, 8))
+        return remote(w.fold_out.at[slot], w.fold_in.at[slot], w.fold_s.at[0], w.fold_r.at[slot], exp=lax.rem(e + 4, 8))
 
     def cross(slot, i):
         to = lax.rem(x + i, 4)
         return remote(
             w.cross_out.at[slot, pl.ds(pl.multiple_of(to * 16, 16), 16)], w.cross_in.at[slot, i - 1],
-            w.cross_s.at[slot, i - 1], w.cross_r.at[slot, i - 1], exp=4 * y + to,
+            w.cross_s.at[0], w.cross_r.at[slot], exp=4 * y + to,
         )
 
     def deliver(slot):
         return remote(
-            w.part_out.at[slot], w.parts.at[z], w.part_s.at[slot], w.part_r.at[slot], ctx=2 * lax.rem(z + 8 - slot, 8) + k
+            w.part_out.at[slot], w.parts.at[z], w.part_s.at[0], w.part_r.at[0], ctx=2 * lax.rem(z + 8 - slot, 8) + k
         )
-
-    def deliver_in(slot):
-        source = lax.rem(z + slot, 8)
-        return remote(w.part_out.at[slot], w.parts.at[source], w.part_s.at[slot], w.part_r.at[slot], ctx=2 * source + k)
 
     def project(slot):
         w.product[slot] = jnp.dot(w.heads[slot], w.proj_all[...], preferred_element_type=f32)
@@ -209,7 +213,7 @@
     def direct(i):
         to = lax.rem(e + i, 8)
         return remote(
-            w.direct_out.at[pl.ds(pl.multiple_of(to * 16, 16), 16)], w.direct_in.at[i - 1], w.direct_s.at[i], w.direct_r.at[i], exp=to
+            w.direct_out.at[pl.ds(pl.multiple_of(to * 16, 16), 16)], w.direct_in.at[i - 1], w.direct_s.at[0], w.direct_r.at[0], exp=to
         )
 
     def project_last():
@@ -220,9 +224,9 @@
 
     def sum_last():
         whole = w.product[4, pl.ds(pl.multiple_of(e * 16, 16), 16), :]
-        for i in range(1, 8):
-            direct(i).wait_recv()
-            whole = whole + w.direct_in[i - 1].astype(f32)
+        take(w.direct_in, w.direct_r.at[0])
+        for i in range(7):
+            whole = whole + w.direct_in[i].astype(f32)
         w.part_out[4] = whole.astype(bf)
         deliver(4).start()
 
@@ -236,9 +240,9 @@
 
     def over_x(slot):
         whole = w.product[slot, pl.ds(pl.multiple_of(y_mine + x_mine, 16), 16), :]
-        for i in range(1, 4):
-            cross(slot, i).wait_recv()
-            whole = whole + w.cross_in[slot, i - 1].astype(f32)
+        take(w.cross_in.at[slot], w.cross_r.at[slot])
+        for i in range(3):
+            whole = whole + w.cross_in[slot, i].astype(f32)
         w.part_out[slot] = whole.astype(bf)
 
         @pl.when(slot >= 1)
@@ -282,51 +286,20 @@
 
     lax.fori_loop(0, 7, turn, 0)
     w.parts[pl.ds(z, 1)] = w.part_out[0:1]
-    for slot in range(1, 8):
-        deliver_in(slot).wait_recv()
+    take(w.parts.at[pl.ds(0, 7)], w.part_r.at[0])
     for other_z in range(8):
         columns = slice(other_z * 896, (other_z + 1) * 896)
         w.stream[:, columns] = (residual_ref[:, columns].astype(f32) + w.parts[other_z].astype(f32)).astype(bf)
 
     def settle():
         pair_proj.wait_send()
-
-        def chained(s, carry):
-            for q in range(4):
-                chain(s, q).wait_send()
-            return carry
-
-        lax.fori_loop(1, 5, chained, 0)
-
-        def shared(s, carry):
-            share(s).wait_send()
-            return carry
-
-        lax.fori_loop(0, 5, shared, 0)
-        for q in range(2):
-            for d in range(2):
-                def gathered(r, carry, d=d, q=q):
-                    gather(d, q, r).wait_send()
-                    return carry
-
-                lax.fori_loop(1, reach(d, q) + 1, gathered, 0)
-
-        for i in range(1, 8):
-            direct(i).wait_send()
-
-        def folded(slot, carry):
-            @pl.when(slot != 4)
-            def _():
-                fold(slot).wait_send()
-                for i in range(1, 4):
-                    cross(slot, i).wait_send()
-
-            @pl.when(slot >= 1)
-            def _():
-                deliver(slot).wait_send()
-            return carry
-
-        lax.fori_loop(0, 8, folded, 0)
+        take(w.keys.at[pl.ds(1, 4), :, my_lanes], w.chain_s.at[0])
+        take(w.keys.at[:, :, my_lanes], w.share_s.at[0])
+        take(w.heads.at[pl.ds(1, 7)], w.head_s.at[0])
+        take(w.fold_out.at[pl.ds(0, 7)], w.fold_s.at[0])
+        take(w.cross_in.at[pl.ds(0, 7)], w.cross_s.at[0])
+        take(w.part_out.at[pl.ds(0, 7)], w.part_s.at[0])
+        take(w.direct_in, w.direct_s.at[0])
 
     return settle
 
@@ -441,7 +414,7 @@
             copy.start()
 
     def spread_table(i):
-        return remote(w.brief.at[0], w.brief.at[i], w.table_s.at[i], w.table_r.at[i], ctx=2 * lax.rem(z + i, 8) + k)
+        return remote(w.brief.at[0], w.brief.at[i], w.table_s.at[0], w.table_r.at[0], ctx=2 * lax.rem(z + i, 8) + k)
 
     def chip_table():
         return jnp.concatenate([w.table[...].reshape(32, 128)] * 4, axis=0)
@@ -460,8 +433,7 @@
 
         @pl.when(r == 6)
         def _():
-            for i in range(1, 8):
-                spread_table(i).wait_recv()
+            take(w.brief.at[pl.ds(0, 7)], w.table_r.at[0])
             for i in range(8):
                 w.column[i * 32 : (i + 1) * 32, :] = jnp.transpose(jnp.concatenate([w.brief[i]] * 16, axis=0))[0:32]
             choose_matrix(w.column[...], w.plane_sel, 8, 80)
@@ -488,7 +460,7 @@
     def relay(d, q, r):
         columns = pl.ds(q * (PLANE // 2), PLANE // 2)
         src, dst, to = (r - 1, r, right) if d == 0 else (lax.rem(9 - r, 8), 8 - r, left)
-        return remote(w.tokens.at[src, :, columns], w.tokens.at[dst, :, columns], w.relay_s.at[d, q, r], w.relay_r.at[d, q, r], ctx=to)
+        return remote(w.tokens.at[src, :, columns], w.tokens.at[dst, :, columns], w.relay_s.at[0], w.relay_r.at[d, q, r - 1], ctx=to)
 
     def relay_round(r):
         for q in range(2):
@@ -504,13 +476,7 @@
 
     def box(part, i):
         to = lax.rem(e + i, 8)
-        return remote(w.outbox.at[part, to], w.inbox.at[part, e], w.box_s.at[part, i], w.box_r.at[part, i], exp=to)
-
-    def box_in(part, i):
-        source = lax.rem(e + 8 - i, 8)
-        return remote(
-            w.outbox.at[part, source], w.inbox.at[part, source], w.box_s.at[part, i], w.box_r.at[part, i], exp=source
-        )
+        return remote(w.outbox.at[part, to], w.inbox.at[part, e], w.box_s.at[0], w.box_r.at[part], exp=to)
 
     for part in range(2):
         chosen = jnp.dot(w.sel[...], w.xg[part], preferred_element_type=f32).astype(bf)
@@ -523,11 +489,10 @@
     def gather(d, q, r):
         columns = pl.ds(q * GROUP, GROUP)
         src, dst, to = (r - 1, r, right) if d == 0 else (lax.rem(9 - r, 8), 8 - r, left)
-        return remote(w.rows.at[src, :, columns], w.rows.at[dst, :, columns], w.ag_s.at[d, q, r], w.ag_r.at[d, q, r], ctx=to)
+        return remote(w.rows.at[src, :, columns], w.rows.at[dst, :, columns], w.ag_s.at[0], w.ag_r.at[d, q, r - 1], ctx=to)
 
     for part in range(2):
-        for i in range(1, 8):
-            box_in(part, i).wait_recv()
+        take(w.inbox.at[part, pl.ds(0, 7)], w.box_r.at[part])
         landed_rows = w.inbox[part].reshape(256, GROUP)
         for g in range(3):
             q = part * 3 + g
@@ -544,11 +509,7 @@
 
     def plane_box(h, i):
         to = lax.rem(e + i, 8)
-        return remote(plane_out[h].at[to], plane_in[h].at[e], w.plane_s.at[h, i], w.plane_r.at[h, i], exp=to)
-
-    def plane_box_in(h, i):
-        source = lax.rem(e + 8 - i, 8)
-        return remote(plane_out[h].at[source], plane_in[h].at[source], w.plane_s.at[h, i], w.plane_r.at[h, i], exp=source)
+        return remote(plane_out[h].at[to], plane_in[h].at[e], w.plane_s.at[h], w.plane_r.at[h], exp=to)
 
     for h, (start, width) in enumerate(SHARES):
         tokens = w.tokens[:, :, start : start + width].reshape(256, width)
@@ -568,7 +529,7 @@
 
     def swap(n):
         slots = pl.ds(*BATCHES[n])
-        return remote(w.half.at[slots], w.half_other.at[slots], w.half_s.at[n], w.half_r.at[n], ctx=other)
+        return remote(w.half.at[slots], w.half_other.at[slots], w.half_s.at[0], w.half_r.at[n], ctx=other)
 
     def ring_half(slot):
         w.half[slot] = w.half[slot] + jnp.dot(w.rows[slot], w.w_in[0:RING, :], preferred_element_type=f32)
@@ -585,6 +546,12 @@
             columns = slice(part * 3 * GROUP, (part + 1) * 3 * GROUP)
             out = jnp.dot(hidden, w.w_down[:, columns], preferred_element_type=f32).astype(bf)
             w.total[slots, :, columns] = out.reshape(count, 80, 3 * GROUP)
+
+    def scatter(d, q, j):
+        far = reach(d, q) + 1 - j
+        slot, to = (far, left) if d == 0 else (8 - far, right)
+        columns = pl.ds(q * GROUP, GROUP)
+        return remote(w.total.at[slot, :, columns], w.arrived.at[d, q, j - 1], w.rs_s.at[0], w.rs_r.at[d, q, j - 1], ctx=to)
 
     w.half[...] = jnp.zeros((8, 80, 512), f32)
     ring_half(0)
@@ -606,8 +573,7 @@
             weigh_matrix(w.column[...], w.plane_mix, 8, 80)
         if r == 3:
             for h, (start, width) in enumerate(SHARES):
-                for i in range(1, 8):
-                    plane_box_in(h, i).wait_recv()
+                take(plane_in[h].at[pl.ds(0, 7)], w.plane_r.at[h])
                 turned = jnp.dot(w.turn[...], plane_in[h][...].reshape(640, width), preferred_element_type=f32).astype(bf)
                 lanes = slice(RING + start, RING + start + width)
                 more = jnp.dot(turned, w.w_in[lanes, :], preferred_element_type=f32)
@@ -616,14 +582,12 @@
             swap(1).start()
             second_half(0)
             second_half(1)
+            for q in range(PIECES):
+                for d in range(2):
+                    if reach(d, q) == 3:
+                        scatter(d, q, 1).start()
     swap(2).start()
     second_half(2)
-
-    def scatter(d, q, j):
-        far = reach(d, q) + 1 - j
-        slot, to = (far, left) if d == 0 else (8 - far, right)
-        columns = pl.ds(q * GROUP, GROUP)
-        return remote(w.total.at[slot, :, columns], w.arrived.at[d, q, j - 1], w.rs_s.at[d, q, j - 1], w.rs_r.at[d, q, j - 1], ctx=to)
 
     def scatter_on(j):
         for q in range(PIECES):
@@ -640,15 +604,12 @@
 
     for q in range(PIECES):
         for d in range(2):
-            scatter(d, q, 1).start()
+            if reach(d, q) == 4:
+                scatter(d, q, 1).start()
 
     def plane_give(h, i):
         to = lax.rem(e + i, 8)
-        return remote(plane_ret[h].at[to], plane_back[h].at[e], w.give_s.at[h, i], w.give_r.at[h, i], exp=to)
-
-    def plane_give_in(h, i):
-        source = lax.rem(e + 8 - i, 8)
-        return remote(plane_ret[h].at[source], plane_back[h].at[source], w.give_s.at[h, i], w.give_r.at[h, i], exp=source)
+        return remote(plane_ret[h].at[to], plane_back[h].at[e], w.give_s.at[h], w.give_r.at[h], exp=to)
 
     hidden = jnp.dot(w.turn[...], w.hidden[...], preferred_element_type=f32).astype(bf)
     for h, (start, width) in enumerate(SHARES):
@@ -664,20 +625,19 @@
         start, width = SUMS[q]
         return remote(
             w.partial.at[slot, :, pl.ds(start, width)], w.plane_arrived.at[d, q, j - 1, :, pl.ds(0, width)],
-            w.red_s.at[d, q, j - 1], w.red_r.at[d, q, j - 1], ctx=to,
+            w.red_s.at[0], w.red_r.at[d, q, j - 1], ctx=to,
         )
 
     def straight(slot):
         start, width = SHARES[1]
         return remote(
-            w.partial.at[slot, :, pl.ds(start, width)], w.straight_in.at[slot], w.straight_s.at[slot], w.straight_r.at[slot],
+            w.partial.at[slot, :, pl.ds(start, width)], w.straight_in.at[slot], w.straight_s.at[0], w.straight_r.at[0],
             ctx=2 * lax.rem(z + 8 - slot, 8) + k,
         )
 
     def reduce_start(h):
         start, width = SHARES[h]
-        for i in range(1, 8):
-            plane_give_in(h, i).wait_recv()
+        take(plane_back[h].at[pl.ds(0, 7)], w.give_r.at[h])
         mixed = jnp.dot(w.plane_mix[...], plane_back[h][...].reshape(640, width), preferred_element_type=f32)
         mixed = mixed[:256] + mixed[256:]
         w.plane_own[:, start : start + width] = mixed[:32]
@@ -723,8 +683,8 @@
         start, width = SHARES[1]
         columns = slice(start, start + width)
         whole = w.plane_own[:, columns] + w.plane_stream[:, columns].astype(f32)
+        take(w.straight_in.at[pl.ds(0, 7)], w.straight_r.at[0])
         for slot in range(1, 8):
-            straight(slot).wait_recv()
             whole = whole + w.straight_in[slot].astype(f32)
         keep(whole, start, width)
         for b in range(2):
@@ -732,11 +692,7 @@
 
     def give(part, i):
         to = lax.rem(e + i, 8)
-        return remote(w.ret.at[part, to], w.back.at[part, e], w.back_s.at[part, i], w.back_r.at[part, i], exp=to)
-
-    def give_in(part, i):
-        source = lax.rem(e + 8 - i, 8)
-        return remote(w.ret.at[part, source], w.back.at[part, source], w.back_s.at[part, i], w.back_r.at[part, i], exp=source)
+        return remote(w.ret.at[part, to], w.back.at[part, e], w.back_s.at[0], w.back_r.at[part], exp=to)
 
     def send_back(part):
         spread = jnp.zeros((256, GROUP), f32)
@@ -757,13 +713,12 @@
         start, width = HANDS[part]
         columns = pl.ds(start, width)
         return remote(
-            w.ready.at[b, :, columns], w.landed.at[core, :, columns], w.fin_s.at[part, b], w.fin_r.at[part, core],
+            w.ready.at[b, :, columns], w.landed.at[core, :, columns], w.fin_s.at[0], w.fin_r.at[0],
             pipe=over, ctx=2 * z + b,
         )
 
     def finish_ring(part):
-        for i in range(1, 8):
-            give_in(part, i).wait_recv()
+        take(w.back.at[part, pl.ds(0, 7)], w.back_r.at[part])
         mixed = jnp.dot(w.mix[...], w.back[part].reshape(256, GROUP), preferred_element_type=f32)
         layer_out = (w.sg[part].astype(f32) + (mixed[:96] + mixed[96:])).astype(bf)
         for g in range(3):
@@ -787,46 +742,25 @@
     reduce_end()
     finish_ring(1)
     straight_end()
-    for part in range(4):
-        for b in range(2):
-            hand(part, b, b).wait_recv()
+    take(w.landed, w.fin_r.at[0])
     for b in range(2):
         out_ref[:, b * HALF : (b + 1) * HALF] = w.landed[b]
 
-    for part in range(4):
-        for b in range(2):
-            hand(part, b, k).wait_send()
+    take(w.ready, w.fin_s.at[0])
     for copy in pair:
         copy.wait_send()
-
-    def sent(i, carry):
-        spread_table(i).wait_send()
-        straight(i).wait_send()
-        for h in range(2):
-            plane_box(h, i).wait_send()
-            plane_give(h, i).wait_send()
-            box(h, i).wait_send()
-            give(h, i).wait_send()
-        return carry
-
-    lax.fori_loop(1, 8, sent, 0)
-
-    def gone(r, carry):
-        for q in range(PIECES):
-            for d in range(2):
-                @pl.when(r <= reach(d, q))
-                def _(d=d, q=q):
-                    gather(d, q, r).wait_send()
-                    scatter(d, q, r).wait_send()
-                    if q < 2:
-                        relay(d, q, r).wait_send()
-                        reduce(d, q, r).wait_send()
-        return carry
-
-    lax.fori_loop(1, 5, gone, 0)
-
-    for n in range(3):
-        swap(n).wait_send()
+    take(w.brief.at[pl.ds(0, 7)], w.table_s.at[0])
+    take(w.tokens.at[pl.ds(1, 7)], w.relay_s.at[0])
+    take(w.inbox.at[:, pl.ds(0, 7)], w.box_s.at[0])
+    take(w.back.at[:, pl.ds(0, 7)], w.back_s.at[0])
+    for h in range(2):
+        take(plane_out[h].at[pl.ds(0, 7)], w.plane_s.at[h])
+        take(plane_ret[h].at[pl.ds(0, 7)], w.give_s.at[h])
+    take(w.rows.at[pl.ds(1, 7)], w.ag_s.at[0])
+    take(w.total.at[pl.ds(1, 7)], w.rs_s.at[0])
+    take(w.half, w.half_s.at[0])
+    take(w.partial.at[pl.ds(1, 7), :, pl.ds(0, 896)], w.red_s.at[0])
+    take(w.straight_in.at[pl.ds(0, 7)], w.straight_s.at[0])
     settle()
 
 
@@ -850,16 +784,17 @@
     "half": ((8, 80, 512), F32), "half_other": ((8, 80, 512), F32), "hidden": ((640, 256), BF), "total": ((8, 80, RING), BF),
     "arrived": ((2, PIECES, 4, 80, GROUP), BF), "partial": ((8, 32, PLANE), BF), "plane_own": ((32, PLANE), F32),
     "plane_arrived": ((2, 2, 4, 32, 512), BF), "ready": ((2, 16, HALF), BF), "landed": ((2, 16, HALF), BF),
-    "load": ((9,), None), "chain_s": ((5, 4), None), "chain_r": ((5, 4), None), "share_s": ((5,), None), "share_r": ((5,), None),
-    "proj_s": ((1,), None), "proj_r": ((1,), None), "head_s": ((2, 2, 5), None), "head_r": ((2, 2, 5), None),
-    "fold_s": ((8,), None), "fold_r": ((8,), None), "cross_s": ((8, 3), None), "cross_r": ((8, 3), None),
-    "part_s": ((8,), None), "part_r": ((8,), None), "direct_s": ((8,), None), "direct_r": ((8,), None),
-    "pair_s": ((6,), None), "pair_r": ((6,), None), "loc": ((3,), None), "table_s": ((8,), None), "table_r": ((8,), None),
-    "box_s": ((2, 8), None), "box_r": ((2, 8), None), "relay_s": ((2, 2, 5), None), "relay_r": ((2, 2, 5), None),
-    "plane_s": ((2, 8), None), "plane_r": ((2, 8), None), "give_s": ((2, 8), None), "give_r": ((2, 8), None),
-    "ag_s": ((2, PIECES, 5), None), "ag_r": ((2, PIECES, 5), None), "half_s": ((3,), None), "half_r": ((3,), None),
-    "rs_s": ((2, PIECES, 4), None), "rs_r": ((2, PIECES, 4), None), "red_s": ((2, 2, 4), None), "red_r": ((2, 2, 4), None), "straight_s": ((8,), None), "straight_r": ((8,), None),
-    "back_s": ((2, 8), None), "back_r": ((2, 8), None), "fin_s": ((4, 2), None), "fin_r": ((4, 2), None),
+    "load": ((2,), None), "chain_s": ((1,), None), "chain_r": ((4, 4), None), "share_s": ((1,), None), "share_r": ((5,), None),
+    "proj_s": ((1,), None), "proj_r": ((1,), None), "head_s": ((1,), None), "head_r": ((2, 2, 4), None),
+    "fold_s": ((1,), None), "fold_r": ((8,), None), "cross_s": ((1,), None), "cross_r": ((8,), None),
+    "part_s": ((1,), None), "part_r": ((1,), None), "direct_s": ((1,), None), "direct_r": ((1,), None),
+    "pair_s": ((6,), None), "pair_r": ((6,), None), "loc": ((3,), None), "table_s": ((1,), None), "table_r": ((1,), None),
+    "box_s": ((1,), None), "box_r": ((2,), None), "relay_s": ((1,), None), "relay_r": ((2, 2, 4), None),
+    "plane_s": ((2,), None), "plane_r": ((2,), None), "give_s": ((2,), None), "give_r": ((2,), None),
+    "ag_s": ((1,), None), "ag_r": ((2, PIECES, 4), None), "half_s": ((1,), None), "half_r": ((3,), None),
+    "rs_s": ((1,), None), "rs_r": ((2, PIECES, 4), None), "red_s": ((1,), None), "red_r": ((2, 2, 4), None),
+    "straight_s": ((1,), None), "straight_r": ((1,), None), "back_s": ((1,), None), "back_r": ((2,), None),
+    "fin_s": ((1,), None), "fin_r": ((1,), None),
 }
 
 

time: 175 us -> 167 us (0.954)
  Pallas kernels: 173 us -> 166 us
    pallas_call x1, Pallas kernels: 173 us -> 166 us  [on_device(): pl.pallas_call(layer_kernel, out_shape=jax.ShapeDtypeStruct((16, D), BF),...]
where the time goes in v7:
time: 167 us
  Pallas kernels  166 us (99%)
    pallas_call x1, Pallas kernels, on_device(): pl.pallas_call(layer_kernel, out_shape=jax.ShapeDtypeStruct((16, D), BF),...  166 us

profile of v7, /device:TPU:1, one launch (start us, length us, event | category | flops | bytes accessed | tf_op | source)
XLA Modules:
  0.0 167.2 jit_solution(6305469062136551694)
XLA Ops:
  0.0 165.5 %layer.1 = bf16[16,7168]{1,0:T(8,128)(2,1)} custom-call(bf16[8,576,128]{2,1,0:T(8,128)(2,1)} %bitcast.25, bf16[576,128]{1,0:T(8,128)(2,1)} %bitcast.29, s32[1,128]{1,0:T(1,128)} %doc_ref.1, s32[2,16]{1,0:T(2,128)} %bitcast.30, f32[2,16]{1,0:T(2,128)} %bitcast.31, bf16[16,7168]{1,0:T(8,128)(2,1)} %bitcast.28, f32[1,7168]{1,0:T(1,128)} %gain_ref.1, ...), custom_call_target="tpu_custom_call" | custom-call | flops 8000000000 | bytes 10000000 | tf_op jit(solution)/shard_map/layer/pallas_call | solution.py:806
  165.6 1.6 copy.14

commit v8 on v7

--- a/solution.py
+++ b/solution.py
@@ -387,7 +387,7 @@
     w.keys[0, KV:, pl.ds(my_lane, 128)] = doc_row[0:16].astype(bf)
     w.query_doc[...] = jnp.broadcast_to(column_of(doc_row), (128, 128))
     meet(
-        [{"ctx": other}, {"pipe": over}, {"pipe": over, "ctx": other}]
+        [{"ctx": other}, {"pipe": over}, {"pipe": over, "ctx": other}, {"pipe": over, "exp": lax.rem(e + 4, 8)}]
         + [{"ctx": 2 * lax.rem(z + i, 8) + k} for i in range(1, 8)]
         + [{"exp": lax.rem(e + i, 8)} for i in range(1, 8)]
     )
@@ -555,6 +555,21 @@
 
     w.half[...] = jnp.zeros((8, 80, 512), f32)
     ring_half(0)
+    def turn_rows(slots):
+        for slot in slots:
+            w.turn[slot * 80 : (slot + 1) * 80, :] = squeeze_map(80, 8, slot)
+
+    between = {
+        (1, 0): lambda: turn_rows((0, 1, 2)),
+        (1, 1): lambda: turn_rows((3, 4, 5)),
+        (1, 2): lambda: turn_rows((6, 7)),
+        (1, 3): lambda: weigh_matrix(chip_table(), w.mix, 3, 32),
+        (2, 0): lambda: ring_half(1),
+        (2, 1): lambda: ring_half(7),
+        (2, 3): lambda: weigh_matrix(w.column[...], w.plane_mix, 8, 80),
+        (3, 0): lambda: ring_half(2),
+        (3, 1): lambda: ring_half(6),
+    }
     for r in range(1, 5):
         for q in range(PIECES):
             for d in range(2):
@@ -562,16 +577,13 @@
                     gather(d, q, r).wait_recv()
                 if r + 1 <= reach(d, q):
                     gather(d, q, r + 1).start()
-        ring_half(r)
-        if r < 4:
-            ring_half(8 - r)
-        if r == 1:
-            weigh_matrix(chip_table(), w.mix, 3, 32)
-            for slot in range(8):
-                w.turn[slot * 80 : (slot + 1) * 80, :] = squeeze_map(80, 8, slot)
-        if r == 2:
-            weigh_matrix(w.column[...], w.plane_mix, 8, 80)
+            if (r, q) in between:
+                between[r, q]()
+        if r == 4:
+            ring_half(4)
         if r == 3:
+            ring_half(3)
+            ring_half(5)
             for h, (start, width) in enumerate(SHARES):
                 take(plane_in[h].at[pl.ds(0, 7)], w.plane_r.at[h])
                 turned = jnp.dot(w.turn[...], plane_in[h][...].reshape(640, width), preferred_element_type=f32).astype(bf)
@@ -676,8 +688,7 @@
                 reduce(d, q, reach(d, q)).wait_recv()
                 whole = whole + w.plane_arrived[d, q, reach(d, q) - 1, :, 0:width].astype(f32)
             keep(whole, start, width)
-        for b in range(2):
-            hand(2, b, k).start()
+        hand(2)
 
     def straight_end():
         start, width = SHARES[1]
@@ -687,8 +698,7 @@
         for slot in range(1, 8):
             whole = whole + w.straight_in[slot].astype(f32)
         keep(whole, start, width)
-        for b in range(2):
-            hand(3, b, k).start()
+        hand(3)
 
     def give(part, i):
         to = lax.rem(e + i, 8)
@@ -709,13 +719,22 @@
             give(part, i).start()
         w.back[part, pl.ds(e, 1)] = w.ret[part, pl.ds(e, 1)]
 
-    def hand(part, b, core):
+    y_low = lax.div(e, 4)
+    before = {"pipe": jnp.where(y_low == 1, p, over), "exp": lax.rem(e + 4, 8)}
+
+    def hand(part):
         start, width = HANDS[part]
         columns = pl.ds(start, width)
-        return remote(
-            w.ready.at[b, :, columns], w.landed.at[core, :, columns], w.fin_s.at[0], w.fin_r.at[0],
-            pipe=over, ctx=2 * z + b,
-        )
+        remote(
+            w.ready.at[kk, :, columns], w.landed.at[k, :, columns], w.fin_s.at[0], w.fin_r.at[0], pipe=over, ctx=other
+        ).start()
+        remote(w.ready.at[k, :, columns], w.transit.at[:, columns], w.fin_s.at[0], w.hop_r.at[part], **before).start()
+
+    def hand_on(part):
+        start, width = HANDS[part]
+        columns = pl.ds(start, width)
+        take(w.transit.at[:, columns], w.hop_r.at[part])
+        remote(w.transit.at[:, columns], w.landed.at[k, :, columns], w.hop_s.at[0], w.fin_r.at[0], **before).start()
 
     def finish_ring(part):
         take(w.back.at[part, pl.ds(0, 7)], w.back_r.at[part])
@@ -725,8 +744,7 @@
             start = (part * 3 + g) * GROUP
             for b in range(2):
                 w.ready[b, :, start : start + GROUP] = layer_out[g * 32 + b * 16 : g * 32 + b * 16 + 16]
-        for b in range(2):
-            hand(part, b, k).start()
+        hand(part)
 
     scatter_on(1)
     scatter_on(2)
@@ -740,13 +758,18 @@
     reduce_on(3)
     finish_ring(0)
     reduce_end()
+    hand_on(0)
     finish_ring(1)
+    hand_on(2)
     straight_end()
+    hand_on(1)
+    hand_on(3)
     take(w.landed, w.fin_r.at[0])
     for b in range(2):
         out_ref[:, b * HALF : (b + 1) * HALF] = w.landed[b]
 
     take(w.ready, w.fin_s.at[0])
+    take(w.transit, w.hop_s.at[0])
     for copy in pair:
         copy.wait_send()
     take(w.brief.at[pl.ds(0, 7)], w.table_s.at[0])
@@ -783,7 +806,7 @@
     "w_in": ((HALF, 512), BF), "w_down": ((256, HALF), BF), "rows": ((8, 80, RING), BF),
     "half": ((8, 80, 512), F32), "half_other": ((8, 80, 512), F32), "hidden": ((640, 256), BF), "total": ((8, 80, RING), BF),
     "arrived": ((2, PIECES, 4, 80, GROUP), BF), "partial": ((8, 32, PLANE), BF), "plane_own": ((32, PLANE), F32),
-    "plane_arrived": ((2, 2, 4, 32, 512), BF), "ready": ((2, 16, HALF), BF), "landed": ((2, 16, HALF), BF),
+    "plane_arrived": ((2, 2, 4, 32, 512), BF), "ready": ((2, 16, HALF), BF), "landed": ((2, 16, HALF), BF), "transit": ((16, HALF), BF),
     "load": ((2,), None), "chain_s": ((1,), None), "chain_r": ((4, 4), None), "share_s": ((1,), None), "share_r": ((5,), None),
     "proj_s": ((1,), None), "proj_r": ((1,), None), "head_s": ((1,), None), "head_r": ((2, 2, 4), None),
     "fold_s": ((1,), None), "fold_r": ((8,), None), "cross_s": ((1,), None), "cross_r": ((8,), None),
@@ -794,7 +817,7 @@
     "ag_s": ((1,), None), "ag_r": ((2, PIECES, 4), None), "half_s": ((1,), None), "half_r": ((3,), None),
     "rs_s": ((1,), None), "rs_r": ((2, PIECES, 4), None), "red_s": ((1,), None), "red_r": ((2, 2, 4), None),
     "straight_s": ((1,), None), "straight_r": ((1,), None), "back_s": ((1,), None), "back_r": ((2,), None),
-    "fin_s": ((1,), None), "fin_r": ((1,), None),
+    "fin_s": ((1,), None), "fin_r": ((1,), None), "hop_s": ((1,), None), "hop_r": ((4,), None),
 }
 
 

time: 167 us -> 170 us (1.018); the launches traced: 167 us -> 168 us
  no operation moved by 1% of the time
where the time goes in v8:
time: 170 us; the launch traced here: 168 us
  Pallas kernels  166 us (98%)
    pallas_call x1, Pallas kernels, on_device(): pl.pallas_call(layer_kernel, out_shape=jax.ShapeDtypeStruct((16, D), BF),...  166 us

profile of v8, /device:TPU:1, one launch (start us, length us, event | category | flops | bytes accessed | tf_op | source)
XLA Modules:
  0.0 168.1 jit_solution(7946752421016764157)
XLA Ops:
  0.0 166.4 %layer.1 = bf16[16,7168]{1,0:T(8,128)(2,1)} custom-call(bf16[8,576,128]{2,1,0:T(8,128)(2,1)} %bitcast.25, bf16[576,128]{1,0:T(8,128)(2,1)} %bitcast.29, s32[1,128]{1,0:T(1,128)} %doc_ref.1, s32[2,16]{1,0:T(2,128)} %bitcast.30, f32[2,16]{1,0:T(2,128)} %bitcast.31, bf16[16,7168]{1,0:T(8,128)(2,1)} %bitcast.28, f32[1,7168]{1,0:T(1,128)} %gain_ref.1, ...), custom_call_target="tpu_custom_call" | custom-call | flops 8000000000 | bytes 10000000 | tf_op jit(solution)/shard_map/layer/pallas_call | solution.py:829
  166.4 1.6 copy.14

commit v9 on v7

--- a/solution.py
+++ b/solution.py
@@ -555,6 +555,21 @@
 
     w.half[...] = jnp.zeros((8, 80, 512), f32)
     ring_half(0)
+    def turn_rows(slots):
+        for slot in slots:
+            w.turn[slot * 80 : (slot + 1) * 80, :] = squeeze_map(80, 8, slot)
+
+    between = {
+        (1, 0): lambda: turn_rows((0, 1, 2)),
+        (1, 1): lambda: turn_rows((3, 4, 5)),
+        (1, 2): lambda: turn_rows((6, 7)),
+        (1, 5): lambda: weigh_matrix(chip_table(), w.mix, 3, 32),
+        (2, 0): lambda: ring_half(1),
+        (2, 1): lambda: ring_half(7),
+        (2, 5): lambda: weigh_matrix(w.column[...], w.plane_mix, 8, 80),
+        (3, 0): lambda: ring_half(2),
+        (3, 1): lambda: ring_half(6),
+    }
     for r in range(1, 5):
         for q in range(PIECES):
             for d in range(2):
@@ -562,16 +577,13 @@
                     gather(d, q, r).wait_recv()
                 if r + 1 <= reach(d, q):
                     gather(d, q, r + 1).start()
-        ring_half(r)
-        if r < 4:
-            ring_half(8 - r)
-        if r == 1:
-            weigh_matrix(chip_table(), w.mix, 3, 32)
-            for slot in range(8):
-                w.turn[slot * 80 : (slot + 1) * 80, :] = squeeze_map(80, 8, slot)
-        if r == 2:
-            weigh_matrix(w.column[...], w.plane_mix, 8, 80)
+            if (r, q) in between:
+                between[r, q]()
+        if r == 4:
+            ring_half(4)
         if r == 3:
+            ring_half(3)
+            ring_half(5)
             for h, (start, width) in enumerate(SHARES):
                 take(plane_in[h].at[pl.ds(0, 7)], w.plane_r.at[h])
                 turned = jnp.dot(w.turn[...], plane_in[h][...].reshape(640, width), preferred_element_type=f32).astype(bf)

time: 167 us -> 167 us (level)
  no operation moved by 1% of the time
where the time goes in v9:
time: 167 us
  Pallas kernels  165 us (99%)
    pallas_call x1, Pallas kernels, on_device(): pl.pallas_call(layer_kernel, out_shape=jax.ShapeDtypeStruct((16, D), BF),...  165 us

profile of v9, /device:TPU:1, one launch (start us, length us, event | category | flops | bytes accessed | tf_op | source)
XLA Modules:
  0.0 166.5 jit_solution(8492249863920575264)
XLA Ops:
  0.0 164.9 %layer.1 = bf16[16,7168]{1,0:T(8,128)(2,1)} custom-call(bf16[8,576,128]{2,1,0:T(8,128)(2,1)} %bitcast.25, bf16[576,128]{1,0:T(8,128)(2,1)} %bitcast.29, s32[1,128]{1,0:T(1,128)} %doc_ref.1, s32[2,16]{1,0:T(2,128)} %bitcast.30, f32[2,16]{1,0:T(2,128)} %bitcast.31, bf16[16,7168]{1,0:T(8,128)(2,1)} %bitcast.28, f32[1,7168]{1,0:T(1,128)} %gain_ref.1, ...), custom_call_target="tpu_custom_call" | custom-call | flops 8000000000 | bytes 10000000 | tf_op jit(solution)/shard_map/layer/pallas_call | solution.py:818
  164.9 1.6 copy.14
